TPU v7x, 32 devices: a whole 2x2x4 slice. The times are simulated.
32 devices in a mesh: grp: 4 (over z), exp: 4 (over y, core), rep: 2 (over x).
Axes of the slice: x: 2, y: 2, z: 4, core: 2. Of those that a mesh axis runs over, the one named last changes fastest.
Arguments:
- tokens: bfloat16 [512, 2048], P(('rep', 'grp', 'exp')), parts along dimension 0, may hold values from -6 to 6
- expert_ids: int32 [512, 8], P(('rep', 'grp', 'exp')), parts along dimension 0, may hold values from 0 to 15, as said below
- gate_weights: bfloat16 [512, 8], P(('rep', 'grp', 'exp')), parts along dimension 0, may hold values from 0.049804688 to 0.3984375
- w_gate: bfloat16 [16, 2048, 768], P(('grp', 'exp')), may hold values from -0.125 to 0.125
- w_up: bfloat16 [16, 2048, 768], P(('grp', 'exp')), may hold values from -0.125 to 0.125
- w_down: bfloat16 [16, 768, 2048], P(('grp', 'exp')), may hold values from -0.21875 to 0.21875
Outputs:
- combined: float32 [512, 2048], P(('rep', 'grp', 'exp')), parts along dimension 0
There are 2 independent parts, one for each index of `rep`. A program takes and returns all parts, laid end to end along the dimension named above; an argument that names none is the same for every part. Nothing has to cross between parts.
Inputs may be any that keep to these rules, and one draw needn't show every extreme that they name: `expert_ids`: expert x belongs to group x // 4. Each row names 8 different experts, 4 of them in each of two different groups. Of the 16 rows of one device (aligned blocks of 16 rows), at most 16 name experts of any one group and at most 16 name any one expert; in every draw one group is named by 16 rows of every device, and each of its experts by 16 rows of every device.
All inputs are finite; a program needn't handle non-finite values.
Results may differ from a plain program's by a relative error of at most 0.0041.
Values may be sent and summed in bfloat16 or wider, within the bound.
No kernel may reach another device: no remote copies, remote signals or barrier semaphores. Data moves between devices by JAX's collectives and lax.ppermute only.
A program may use at most 64 MiB of HBM per device.

v0:
```python
import functools

import jax
import jax.numpy as jnp
from jax import lax
from jax.experimental import pallas as pl
from jax.experimental.pallas import tpu as pltpu
from jax.sharding import PartitionSpec as P

CORES = 2
LANES = 128
WHOLE_ROWS = 512
PLACE_FLOPS = 1 << 31
PREP_FLOPS = 1 << 35
VMEM = pl.BlockSpec(memory_space=pltpu.VMEM)
SMEM = pl.BlockSpec(memory_space=pltpu.SMEM)
HBM = pl.BlockSpec(memory_space=pltpu.HBM)


def partner(index, step, count):
    return index ^ step if count & (count - 1) == 0 else (index + step) % count


def place_kernel(mine_ref, out_ref):
    out_ref[...] = jnp.zeros_like(out_ref) + mine_ref[0]


def find_place(mine, width):
    return pl.pallas_call(
        place_kernel,
        out_shape=jax.ShapeDtypeStruct((8, width), jnp.int32),
        in_specs=[SMEM],
        out_specs=VMEM,
        compiler_params=pltpu.CompilerParams(vmem_limit_bytes=8 << 20),
        cost_estimate=pl.CostEstimate(flops=PLACE_FLOPS, bytes_accessed=0, transcendentals=0),
    )(mine)


def prep_kernel(place_ref, ids_ref, gates_ref, tokens_ref, out_ref):
    model_width = tokens_ref.shape[1]
    width = out_ref.shape[1] - model_width
    out_ref[:, :model_width] = tokens_ref[...]
    ids = ids_ref[...]
    gates = gates_ref[...].astype(jnp.float32)
    top_count, rows = ids.shape
    expert = lax.broadcasted_iota(jnp.int32, (width, rows), 0)
    turned = jnp.zeros((width, rows), jnp.float32)
    for k in range(top_count):
        turned += jnp.where(ids[k : k + 1, :] == expert, gates[k : k + 1, :], 0.0)
    same = lax.broadcasted_iota(jnp.int32, (rows, rows), 0) == lax.broadcasted_iota(
        jnp.int32, (rows, rows), 1
    )
    table = lax.dot_general(
        same.astype(jnp.bfloat16),
        turned.astype(jnp.bfloat16),
        (((1,), (1,)), ((), ())),
        preferred_element_type=jnp.float32,
    )
    out_ref[:, model_width:] = table.astype(jnp.bfloat16)


def prepare(place, tokens, expert_ids, gate_weights):
    rows, model_width = tokens.shape
    return pl.pallas_call(
        prep_kernel,
        out_shape=jax.ShapeDtypeStruct((rows, model_width + place.shape[1]), jnp.bfloat16),
        in_specs=[HBM] + [VMEM] * 3,
        out_specs=VMEM,
        compiler_params=pltpu.CompilerParams(vmem_limit_bytes=8 << 20),
        cost_estimate=pl.CostEstimate(flops=PREP_FLOPS, bytes_accessed=0, transcendentals=0),
    )(place, expert_ids.T, gate_weights.T, tokens)


def row_scale(place_ref, table):
    table = table.astype(jnp.float32)
    lane = lax.broadcasted_iota(jnp.int32, table.shape, 1)
    return jnp.sum(jnp.where(lane == place_ref[:1, :], table, 0.0), axis=1, keepdims=True)


def activate(gate_pre, up_pre):
    return (gate_pre / (1.0 + jnp.exp(-gate_pre)) * up_pre).astype(jnp.bfloat16)


def join(pieces, out_ref):
    at = 0
    for ref in pieces:
        out_ref[at : at + ref.shape[0], :] = ref[...]
        at += ref.shape[0]


def expert_kernel(count, place_ref, *refs):
    kept_ref, given_ref, held = refs[-3:]
    gate_ref, up_ref, down_ref = refs[count : count + 3]
    rows, model_width = kept_ref.shape
    join(refs[:count], held)
    x = held[:, :model_width]
    scale = row_scale(place_ref, held[:, model_width:])
    gate_pre = jnp.dot(x, gate_ref[0], preferred_element_type=jnp.float32)
    up_pre = jnp.dot(x, up_ref[0], preferred_element_type=jnp.float32)
    hidden = activate(gate_pre, up_pre)
    result = jnp.dot(hidden, down_ref[0], preferred_element_type=jnp.float32) * scale
    kept_ref[...] = result[:rows]
    given_ref[...] = result[rows:].astype(given_ref.dtype)


def expert_rows(place, weights, own, other, *after):
    width = own[0].shape[1]
    _, model_width, hidden_width = weights[0].shape
    count = len(own) + len(other)
    rows = sum(piece.shape[0] for piece in own)
    return pl.pallas_call(
        functools.partial(expert_kernel, count),
        out_shape=[
            jax.ShapeDtypeStruct((rows, model_width), jnp.float32),
            jax.ShapeDtypeStruct((rows, model_width), jnp.bfloat16),
        ],
        in_specs=[VMEM] * (count + 4) + [HBM] * len(after),
        out_specs=[VMEM] * 2,
        scratch_shapes=[pltpu.VMEM((2 * rows, width), jnp.bfloat16)],
        compiler_params=pltpu.CompilerParams(vmem_limit_bytes=16 << 20),
        cost_estimate=pl.CostEstimate(
            flops=12 * rows * model_width * hidden_width,
            bytes_accessed=0,
            transcendentals=2 * rows * hidden_width,
        ),
    )(place, *own, *other, *weights, *after)


def pack_kernel(count, *refs):
    join(refs[:count], refs[-1])


def pack(pieces, *after):
    rows = sum(piece.shape[0] for piece in pieces)
    return pl.pallas_call(
        functools.partial(pack_kernel, len(pieces)),
        out_shape=jax.ShapeDtypeStruct((rows, pieces[0].shape[1]), pieces[0].dtype),
        in_specs=[VMEM] * len(pieces) + [HBM] * len(after),
        out_specs=VMEM,
        compiler_params=pltpu.CompilerParams(vmem_limit_bytes=8 << 20),
    )(*pieces, *after)


def add_kernel(first, *refs):
    out_ref = refs[-1]
    rows = out_ref.shape[0]
    total = None
    for ref in refs[:-1]:
        part = ref[...] if ref.shape[0] == rows else ref[first : first + rows, :]
        part = part.astype(jnp.float32)
        total = part if total is None else total + part
    out_ref[...] = total.astype(out_ref.dtype)


def add_rows(first, rows, out_type, *terms):
    return pl.pallas_call(
        functools.partial(add_kernel, first),
        out_shape=jax.ShapeDtypeStruct((rows, terms[0].shape[1]), out_type),
        in_specs=[VMEM] * len(terms),
        out_specs=VMEM,
        compiler_params=pltpu.CompilerParams(vmem_limit_bytes=8 << 20),
    )(*terms)


def shards(tokens, expert_ids, gate_weights, w_gate, w_up, w_down):
    tok_rows, model_width = tokens.shape
    groups = lax.axis_size("grp")
    owners = lax.axis_size("exp")
    experts = groups * owners
    chips = owners // CORES
    mine = lax.axis_index("grp") * owners + lax.axis_index("exp")

    def step_to(value, g, s, back=False):
        pairs = [
            (
                (i * chips + j) * CORES + c,
                (partner(i, g, groups) * chips + partner(j, s, chips)) * CORES + c,
            )
            for i in range(groups)
            for j in range(chips)
            for c in range(CORES)
        ]
        return lax.ppermute(value, ("grp", "exp"), [(d, o) for o, d in pairs] if back else pairs)

    def swap(value):
        return lax.ppermute(value, "exp", [(i, i ^ 1) for i in range(owners)])

    place = find_place(mine[None], experts + -experts % LANES)
    own = prepare(place, tokens, expert_ids, gate_weights)
    weights = (w_gate, w_up, w_down)
    width = groups if experts * tok_rows <= WHOLE_ROWS else 1
    total = None
    for first in range(0, groups, width):
        if first:
            own, total = lax.optimization_barrier((own, total))
        steps = range(first, first + width)
        near = [step_to(own, g, 0) if g else own for g in steps]
        far = [step_to(piece, 0, s) for piece in near for s in range(1, chips)]
        near_other = [swap(piece) for piece in near]
        far_block = pack(far, *near_other)
        near_kept, near_back = expert_rows(
            place, weights, near, near_other, far_block
        )
        far_kept, far_back = expert_rows(place, weights, [far_block], [swap(far_block)], near_kept)
        far_back, near_back = swap(far_back), swap(near_back)

        def near_sum(at, *terms):
            begin = at * tok_rows
            return add_rows(begin, tok_rows, jnp.bfloat16, near_kept, near_back, *terms)

        def far_sum(at, s):
            begin = (at * (chips - 1) + s - 1) * tok_rows
            return add_rows(begin, tok_rows, jnp.bfloat16, far_kept, far_back)

        terms = []
        if first == 0:
            terms += [part[:tok_rows] for part in (near_kept, near_back)]
        by_chip = {
            at: [step_to(far_sum(at, s), 0, s, True) for s in range(1, chips)]
            for at in reversed(range(width))
        }
        for at, g in reversed(list(enumerate(steps))):
            terms += [step_to(near_sum(at, *by_chip[at]), g, 0, True)] if g else by_chip[at]
        for term in terms:
            term = term.astype(jnp.float32)
            total = term if total is None else total + term
    return total


def solution(mesh):
    return jax.shard_map(
        shards,
        mesh=mesh,
        in_specs=(
            P(("rep", "grp", "exp"), None),
            P(("rep", "grp", "exp"), None),
            P(("rep", "grp", "exp"), None),
            P(("grp", "exp"), None, None),
            P(("grp", "exp"), None, None),
            P(("grp", "exp"), None, None),
        ),
        out_specs=P(("rep", "grp", "exp"), None),
        check_vma=False,
    )
```

profile of v0, /device:TPU:0, one launch (start us, length us, event | category | flops | bytes accessed | tf_op | source)
XLA Modules:
  0.0 37.3 jit_solution(13756248524107527822)
XLA Ops:
  0.0 0.8 %copy-done.3 = bf16[16,2048]{1,0:T(8,128)(2,1)S(1)} copy-done((bf16[16,2048]{1,0:T(8,128)(2,1)S(1)}, bf16[16,2048]{1,0:T(8,128)(2,1)}, u32[]{:S(2)}) %copy-start.3) | copy-done | bytes 65560
  1.0 5.1 %collective-permute-start.2 = (bf16[16,2176]{1,0:T(8,128)(2,1)S(1)}, bf16[16,2176]{1,0:T(8,128)(2,1)S(1)}, u32[]{:S(2)}, u32[]{:S(2)}) collective-permute-start(bf16[16,2176]{1,0:T(8,128)(2,1)S(1)} %shard_map.65.refs_0_), channel_id=1, source_target_pairs={{0,24},{2,26},{4,28},{6,30},{8,16},{10,18},{12,20},{14,22},{16,8},... | collective-permute-start | bytes 208904 | tf_op jit(solution)/shard_map/ppermute | solution.py:183
  6.1 1.5 %collective-permute-start.7 = (bf16[16,2176]{1,0:T(8,128)(2,1)S(1)}, bf16[16,2176]{1,0:T(8,128)(2,1)S(1)}, u32[]{:S(2)}, u32[]{:S(2)}) collective-permute-start(bf16[16,2176]{1,0:T(8,128)(2,1)S(1)} %shard_map.65.refs_0_), channel_id=1, source_target_pairs={{0,4},{2,6},{4,0},{6,2},{8,12},{10,14},{12,8},{14,10},{16,20},{18,... | collective-permute-start | bytes 208904 | tf_op jit(solution)/shard_map/ppermute | solution.py:183
  7.6 0.8 %collective-permute-start = (bf16[16,2176]{1,0:T(8,128)(2,1)S(1)}, bf16[16,2176]{1,0:T(8,128)(2,1)S(1)}, u32[]{:S(2)}, u32[]{:S(2)}) collective-permute-start(bf16[16,2176]{1,0:T(8,128)(2,1)S(1)} %shard_map.65.refs_0_), channel_id=1, source_target_pairs={{0,8},{2,10},{4,12},{6,14},{8,0},{10,2},{12,4},{14,6},{16,24},{18,... | collective-permute-start | bytes 208904 | tf_op jit(solution)/shard_map/ppermute | solution.py:183
  8.6 1.9 %collective-permute-start.10 = (bf16[16,2176]{1,0:T(8,128)(2,1)S(1)}, bf16[16,2176]{1,0:T(8,128)(2,1)S(1)}, u32[]{:S(2)}, u32[]{:S(2)}) collective-permute-start(bf16[16,2176]{1,0:T(8,128)(2,1)S(1)} %collective-permute-done.2.refs_3_), channel_id=1, source_target_pairs={{0,4},{2,6},{4,0},{6,2},{8,12},{10,14},{12,8},{14,10},{16,20},{18,... | collective-permute-start | bytes 208904 | tf_op jit(solution)/shard_map/ppermute | solution.py:183
  10.5 2.4 %collective-permute-done.1.refs_2_ = bf16[16,2176]{1,0:T(8,128)(2,1)S(1)} collective-permute-done((bf16[16,2176]{1,0:T(8,128)(2,1)S(1)}, bf16[16,2176]{1,0:T(8,128)(2,1)S(1)}, u32[]{:S(2)}, u32[]{:S(2)}) %collective-permute-start.1) | collective-permute-done | bytes 69664 | tf_op jit(solution)/shard_map/ppermute | solution.py:183
  12.9 0.7 %collective-permute-start.9 = (bf16[16,2176]{1,0:T(8,128)(2,1)S(1)}, bf16[16,2176]{1,0:T(8,128)(2,1)S(1)}, u32[]{:S(2)}, u32[]{:S(2)}) collective-permute-start(bf16[16,2176]{1,0:T(8,128)(2,1)S(1)} %collective-permute-done.1.refs_2_), channel_id=1, source_target_pairs={{0,4},{2,6},{4,0},{6,2},{8,12},{10,14},{12,8},{14,10},{16,20},{18,... | collective-permute-start | bytes 208904 | tf_op jit(solution)/shard_map/ppermute | solution.py:183
  13.6 1.4 %collective-permute-start.8 = (bf16[16,2176]{1,0:T(8,128)(2,1)S(1)}, bf16[16,2176]{1,0:T(8,128)(2,1)S(1)}, u32[]{:S(2)}, u32[]{:S(2)}) collective-permute-start(bf16[16,2176]{1,0:T(8,128)(2,1)S(1)} %collective-permute-done.refs_1_), channel_id=1, source_target_pairs={{0,4},{2,6},{4,0},{6,2},{8,12},{10,14},{12,8},{14,10},{16,20},{18,... | collective-permute-start | bytes 208904 | tf_op jit(solution)/shard_map/ppermute | solution.py:183
  15.2 2.5 %collective-permute-done.9.refs_2_ = bf16[16,2176]{1,0:T(8,128)(2,1)S(1)} collective-permute-done((bf16[16,2176]{1,0:T(8,128)(2,1)S(1)}, bf16[16,2176]{1,0:T(8,128)(2,1)S(1)}, u32[]{:S(2)}, u32[]{:S(2)}) %collective-permute-start.9) | collective-permute-done | bytes 69664 | tf_op jit(solution)/shard_map/ppermute | solution.py:183
  17.8 1.0 %collective-permute-done.8.refs_1_ = bf16[16,2176]{1,0:T(8,128)(2,1)S(1)} collective-permute-done((bf16[16,2176]{1,0:T(8,128)(2,1)S(1)}, bf16[16,2176]{1,0:T(8,128)(2,1)S(1)}, u32[]{:S(2)}, u32[]{:S(2)}) %collective-permute-start.8) | collective-permute-done | bytes 69664 | tf_op jit(solution)/shard_map/ppermute | solution.py:183
  18.9 1.5 %shard_map.67 = (f32[64,2048]{1,0:T(8,128)S(1)}, bf16[64,2048]{1,0:T(8,128)(2,1)S(1)}) custom-call(s32[8,128]{1,0:T(8,128)S(1)} %shard_map.64.place_ref, bf16[16,2176]{1,0:T(8,128)(2,1)S(1)} %shard_map.65.refs_0_, bf16[16,2176]{1,0:T(8,128)(2,1)S(1)} %collective-permute-done.refs_1_, bf16[16,2176]{1,0:T(8,128)(2,1)S(1)} %collective-permute-done.1.refs_2_, ...), custom_call_target="tpu_custom_call" | custom-call | flops 1207959552 | tf_op jit(solution)/shard_map/pallas_call | solution.py:111
  20.4 1.5 %shard_map.68 = (f32[64,2048]{1,0:T(8,128)S(1)}, bf16[64,2048]{1,0:T(8,128)(2,1)S(1)}) custom-call(s32[8,128]{1,0:T(8,128)S(1)} %shard_map.64.place_ref, bf16[64,2176]{1,0:T(8,128)(2,1)S(1)} %shard_map.66.refs_11_.refs_0_, bf16[64,2176]{1,0:T(8,128)(2,1)S(1)} %collective-permute-done.12.refs_1_, bf16[1,2048,768]{2,1,0:T(8,128)(2,1)S(1)} %copy-done, ...), custom_call_target="tpu_custom_call" | custom-call | flops 1207959552 | tf_op jit(solution)/shard_map/pallas_call | solution.py:111
  22.5 1.1 %collective-permute-done.13.refs_1_ = bf16[64,2048]{1,0:T(8,128)(2,1)S(1)} collective-permute-done((bf16[64,2048]{1,0:T(8,128)(2,1)S(1)}, bf16[64,2048]{1,0:T(8,128)(2,1)S(1)}, u32[]{:S(2)}, u32[]{:S(2)}) %collective-permute-start.13) | collective-permute-done | bytes 262176 | tf_op jit(solution)/shard_map/ppermute | solution.py:186
  23.6 0.9 %collective-permute-start.14 = (bf16[16,2048]{1,0:T(8,128)(2,1)S(1)}, bf16[16,2048]{1,0:T(8,128)(2,1)S(1)}, u32[]{:S(2)}, u32[]{:S(2)}) collective-permute-start(bf16[16,2048]{1,0:T(8,128)(2,1)S(1)} %shard_map.69), channel_id=1, source_target_pairs={{4,0},{6,2},{0,4},{2,6},{12,8},{14,10},{8,12},{10,14},{20,16},{22,... | collective-permute-start | bytes 196616 | tf_op jit(solution)/shard_map/ppermute | solution.py:183
  24.6 1.3 %collective-permute-start.16 = (bf16[16,2048]{1,0:T(8,128)(2,1)S(1)}, bf16[16,2048]{1,0:T(8,128)(2,1)S(1)}, u32[]{:S(2)}, u32[]{:S(2)}) collective-permute-start(bf16[16,2048]{1,0:T(8,128)(2,1)S(1)} %shard_map.71), channel_id=1, source_target_pairs={{4,0},{6,2},{0,4},{2,6},{12,8},{14,10},{8,12},{10,14},{20,16},{22,... | collective-permute-start | bytes 196616 | tf_op jit(solution)/shard_map/ppermute | solution.py:183
  25.9 0.9 %collective-permute-start.18 = (bf16[16,2048]{1,0:T(8,128)(2,1)S(1)}, bf16[16,2048]{1,0:T(8,128)(2,1)S(1)}, u32[]{:S(2)}, u32[]{:S(2)}) collective-permute-start(bf16[16,2048]{1,0:T(8,128)(2,1)S(1)} %shard_map.73), channel_id=1, source_target_pairs={{4,0},{6,2},{0,4},{2,6},{12,8},{14,10},{8,12},{10,14},{20,16},{22,... | collective-permute-start | bytes 196616 | tf_op jit(solution)/shard_map/ppermute | solution.py:183
  26.8 1.3 %collective-permute-start.20 = (bf16[16,2048]{1,0:T(8,128)(2,1)S(1)}, bf16[16,2048]{1,0:T(8,128)(2,1)S(1)}, u32[]{:S(2)}, u32[]{:S(2)}) collective-permute-start(bf16[16,2048]{1,0:T(8,128)(2,1)S(1)} %shard_map.75), channel_id=1, source_target_pairs={{4,0},{6,2},{0,4},{2,6},{12,8},{14,10},{8,12},{10,14},{20,16},{22,... | collective-permute-start | bytes 196616 | tf_op jit(solution)/shard_map/ppermute | solution.py:183
  28.0 0.6 %collective-permute-done.14.refs_2_ = bf16[16,2048]{1,0:T(8,128)(2,1)S(1)} collective-permute-done((bf16[16,2048]{1,0:T(8,128)(2,1)S(1)}, bf16[16,2048]{1,0:T(8,128)(2,1)S(1)}, u32[]{:S(2)}, u32[]{:S(2)}) %collective-permute-start.14) | collective-permute-done | bytes 65568 | tf_op jit(solution)/shard_map/ppermute | solution.py:183
  28.7 2.1 %collective-permute-start.15 = (bf16[16,2048]{1,0:T(8,128)(2,1)S(1)}, bf16[16,2048]{1,0:T(8,128)(2,1)S(1)}, u32[]{:S(2)}, u32[]{:S(2)}) collective-permute-start(bf16[16,2048]{1,0:T(8,128)(2,1)S(1)} %shard_map.70), channel_id=1, source_target_pairs={{24,0},{26,2},{28,4},{30,6},{16,8},{18,10},{20,12},{22,14},{8,16},... | collective-permute-start | bytes 196616 | tf_op jit(solution)/shard_map/ppermute | solution.py:183
  30.8 0.6 %collective-permute-start.17 = (bf16[16,2048]{1,0:T(8,128)(2,1)S(1)}, bf16[16,2048]{1,0:T(8,128)(2,1)S(1)}, u32[]{:S(2)}, u32[]{:S(2)}) collective-permute-start(bf16[16,2048]{1,0:T(8,128)(2,1)S(1)} %shard_map.72), channel_id=1, source_target_pairs={{16,0},{18,2},{20,4},{22,6},{24,8},{26,10},{28,12},{30,14},{0,16},... | collective-permute-start | bytes 196616 | tf_op jit(solution)/shard_map/ppermute | solution.py:183
  31.5 1.8 %collective-permute-start.19 = (bf16[16,2048]{1,0:T(8,128)(2,1)S(1)}, bf16[16,2048]{1,0:T(8,128)(2,1)S(1)}, u32[]{:S(2)}, u32[]{:S(2)}) collective-permute-start(bf16[16,2048]{1,0:T(8,128)(2,1)S(1)} %shard_map.74), channel_id=1, source_target_pairs={{8,0},{10,2},{12,4},{14,6},{0,8},{2,10},{4,12},{6,14},{24,16},{26,... | collective-permute-start | bytes 196616 | tf_op jit(solution)/shard_map/ppermute | solution.py:183
  33.3 1.9 %collective-permute-done.15 = bf16[16,2048]{1,0:T(8,128)(2,1)S(1)} collective-permute-done((bf16[16,2048]{1,0:T(8,128)(2,1)S(1)}, bf16[16,2048]{1,0:T(8,128)(2,1)S(1)}, u32[]{:S(2)}, u32[]{:S(2)}) %collective-permute-start.15) | collective-permute-done | bytes 65568 | tf_op jit(solution)/shard_map/ppermute | solution.py:183
  35.2 1.5 %collective-permute-done.17 = bf16[16,2048]{1,0:T(8,128)(2,1)S(1)} collective-permute-done((bf16[16,2048]{1,0:T(8,128)(2,1)S(1)}, bf16[16,2048]{1,0:T(8,128)(2,1)S(1)}, u32[]{:S(2)}, u32[]{:S(2)}) %collective-permute-start.17) | collective-permute-done | bytes 65568 | tf_op jit(solution)/shard_map/ppermute | solution.py:183
  36.6 0.7 %convert_add_fusion = f32[16,2048]{1,0:T(8,128)} fusion(bf16[16,2048]{1,0:T(8,128)(2,1)S(1)} %collective-permute-done.20, bf16[16,2048]{1,0:T(8,128)(2,1)S(1)} %collective-permute-done.19, bf16[16,2048]{1,0:T(8,128)(2,1)S(1)} %collective-permute-done.17, bf16[16,2048]{1,0:T(8,128)(2,1)S(1)} %collective-permute-done.15, ...), kind=kLoop, calls=%fused_computation | loop fusion | flops 327680 | bytes 589824 | tf_op jit(solution)/shard_map/add | solution.py:226
  (43 shorter events, 1.5 us)
Async XLA Ops:
  0.8 18.0 %copy-start = (bf16[1,2048,768]{2,1,0:T(8,128)(2,1)S(1)}, bf16[1,2048,768]{2,1,0:T(8,128)(2,1)}, u32[]{:S(2)}) copy-start(bf16[1,2048,768]{2,1,0:T(8,128)(2,1)} %refs_2_.1) | copy-start | bytes 9437188
  0.8 18.0 %copy-start.1 = (bf16[1,2048,768]{2,1,0:T(8,128)(2,1)S(1)}, bf16[1,2048,768]{2,1,0:T(8,128)(2,1)}, u32[]{:S(2)}) copy-start(bf16[1,2048,768]{2,1,0:T(8,128)(2,1)} %refs_3_.1) | copy-start | bytes 9437188
  0.9 18.0 %copy-start.2 = (bf16[1,768,2048]{2,1,0:T(8,128)(2,1)S(1)}, bf16[1,768,2048]{2,1,0:T(8,128)(2,1)}, u32[]{:S(2)}) copy-start(bf16[1,768,2048]{2,1,0:T(8,128)(2,1)} %refs_4_.1) | copy-start | bytes 9437188
  1.0 7.5 %collective-permute-start.2 = (bf16[16,2176]{1,0:T(8,128)(2,1)S(1)}, bf16[16,2176]{1,0:T(8,128)(2,1)S(1)}, u32[]{:S(2)}, u32[]{:S(2)}) collective-permute-start(bf16[16,2176]{1,0:T(8,128)(2,1)S(1)} %shard_map.65.refs_0_), channel_id=1, source_target_pairs={{0,24},{2,26},{4,28},{6,30},{8,16},{10,18},{12,20},{14,22},{16,8},... | collective-permute-start | bytes 208904 | tf_op jit(solution)/shard_map/ppermute | solution.py:183
  6.1 4.4 %collective-permute-start.7 = (bf16[16,2176]{1,0:T(8,128)(2,1)S(1)}, bf16[16,2176]{1,0:T(8,128)(2,1)S(1)}, u32[]{:S(2)}, u32[]{:S(2)}) collective-permute-start(bf16[16,2176]{1,0:T(8,128)(2,1)S(1)} %shard_map.65.refs_0_), channel_id=1, source_target_pairs={{0,4},{2,6},{4,0},{6,2},{8,12},{10,14},{12,8},{14,10},{16,20},{18,... | collective-permute-start | bytes 208904 | tf_op jit(solution)/shard_map/ppermute | solution.py:183
  7.6 5.3 %collective-permute-start.1 = (bf16[16,2176]{1,0:T(8,128)(2,1)S(1)}, bf16[16,2176]{1,0:T(8,128)(2,1)S(1)}, u32[]{:S(2)}, u32[]{:S(2)}) collective-permute-start(bf16[16,2176]{1,0:T(8,128)(2,1)S(1)} %shard_map.65.refs_0_), channel_id=1, source_target_pairs={{0,16},{2,18},{4,20},{6,22},{8,24},{10,26},{12,28},{14,30},{16,0},... | collective-permute-start | bytes 208904 | tf_op jit(solution)/shard_map/ppermute | solution.py:183
  7.6 6.0 %collective-permute-start.3 = (bf16[16,2176]{1,0:T(8,128)(2,1)S(1)}, bf16[16,2176]{1,0:T(8,128)(2,1)S(1)}, u32[]{:S(2)}, u32[]{:S(2)}) collective-permute-start(bf16[16,2176]{1,0:T(8,128)(2,1)S(1)} %shard_map.65.refs_0_), channel_id=1, source_target_pairs={{0,2},{2,0},{4,6},{6,4},{1,3},{3,1},{5,7},{7,5},{8,10},{10,8},{12,... | collective-permute-start | bytes 208904 | tf_op jit(solution)/shard_map/ppermute | solution.py:186
  7.6 6.0 %collective-permute-start = (bf16[16,2176]{1,0:T(8,128)(2,1)S(1)}, bf16[16,2176]{1,0:T(8,128)(2,1)S(1)}, u32[]{:S(2)}, u32[]{:S(2)}) collective-permute-start(bf16[16,2176]{1,0:T(8,128)(2,1)S(1)} %shard_map.65.refs_0_), channel_id=1, source_target_pairs={{0,8},{2,10},{4,12},{6,14},{8,0},{10,2},{12,4},{14,6},{16,24},{18,... | collective-permute-start | bytes 208904 | tf_op jit(solution)/shard_map/ppermute | solution.py:183
  8.6 6.5 %collective-permute-start.10 = (bf16[16,2176]{1,0:T(8,128)(2,1)S(1)}, bf16[16,2176]{1,0:T(8,128)(2,1)S(1)}, u32[]{:S(2)}, u32[]{:S(2)}) collective-permute-start(bf16[16,2176]{1,0:T(8,128)(2,1)S(1)} %collective-permute-done.2.refs_3_), channel_id=1, source_target_pairs={{0,4},{2,6},{4,0},{6,2},{8,12},{10,14},{12,8},{14,10},{16,20},{18,... | collective-permute-start | bytes 208904 | tf_op jit(solution)/shard_map/ppermute | solution.py:183
  10.5 4.7 %collective-permute-start.6 = (bf16[16,2176]{1,0:T(8,128)(2,1)S(1)}, bf16[16,2176]{1,0:T(8,128)(2,1)S(1)}, u32[]{:S(2)}, u32[]{:S(2)}) collective-permute-start(bf16[16,2176]{1,0:T(8,128)(2,1)S(1)} %collective-permute-done.2.refs_3_), channel_id=1, source_target_pairs={{0,2},{2,0},{4,6},{6,4},{1,3},{3,1},{5,7},{7,5},{8,10},{10,8},{12,... | collective-permute-start | bytes 208904 | tf_op jit(solution)/shard_map/ppermute | solution.py:186
  12.9 4.8 %collective-permute-start.9 = (bf16[16,2176]{1,0:T(8,128)(2,1)S(1)}, bf16[16,2176]{1,0:T(8,128)(2,1)S(1)}, u32[]{:S(2)}, u32[]{:S(2)}) collective-permute-start(bf16[16,2176]{1,0:T(8,128)(2,1)S(1)} %collective-permute-done.1.refs_2_), channel_id=1, source_target_pairs={{0,4},{2,6},{4,0},{6,2},{8,12},{10,14},{12,8},{14,10},{16,20},{18,... | collective-permute-start | bytes 208904 | tf_op jit(solution)/shard_map/ppermute | solution.py:183
  13.6 4.1 %collective-permute-start.5 = (bf16[16,2176]{1,0:T(8,128)(2,1)S(1)}, bf16[16,2176]{1,0:T(8,128)(2,1)S(1)}, u32[]{:S(2)}, u32[]{:S(2)}) collective-permute-start(bf16[16,2176]{1,0:T(8,128)(2,1)S(1)} %collective-permute-done.1.refs_2_), channel_id=1, source_target_pairs={{0,2},{2,0},{4,6},{6,4},{1,3},{3,1},{5,7},{7,5},{8,10},{10,8},{12,... | collective-permute-start | bytes 208904 | tf_op jit(solution)/shard_map/ppermute | solution.py:186
  13.6 5.1 %collective-permute-start.8 = (bf16[16,2176]{1,0:T(8,128)(2,1)S(1)}, bf16[16,2176]{1,0:T(8,128)(2,1)S(1)}, u32[]{:S(2)}, u32[]{:S(2)}) collective-permute-start(bf16[16,2176]{1,0:T(8,128)(2,1)S(1)} %collective-permute-done.refs_1_), channel_id=1, source_target_pairs={{0,4},{2,6},{4,0},{6,2},{8,12},{10,14},{12,8},{14,10},{16,20},{18,... | collective-permute-start | bytes 208904 | tf_op jit(solution)/shard_map/ppermute | solution.py:183
  15.0 3.7 %collective-permute-start.4 = (bf16[16,2176]{1,0:T(8,128)(2,1)S(1)}, bf16[16,2176]{1,0:T(8,128)(2,1)S(1)}, u32[]{:S(2)}, u32[]{:S(2)}) collective-permute-start(bf16[16,2176]{1,0:T(8,128)(2,1)S(1)} %collective-permute-done.refs_1_), channel_id=1, source_target_pairs={{0,2},{2,0},{4,6},{6,4},{1,3},{3,1},{5,7},{7,5},{8,10},{10,8},{12,... | collective-permute-start | bytes 208904 | tf_op jit(solution)/shard_map/ppermute | solution.py:186
  18.8 1.6 %collective-permute-start.12 = (bf16[64,2176]{1,0:T(8,128)(2,1)S(1)}, bf16[64,2176]{1,0:T(8,128)(2,1)S(1)}, u32[]{:S(2)}, u32[]{:S(2)}) collective-permute-start(bf16[64,2176]{1,0:T(8,128)(2,1)S(1)} %shard_map.66.refs_11_.refs_0_), channel_id=1, source_target_pairs={{0,2},{2,0},{4,6},{6,4},{1,3},{3,1},{5,7},{7,5},{8,10},{10,8},{12,... | collective-permute-start | bytes 835592 | tf_op jit(solution)/shard_map/ppermute | solution.py:186
  21.9 1.7 %collective-permute-start.13 = (bf16[64,2048]{1,0:T(8,128)(2,1)S(1)}, bf16[64,2048]{1,0:T(8,128)(2,1)S(1)}, u32[]{:S(2)}, u32[]{:S(2)}) collective-permute-start(bf16[64,2048]{1,0:T(8,128)(2,1)S(1)} %get-tuple-element.12), channel_id=1, source_target_pairs={{0,2},{2,0},{4,6},{6,4},{1,3},{3,1},{5,7},{7,5},{8,10},{10,8},{12,... | collective-permute-start | bytes 786440 | tf_op jit(solution)/shard_map/ppermute | solution.py:186
  22.5 5.6 %collective-permute-start.11 = (bf16[64,2048]{1,0:T(8,128)(2,1)S(1)}, bf16[64,2048]{1,0:T(8,128)(2,1)S(1)}, u32[]{:S(2)}, u32[]{:S(2)}) collective-permute-start(bf16[64,2048]{1,0:T(8,128)(2,1)S(1)} %get-tuple-element.10), channel_id=1, source_target_pairs={{0,2},{2,0},{4,6},{6,4},{1,3},{3,1},{5,7},{7,5},{8,10},{10,8},{12,... | collective-permute-start | bytes 786440 | tf_op jit(solution)/shard_map/ppermute | solution.py:186
  23.6 5.0 %collective-permute-start.14 = (bf16[16,2048]{1,0:T(8,128)(2,1)S(1)}, bf16[16,2048]{1,0:T(8,128)(2,1)S(1)}, u32[]{:S(2)}, u32[]{:S(2)}) collective-permute-start(bf16[16,2048]{1,0:T(8,128)(2,1)S(1)} %shard_map.69), channel_id=1, source_target_pairs={{4,0},{6,2},{0,4},{2,6},{12,8},{14,10},{8,12},{10,14},{20,16},{22,... | collective-permute-start | bytes 196616 | tf_op jit(solution)/shard_map/ppermute | solution.py:183
  24.6 6.2 %collective-permute-start.16 = (bf16[16,2048]{1,0:T(8,128)(2,1)S(1)}, bf16[16,2048]{1,0:T(8,128)(2,1)S(1)}, u32[]{:S(2)}, u32[]{:S(2)}) collective-permute-start(bf16[16,2048]{1,0:T(8,128)(2,1)S(1)} %shard_map.71), channel_id=1, source_target_pairs={{4,0},{6,2},{0,4},{2,6},{12,8},{14,10},{8,12},{10,14},{20,16},{22,... | collective-permute-start | bytes 196616 | tf_op jit(solution)/shard_map/ppermute | solution.py:183
  25.9 5.6 %collective-permute-start.18 = (bf16[16,2048]{1,0:T(8,128)(2,1)S(1)}, bf16[16,2048]{1,0:T(8,128)(2,1)S(1)}, u32[]{:S(2)}, u32[]{:S(2)}) collective-permute-start(bf16[16,2048]{1,0:T(8,128)(2,1)S(1)} %shard_map.73), channel_id=1, source_target_pairs={{4,0},{6,2},{0,4},{2,6},{12,8},{14,10},{8,12},{10,14},{20,16},{22,... | collective-permute-start | bytes 196616 | tf_op jit(solution)/shard_map/ppermute | solution.py:183
  26.8 6.6 %collective-permute-start.20 = (bf16[16,2048]{1,0:T(8,128)(2,1)S(1)}, bf16[16,2048]{1,0:T(8,128)(2,1)S(1)}, u32[]{:S(2)}, u32[]{:S(2)}) collective-permute-start(bf16[16,2048]{1,0:T(8,128)(2,1)S(1)} %shard_map.75), channel_id=1, source_target_pairs={{4,0},{6,2},{0,4},{2,6},{12,8},{14,10},{8,12},{10,14},{20,16},{22,... | collective-permute-start | bytes 196616 | tf_op jit(solution)/shard_map/ppermute | solution.py:183
  28.7 6.5 %collective-permute-start.15 = (bf16[16,2048]{1,0:T(8,128)(2,1)S(1)}, bf16[16,2048]{1,0:T(8,128)(2,1)S(1)}, u32[]{:S(2)}, u32[]{:S(2)}) collective-permute-start(bf16[16,2048]{1,0:T(8,128)(2,1)S(1)} %shard_map.70), channel_id=1, source_target_pairs={{24,0},{26,2},{28,4},{30,6},{16,8},{18,10},{20,12},{22,14},{8,16},... | collective-permute-start | bytes 196616 | tf_op jit(solution)/shard_map/ppermute | solution.py:183
  30.8 5.8 %collective-permute-start.17 = (bf16[16,2048]{1,0:T(8,128)(2,1)S(1)}, bf16[16,2048]{1,0:T(8,128)(2,1)S(1)}, u32[]{:S(2)}, u32[]{:S(2)}) collective-permute-start(bf16[16,2048]{1,0:T(8,128)(2,1)S(1)} %shard_map.72), channel_id=1, source_target_pairs={{16,0},{18,2},{20,4},{22,6},{24,8},{26,10},{28,12},{30,14},{0,16},... | collective-permute-start | bytes 196616 | tf_op jit(solution)/shard_map/ppermute | solution.py:183
  31.5 5.2 %collective-permute-start.19 = (bf16[16,2048]{1,0:T(8,128)(2,1)S(1)}, bf16[16,2048]{1,0:T(8,128)(2,1)S(1)}, u32[]{:S(2)}, u32[]{:S(2)}) collective-permute-start(bf16[16,2048]{1,0:T(8,128)(2,1)S(1)} %shard_map.74), channel_id=1, source_target_pairs={{8,0},{10,2},{12,4},{14,6},{0,8},{2,10},{4,12},{6,14},{24,16},{26,... | collective-permute-start | bytes 196616 | tf_op jit(solution)/shard_map/ppermute | solution.py:183
  (3 other events, 2.5 us)
where the time goes:
time: 37.5 us; the launch traced here: 37.3 us
  starting transfers between devices  21.1 us (56%)
  waiting for transfers between devices  11.2 us (30%)
  Pallas kernels  3.36 us (9%)
  local copies, waits for them, and re-layouts  0.85 us (2%)
  other arithmetic  0.7 us (2%)
    ppermute x14, starting transfers between devices, step_to(): lax.ppermute(value, ('grp', 'exp'), [(d, o) for o, d in pairs] if back el...  20.3 us
    ppermute x14, waiting for transfers between devices, step_to(): lax.ppermute(value, ('grp', 'exp'), [(d, o) for o, d in pairs] if back el...  10.1 us
    pallas_call x2, Pallas kernels, expert_rows(): pl.pallas_call(functools.partial(expert_kernel, count), out_shape=[jax.Sh...  3.01 us
    ppermute x7, waiting for transfers between devices, swap(): return lax.ppermute(value, 'exp', [(i, i ^ 1) for i in range(owners)])  1.1 us
    ppermute x7, starting transfers between devices, swap(): return lax.ppermute(value, 'exp', [(i, i ^ 1) for i in range(owners)])  0.86 us
    unnamed x12, local copies, waits for them, and re-layouts  0.85 us
  transfers between devices with their start and end apart: 21, of which 8 were waited for; matrix products, arithmetic and copies ran while one was open for 0% of the time, Pallas kernels for 4%

commit v1 on v0

--- a/solution.py
+++ b/solution.py
@@ -195,7 +195,11 @@
             own, total = lax.optimization_barrier((own, total))
         steps = range(first, first + width)
         near = [step_to(own, g, 0) if g else own for g in steps]
-        far = [step_to(piece, 0, s) for piece in near for s in range(1, chips)]
+        far = [
+            step_to(own, g, s) if g == 1 else step_to(near[at], 0, s)
+            for at, g in enumerate(steps)
+            for s in range(1, chips)
+        ]
         near_other = [swap(piece) for piece in near]
         far_block = pack(far, *near_other)
         near_kept, near_back = expert_rows(

time: 37.5 us -> 38.2 us (1.019)
  waiting for transfers between devices: 11.2 us -> 12.6 us
  starting transfers between devices: 21.1 us -> 20.3 us
    ppermute x14, waiting for transfers between devices: 10.1 us -> 11.5 us  [step_to(): lax.ppermute(value, ('grp', 'exp'), [(d, o) for o, d in pairs] if back el...]
    ppermute x14, starting transfers between devices: 20.3 us -> 19.1 us  [step_to(): lax.ppermute(value, ('grp', 'exp'), [(d, o) for o, d in pairs] if back el...]
where the time goes in v1:
time: 38.2 us; the launch traced here: 38 us
  starting transfers between devices  20.3 us (53%)
  waiting for transfers between devices  12.6 us (33%)
  Pallas kernels  3.38 us (9%)
  local copies, waits for them, and re-layouts  0.85 us (2%)
  other arithmetic  0.7 us (2%)
    ppermute x14, starting transfers between devices, step_to(): lax.ppermute(value, ('grp', 'exp'), [(d, o) for o, d in pairs] if back el...  19.1 us
    ppermute x14, waiting for transfers between devices, step_to(): lax.ppermute(value, ('grp', 'exp'), [(d, o) for o, d in pairs] if back el...  11.5 us
    pallas_call x2, Pallas kernels, expert_rows(): pl.pallas_call(functools.partial(expert_kernel, count), out_shape=[jax.Sh...  3.03 us
    ppermute x7, starting transfers between devices, swap(): return lax.ppermute(value, 'exp', [(i, i ^ 1) for i in range(owners)])  1.18 us
    ppermute x7, waiting for transfers between devices, swap(): return lax.ppermute(value, 'exp', [(i, i ^ 1) for i in range(owners)])  1.1 us
    unnamed x12, local copies, waits for them, and re-layouts  0.85 us
  transfers between devices with their start and end apart: 21, of which 8 were waited for; matrix products, arithmetic and copies ran while one was open for 0% of the time, Pallas kernels for 4%

profile of v1, /device:TPU:0, one launch (start us, length us, event | category | flops | bytes accessed | tf_op | source)
XLA Modules:
  0.0 38.0 jit_solution(9172740581887941898)
XLA Ops:
  0.0 0.8 %copy-done.3 = bf16[16,2048]{1,0:T(8,128)(2,1)S(1)} copy-done((bf16[16,2048]{1,0:T(8,128)(2,1)S(1)}, bf16[16,2048]{1,0:T(8,128)(2,1)}, u32[]{:S(2)}) %copy-start.3) | copy-done | bytes 65560
  1.0 4.0 %collective-permute-start.8 = (bf16[16,2176]{1,0:T(8,128)(2,1)S(1)}, bf16[16,2176]{1,0:T(8,128)(2,1)S(1)}, u32[]{:S(2)}, u32[]{:S(2)}) collective-permute-start(bf16[16,2176]{1,0:T(8,128)(2,1)S(1)} %shard_map.65.refs_0_), channel_id=1, source_target_pairs={{0,12},{2,14},{4,8},{6,10},{8,4},{10,6},{12,0},{14,2},{16,28},{18,... | collective-permute-start | bytes 208904 | tf_op jit(solution)/shard_map/ppermute | solution.py:183
  5.0 2.5 %collective-permute-start.2 = (bf16[16,2176]{1,0:T(8,128)(2,1)S(1)}, bf16[16,2176]{1,0:T(8,128)(2,1)S(1)}, u32[]{:S(2)}, u32[]{:S(2)}) collective-permute-start(bf16[16,2176]{1,0:T(8,128)(2,1)S(1)} %shard_map.65.refs_0_), channel_id=1, source_target_pairs={{0,24},{2,26},{4,28},{6,30},{8,16},{10,18},{12,20},{14,22},{16,8},... | collective-permute-start | bytes 208904 | tf_op jit(solution)/shard_map/ppermute | solution.py:183
  7.5 0.5 %collective-permute-start.7 = (bf16[16,2176]{1,0:T(8,128)(2,1)S(1)}, bf16[16,2176]{1,0:T(8,128)(2,1)S(1)}, u32[]{:S(2)}, u32[]{:S(2)}) collective-permute-start(bf16[16,2176]{1,0:T(8,128)(2,1)S(1)} %shard_map.65.refs_0_), channel_id=1, source_target_pairs={{0,4},{2,6},{4,0},{6,2},{8,12},{10,14},{12,8},{14,10},{16,20},{18,... | collective-permute-start | bytes 208904 | tf_op jit(solution)/shard_map/ppermute | solution.py:183
  8.1 1.8 %collective-permute-start = (bf16[16,2176]{1,0:T(8,128)(2,1)S(1)}, bf16[16,2176]{1,0:T(8,128)(2,1)S(1)}, u32[]{:S(2)}, u32[]{:S(2)}) collective-permute-start(bf16[16,2176]{1,0:T(8,128)(2,1)S(1)} %shard_map.65.refs_0_), channel_id=1, source_target_pairs={{0,8},{2,10},{4,12},{6,14},{8,0},{10,2},{12,4},{14,6},{16,24},{18,... | collective-permute-start | bytes 208904 | tf_op jit(solution)/shard_map/ppermute | solution.py:183
  9.9 1.9 %collective-permute-done.2.refs_3_ = bf16[16,2176]{1,0:T(8,128)(2,1)S(1)} collective-permute-done((bf16[16,2176]{1,0:T(8,128)(2,1)S(1)}, bf16[16,2176]{1,0:T(8,128)(2,1)S(1)}, u32[]{:S(2)}, u32[]{:S(2)}) %collective-permute-start.2) | collective-permute-done | bytes 69664 | tf_op jit(solution)/shard_map/ppermute | solution.py:183
  11.9 2.5 %collective-permute-done.1.refs_2_ = bf16[16,2176]{1,0:T(8,128)(2,1)S(1)} collective-permute-done((bf16[16,2176]{1,0:T(8,128)(2,1)S(1)}, bf16[16,2176]{1,0:T(8,128)(2,1)S(1)}, u32[]{:S(2)}, u32[]{:S(2)}) %collective-permute-start.1) | collective-permute-done | bytes 69664 | tf_op jit(solution)/shard_map/ppermute | solution.py:183
  14.4 1.2 %collective-permute-start.9 = (bf16[16,2176]{1,0:T(8,128)(2,1)S(1)}, bf16[16,2176]{1,0:T(8,128)(2,1)S(1)}, u32[]{:S(2)}, u32[]{:S(2)}) collective-permute-start(bf16[16,2176]{1,0:T(8,128)(2,1)S(1)} %collective-permute-done.1.refs_2_), channel_id=1, source_target_pairs={{0,4},{2,6},{4,0},{6,2},{8,12},{10,14},{12,8},{14,10},{16,20},{18,... | collective-permute-start | bytes 208904 | tf_op jit(solution)/shard_map/ppermute | solution.py:183
  15.6 0.5 %collective-permute-start.4 = (bf16[16,2176]{1,0:T(8,128)(2,1)S(1)}, bf16[16,2176]{1,0:T(8,128)(2,1)S(1)}, u32[]{:S(2)}, u32[]{:S(2)}) collective-permute-start(bf16[16,2176]{1,0:T(8,128)(2,1)S(1)} %collective-permute-done.refs_1_), channel_id=1, source_target_pairs={{0,2},{2,0},{4,6},{6,4},{1,3},{3,1},{5,7},{7,5},{8,10},{10,8},{12,... | collective-permute-start | bytes 208904 | tf_op jit(solution)/shard_map/ppermute | solution.py:186
  16.2 2.5 %collective-permute-done.9.refs_2_ = bf16[16,2176]{1,0:T(8,128)(2,1)S(1)} collective-permute-done((bf16[16,2176]{1,0:T(8,128)(2,1)S(1)}, bf16[16,2176]{1,0:T(8,128)(2,1)S(1)}, u32[]{:S(2)}, u32[]{:S(2)}) %collective-permute-start.9) | collective-permute-done | bytes 69664 | tf_op jit(solution)/shard_map/ppermute | solution.py:183
  18.8 1.5 %shard_map.67 = (f32[64,2048]{1,0:T(8,128)S(1)}, bf16[64,2048]{1,0:T(8,128)(2,1)S(1)}) custom-call(s32[8,128]{1,0:T(8,128)S(1)} %shard_map.64.place_ref, bf16[16,2176]{1,0:T(8,128)(2,1)S(1)} %shard_map.65.refs_0_, bf16[16,2176]{1,0:T(8,128)(2,1)S(1)} %collective-permute-done.refs_1_, bf16[16,2176]{1,0:T(8,128)(2,1)S(1)} %collective-permute-done.1.refs_2_, ...), custom_call_target="tpu_custom_call" | custom-call | flops 1207959552 | tf_op jit(solution)/shard_map/pallas_call | solution.py:111
  20.4 1.5 %shard_map.68 = (f32[64,2048]{1,0:T(8,128)S(1)}, bf16[64,2048]{1,0:T(8,128)(2,1)S(1)}) custom-call(s32[8,128]{1,0:T(8,128)S(1)} %shard_map.64.place_ref, bf16[64,2176]{1,0:T(8,128)(2,1)S(1)} %shard_map.66.refs_11_.refs_0_, bf16[64,2176]{1,0:T(8,128)(2,1)S(1)} %collective-permute-done.12.refs_1_, bf16[1,2048,768]{2,1,0:T(8,128)(2,1)S(1)} %copy-done, ...), custom_call_target="tpu_custom_call" | custom-call | flops 1207959552 | tf_op jit(solution)/shard_map/pallas_call | solution.py:111
  21.9 0.5 %collective-permute-start.13 = (bf16[64,2048]{1,0:T(8,128)(2,1)S(1)}, bf16[64,2048]{1,0:T(8,128)(2,1)S(1)}, u32[]{:S(2)}, u32[]{:S(2)}) collective-permute-start(bf16[64,2048]{1,0:T(8,128)(2,1)S(1)} %get-tuple-element.12), channel_id=1, source_target_pairs={{0,2},{2,0},{4,6},{6,4},{1,3},{3,1},{5,7},{7,5},{8,10},{10,8},{12,... | collective-permute-start | bytes 786440 | tf_op jit(solution)/shard_map/ppermute | solution.py:186
  22.5 1.1 %collective-permute-done.13.refs_1_ = bf16[64,2048]{1,0:T(8,128)(2,1)S(1)} collective-permute-done((bf16[64,2048]{1,0:T(8,128)(2,1)S(1)}, bf16[64,2048]{1,0:T(8,128)(2,1)S(1)}, u32[]{:S(2)}, u32[]{:S(2)}) %collective-permute-start.13) | collective-permute-done | bytes 262176 | tf_op jit(solution)/shard_map/ppermute | solution.py:186
  23.6 1.3 %collective-permute-start.14 = (bf16[16,2048]{1,0:T(8,128)(2,1)S(1)}, bf16[16,2048]{1,0:T(8,128)(2,1)S(1)}, u32[]{:S(2)}, u32[]{:S(2)}) collective-permute-start(bf16[16,2048]{1,0:T(8,128)(2,1)S(1)} %shard_map.69), channel_id=1, source_target_pairs={{4,0},{6,2},{0,4},{2,6},{12,8},{14,10},{8,12},{10,14},{20,16},{22,... | collective-permute-start | bytes 196616 | tf_op jit(solution)/shard_map/ppermute | solution.py:183
  24.9 0.9 %collective-permute-start.16 = (bf16[16,2048]{1,0:T(8,128)(2,1)S(1)}, bf16[16,2048]{1,0:T(8,128)(2,1)S(1)}, u32[]{:S(2)}, u32[]{:S(2)}) collective-permute-start(bf16[16,2048]{1,0:T(8,128)(2,1)S(1)} %shard_map.71), channel_id=1, source_target_pairs={{4,0},{6,2},{0,4},{2,6},{12,8},{14,10},{8,12},{10,14},{20,16},{22,... | collective-permute-start | bytes 196616 | tf_op jit(solution)/shard_map/ppermute | solution.py:183
  25.8 1.3 %collective-permute-start.18 = (bf16[16,2048]{1,0:T(8,128)(2,1)S(1)}, bf16[16,2048]{1,0:T(8,128)(2,1)S(1)}, u32[]{:S(2)}, u32[]{:S(2)}) collective-permute-start(bf16[16,2048]{1,0:T(8,128)(2,1)S(1)} %shard_map.73), channel_id=1, source_target_pairs={{4,0},{6,2},{0,4},{2,6},{12,8},{14,10},{8,12},{10,14},{20,16},{22,... | collective-permute-start | bytes 196616 | tf_op jit(solution)/shard_map/ppermute | solution.py:183
  27.1 0.8 %collective-permute-start.20 = (bf16[16,2048]{1,0:T(8,128)(2,1)S(1)}, bf16[16,2048]{1,0:T(8,128)(2,1)S(1)}, u32[]{:S(2)}, u32[]{:S(2)}) collective-permute-start(bf16[16,2048]{1,0:T(8,128)(2,1)S(1)} %shard_map.75), channel_id=1, source_target_pairs={{4,0},{6,2},{0,4},{2,6},{12,8},{14,10},{8,12},{10,14},{20,16},{22,... | collective-permute-start | bytes 196616 | tf_op jit(solution)/shard_map/ppermute | solution.py:183
  28.4 2.7 %collective-permute-start.15 = (bf16[16,2048]{1,0:T(8,128)(2,1)S(1)}, bf16[16,2048]{1,0:T(8,128)(2,1)S(1)}, u32[]{:S(2)}, u32[]{:S(2)}) collective-permute-start(bf16[16,2048]{1,0:T(8,128)(2,1)S(1)} %shard_map.70), channel_id=1, source_target_pairs={{24,0},{26,2},{28,4},{30,6},{16,8},{18,10},{20,12},{22,14},{8,16},... | collective-permute-start | bytes 196616 | tf_op jit(solution)/shard_map/ppermute | solution.py:183
  31.1 0.9 %collective-permute-start.17 = (bf16[16,2048]{1,0:T(8,128)(2,1)S(1)}, bf16[16,2048]{1,0:T(8,128)(2,1)S(1)}, u32[]{:S(2)}, u32[]{:S(2)}) collective-permute-start(bf16[16,2048]{1,0:T(8,128)(2,1)S(1)} %shard_map.72), channel_id=1, source_target_pairs={{16,0},{18,2},{20,4},{22,6},{24,8},{26,10},{28,12},{30,14},{0,16},... | collective-permute-start | bytes 196616 | tf_op jit(solution)/shard_map/ppermute | solution.py:183
  32.1 1.1 %collective-permute-start.19 = (bf16[16,2048]{1,0:T(8,128)(2,1)S(1)}, bf16[16,2048]{1,0:T(8,128)(2,1)S(1)}, u32[]{:S(2)}, u32[]{:S(2)}) collective-permute-start(bf16[16,2048]{1,0:T(8,128)(2,1)S(1)} %shard_map.74), channel_id=1, source_target_pairs={{8,0},{10,2},{12,4},{14,6},{0,8},{2,10},{4,12},{6,14},{24,16},{26,... | collective-permute-start | bytes 196616 | tf_op jit(solution)/shard_map/ppermute | solution.py:183
  33.2 1.5 %collective-permute-done.15 = bf16[16,2048]{1,0:T(8,128)(2,1)S(1)} collective-permute-done((bf16[16,2048]{1,0:T(8,128)(2,1)S(1)}, bf16[16,2048]{1,0:T(8,128)(2,1)S(1)}, u32[]{:S(2)}, u32[]{:S(2)}) %collective-permute-start.15) | collective-permute-done | bytes 65568 | tf_op jit(solution)/shard_map/ppermute | solution.py:183
  34.6 2.4 %collective-permute-done.17 = bf16[16,2048]{1,0:T(8,128)(2,1)S(1)} collective-permute-done((bf16[16,2048]{1,0:T(8,128)(2,1)S(1)}, bf16[16,2048]{1,0:T(8,128)(2,1)S(1)}, u32[]{:S(2)}, u32[]{:S(2)}) %collective-permute-start.17) | collective-permute-done | bytes 65568 | tf_op jit(solution)/shard_map/ppermute | solution.py:183
  37.3 0.7 %convert_add_fusion = f32[16,2048]{1,0:T(8,128)} fusion(bf16[16,2048]{1,0:T(8,128)(2,1)S(1)} %collective-permute-done.20, bf16[16,2048]{1,0:T(8,128)(2,1)S(1)} %collective-permute-done.19, bf16[16,2048]{1,0:T(8,128)(2,1)S(1)} %collective-permute-done.17, bf16[16,2048]{1,0:T(8,128)(2,1)S(1)} %collective-permute-done.15, ...), kind=kLoop, calls=%fused_computation | loop fusion | flops 327680 | bytes 589824 | tf_op jit(solution)/shard_map/add | solution.py:230
  (43 shorter events, 1.4 us)
Async XLA Ops:
  0.8 17.9 %copy-start = (bf16[1,2048,768]{2,1,0:T(8,128)(2,1)S(1)}, bf16[1,2048,768]{2,1,0:T(8,128)(2,1)}, u32[]{:S(2)}) copy-start(bf16[1,2048,768]{2,1,0:T(8,128)(2,1)} %refs_2_.1) | copy-start | bytes 9437188
  0.8 18.0 %copy-start.1 = (bf16[1,2048,768]{2,1,0:T(8,128)(2,1)S(1)}, bf16[1,2048,768]{2,1,0:T(8,128)(2,1)}, u32[]{:S(2)}) copy-start(bf16[1,2048,768]{2,1,0:T(8,128)(2,1)} %refs_3_.1) | copy-start | bytes 9437188
  0.9 18.0 %copy-start.2 = (bf16[1,768,2048]{2,1,0:T(8,128)(2,1)S(1)}, bf16[1,768,2048]{2,1,0:T(8,128)(2,1)}, u32[]{:S(2)}) copy-start(bf16[1,768,2048]{2,1,0:T(8,128)(2,1)} %refs_4_.1) | copy-start | bytes 9437188
  1.0 7.1 %collective-permute-start.8 = (bf16[16,2176]{1,0:T(8,128)(2,1)S(1)}, bf16[16,2176]{1,0:T(8,128)(2,1)S(1)}, u32[]{:S(2)}, u32[]{:S(2)}) collective-permute-start(bf16[16,2176]{1,0:T(8,128)(2,1)S(1)} %shard_map.65.refs_0_), channel_id=1, source_target_pairs={{0,12},{2,14},{4,8},{6,10},{8,4},{10,6},{12,0},{14,2},{16,28},{18,... | collective-permute-start | bytes 208904 | tf_op jit(solution)/shard_map/ppermute | solution.py:183
  5.0 6.8 %collective-permute-start.2 = (bf16[16,2176]{1,0:T(8,128)(2,1)S(1)}, bf16[16,2176]{1,0:T(8,128)(2,1)S(1)}, u32[]{:S(2)}, u32[]{:S(2)}) collective-permute-start(bf16[16,2176]{1,0:T(8,128)(2,1)S(1)} %shard_map.65.refs_0_), channel_id=1, source_target_pairs={{0,24},{2,26},{4,28},{6,30},{8,16},{10,18},{12,20},{14,22},{16,8},... | collective-permute-start | bytes 208904 | tf_op jit(solution)/shard_map/ppermute | solution.py:183
  7.5 4.4 %collective-permute-start.7 = (bf16[16,2176]{1,0:T(8,128)(2,1)S(1)}, bf16[16,2176]{1,0:T(8,128)(2,1)S(1)}, u32[]{:S(2)}, u32[]{:S(2)}) collective-permute-start(bf16[16,2176]{1,0:T(8,128)(2,1)S(1)} %shard_map.65.refs_0_), channel_id=1, source_target_pairs={{0,4},{2,6},{4,0},{6,2},{8,12},{10,14},{12,8},{14,10},{16,20},{18,... | collective-permute-start | bytes 208904 | tf_op jit(solution)/shard_map/ppermute | solution.py:183
  8.0 6.4 %collective-permute-start.1 = (bf16[16,2176]{1,0:T(8,128)(2,1)S(1)}, bf16[16,2176]{1,0:T(8,128)(2,1)S(1)}, u32[]{:S(2)}, u32[]{:S(2)}) collective-permute-start(bf16[16,2176]{1,0:T(8,128)(2,1)S(1)} %shard_map.65.refs_0_), channel_id=1, source_target_pairs={{0,16},{2,18},{4,20},{6,22},{8,24},{10,26},{12,28},{14,30},{16,0},... | collective-permute-start | bytes 208904 | tf_op jit(solution)/shard_map/ppermute | solution.py:183
  8.1 7.5 %collective-permute-start.3 = (bf16[16,2176]{1,0:T(8,128)(2,1)S(1)}, bf16[16,2176]{1,0:T(8,128)(2,1)S(1)}, u32[]{:S(2)}, u32[]{:S(2)}) collective-permute-start(bf16[16,2176]{1,0:T(8,128)(2,1)S(1)} %shard_map.65.refs_0_), channel_id=1, source_target_pairs={{0,2},{2,0},{4,6},{6,4},{1,3},{3,1},{5,7},{7,5},{8,10},{10,8},{12,... | collective-permute-start | bytes 208904 | tf_op jit(solution)/shard_map/ppermute | solution.py:186
  8.1 7.5 %collective-permute-start = (bf16[16,2176]{1,0:T(8,128)(2,1)S(1)}, bf16[16,2176]{1,0:T(8,128)(2,1)S(1)}, u32[]{:S(2)}, u32[]{:S(2)}) collective-permute-start(bf16[16,2176]{1,0:T(8,128)(2,1)S(1)} %shard_map.65.refs_0_), channel_id=1, source_target_pairs={{0,8},{2,10},{4,12},{6,14},{8,0},{10,2},{12,4},{14,6},{16,24},{18,... | collective-permute-start | bytes 208904 | tf_op jit(solution)/shard_map/ppermute | solution.py:183
  11.9 4.3 %collective-permute-start.10 = (bf16[16,2176]{1,0:T(8,128)(2,1)S(1)}, bf16[16,2176]{1,0:T(8,128)(2,1)S(1)}, u32[]{:S(2)}, u32[]{:S(2)}) collective-permute-start(bf16[16,2176]{1,0:T(8,128)(2,1)S(1)} %collective-permute-done.2.refs_3_), channel_id=1, source_target_pairs={{0,4},{2,6},{4,0},{6,2},{8,12},{10,14},{12,8},{14,10},{16,20},{18,... | collective-permute-start | bytes 208904 | tf_op jit(solution)/shard_map/ppermute | solution.py:183
  11.9 4.3 %collective-permute-start.6 = (bf16[16,2176]{1,0:T(8,128)(2,1)S(1)}, bf16[16,2176]{1,0:T(8,128)(2,1)S(1)}, u32[]{:S(2)}, u32[]{:S(2)}) collective-permute-start(bf16[16,2176]{1,0:T(8,128)(2,1)S(1)} %collective-permute-done.2.refs_3_), channel_id=1, source_target_pairs={{0,2},{2,0},{4,6},{6,4},{1,3},{3,1},{5,7},{7,5},{8,10},{10,8},{12,... | collective-permute-start | bytes 208904 | tf_op jit(solution)/shard_map/ppermute | solution.py:186
  14.4 4.3 %collective-permute-start.9 = (bf16[16,2176]{1,0:T(8,128)(2,1)S(1)}, bf16[16,2176]{1,0:T(8,128)(2,1)S(1)}, u32[]{:S(2)}, u32[]{:S(2)}) collective-permute-start(bf16[16,2176]{1,0:T(8,128)(2,1)S(1)} %collective-permute-done.1.refs_2_), channel_id=1, source_target_pairs={{0,4},{2,6},{4,0},{6,2},{8,12},{10,14},{12,8},{14,10},{16,20},{18,... | collective-permute-start | bytes 208904 | tf_op jit(solution)/shard_map/ppermute | solution.py:183
  15.6 3.1 %collective-permute-start.5 = (bf16[16,2176]{1,0:T(8,128)(2,1)S(1)}, bf16[16,2176]{1,0:T(8,128)(2,1)S(1)}, u32[]{:S(2)}, u32[]{:S(2)}) collective-permute-start(bf16[16,2176]{1,0:T(8,128)(2,1)S(1)} %collective-permute-done.1.refs_2_), channel_id=1, source_target_pairs={{0,2},{2,0},{4,6},{6,4},{1,3},{3,1},{5,7},{7,5},{8,10},{10,8},{12,... | collective-permute-start | bytes 208904 | tf_op jit(solution)/shard_map/ppermute | solution.py:186
  15.6 3.1 %collective-permute-start.4 = (bf16[16,2176]{1,0:T(8,128)(2,1)S(1)}, bf16[16,2176]{1,0:T(8,128)(2,1)S(1)}, u32[]{:S(2)}, u32[]{:S(2)}) collective-permute-start(bf16[16,2176]{1,0:T(8,128)(2,1)S(1)} %collective-permute-done.refs_1_), channel_id=1, source_target_pairs={{0,2},{2,0},{4,6},{6,4},{1,3},{3,1},{5,7},{7,5},{8,10},{10,8},{12,... | collective-permute-start | bytes 208904 | tf_op jit(solution)/shard_map/ppermute | solution.py:186
  18.7 1.6 %collective-permute-start.12 = (bf16[64,2176]{1,0:T(8,128)(2,1)S(1)}, bf16[64,2176]{1,0:T(8,128)(2,1)S(1)}, u32[]{:S(2)}, u32[]{:S(2)}) collective-permute-start(bf16[64,2176]{1,0:T(8,128)(2,1)S(1)} %shard_map.66.refs_11_.refs_0_), channel_id=1, source_target_pairs={{0,2},{2,0},{4,6},{6,4},{1,3},{3,1},{5,7},{7,5},{8,10},{10,8},{12,... | collective-permute-start | bytes 835592 | tf_op jit(solution)/shard_map/ppermute | solution.py:186
  21.9 1.7 %collective-permute-start.13 = (bf16[64,2048]{1,0:T(8,128)(2,1)S(1)}, bf16[64,2048]{1,0:T(8,128)(2,1)S(1)}, u32[]{:S(2)}, u32[]{:S(2)}) collective-permute-start(bf16[64,2048]{1,0:T(8,128)(2,1)S(1)} %get-tuple-element.12), channel_id=1, source_target_pairs={{0,2},{2,0},{4,6},{6,4},{1,3},{3,1},{5,7},{7,5},{8,10},{10,8},{12,... | collective-permute-start | bytes 786440 | tf_op jit(solution)/shard_map/ppermute | solution.py:186
  22.4 5.6 %collective-permute-start.11 = (bf16[64,2048]{1,0:T(8,128)(2,1)S(1)}, bf16[64,2048]{1,0:T(8,128)(2,1)S(1)}, u32[]{:S(2)}, u32[]{:S(2)}) collective-permute-start(bf16[64,2048]{1,0:T(8,128)(2,1)S(1)} %get-tuple-element.10), channel_id=1, source_target_pairs={{0,2},{2,0},{4,6},{6,4},{1,3},{3,1},{5,7},{7,5},{8,10},{10,8},{12,... | collective-permute-start | bytes 786440 | tf_op jit(solution)/shard_map/ppermute | solution.py:186
  23.6 4.8 %collective-permute-start.14 = (bf16[16,2048]{1,0:T(8,128)(2,1)S(1)}, bf16[16,2048]{1,0:T(8,128)(2,1)S(1)}, u32[]{:S(2)}, u32[]{:S(2)}) collective-permute-start(bf16[16,2048]{1,0:T(8,128)(2,1)S(1)} %shard_map.69), channel_id=1, source_target_pairs={{4,0},{6,2},{0,4},{2,6},{12,8},{14,10},{8,12},{10,14},{20,16},{22,... | collective-permute-start | bytes 196616 | tf_op jit(solution)/shard_map/ppermute | solution.py:183
  24.9 6.2 %collective-permute-start.16 = (bf16[16,2048]{1,0:T(8,128)(2,1)S(1)}, bf16[16,2048]{1,0:T(8,128)(2,1)S(1)}, u32[]{:S(2)}, u32[]{:S(2)}) collective-permute-start(bf16[16,2048]{1,0:T(8,128)(2,1)S(1)} %shard_map.71), channel_id=1, source_target_pairs={{4,0},{6,2},{0,4},{2,6},{12,8},{14,10},{8,12},{10,14},{20,16},{22,... | collective-permute-start | bytes 196616 | tf_op jit(solution)/shard_map/ppermute | solution.py:183
  25.8 6.3 %collective-permute-start.18 = (bf16[16,2048]{1,0:T(8,128)(2,1)S(1)}, bf16[16,2048]{1,0:T(8,128)(2,1)S(1)}, u32[]{:S(2)}, u32[]{:S(2)}) collective-permute-start(bf16[16,2048]{1,0:T(8,128)(2,1)S(1)} %shard_map.73), channel_id=1, source_target_pairs={{4,0},{6,2},{0,4},{2,6},{12,8},{14,10},{8,12},{10,14},{20,16},{22,... | collective-permute-start | bytes 196616 | tf_op jit(solution)/shard_map/ppermute | solution.py:183
  27.1 6.0 %collective-permute-start.20 = (bf16[16,2048]{1,0:T(8,128)(2,1)S(1)}, bf16[16,2048]{1,0:T(8,128)(2,1)S(1)}, u32[]{:S(2)}, u32[]{:S(2)}) collective-permute-start(bf16[16,2048]{1,0:T(8,128)(2,1)S(1)} %shard_map.75), channel_id=1, source_target_pairs={{4,0},{6,2},{0,4},{2,6},{12,8},{14,10},{8,12},{10,14},{20,16},{22,... | collective-permute-start | bytes 196616 | tf_op jit(solution)/shard_map/ppermute | solution.py:183
  28.4 6.2 %collective-permute-start.15 = (bf16[16,2048]{1,0:T(8,128)(2,1)S(1)}, bf16[16,2048]{1,0:T(8,128)(2,1)S(1)}, u32[]{:S(2)}, u32[]{:S(2)}) collective-permute-start(bf16[16,2048]{1,0:T(8,128)(2,1)S(1)} %shard_map.70), channel_id=1, source_target_pairs={{24,0},{26,2},{28,4},{30,6},{16,8},{18,10},{20,12},{22,14},{8,16},... | collective-permute-start | bytes 196616 | tf_op jit(solution)/shard_map/ppermute | solution.py:183
  31.1 6.0 %collective-permute-start.17 = (bf16[16,2048]{1,0:T(8,128)(2,1)S(1)}, bf16[16,2048]{1,0:T(8,128)(2,1)S(1)}, u32[]{:S(2)}, u32[]{:S(2)}) collective-permute-start(bf16[16,2048]{1,0:T(8,128)(2,1)S(1)} %shard_map.72), channel_id=1, source_target_pairs={{16,0},{18,2},{20,4},{22,6},{24,8},{26,10},{28,12},{30,14},{0,16},... | collective-permute-start | bytes 196616 | tf_op jit(solution)/shard_map/ppermute | solution.py:183
  32.1 5.2 %collective-permute-start.19 = (bf16[16,2048]{1,0:T(8,128)(2,1)S(1)}, bf16[16,2048]{1,0:T(8,128)(2,1)S(1)}, u32[]{:S(2)}, u32[]{:S(2)}) collective-permute-start(bf16[16,2048]{1,0:T(8,128)(2,1)S(1)} %shard_map.74), channel_id=1, source_target_pairs={{8,0},{10,2},{12,4},{14,6},{0,8},{2,10},{4,12},{6,14},{24,16},{26,... | collective-permute-start | bytes 196616 | tf_op jit(solution)/shard_map/ppermute | solution.py:183
  (3 other events, 2.5 us)

commit v2 on v0

--- a/solution.py
+++ b/solution.py
@@ -88,8 +88,8 @@
         at += ref.shape[0]
 
 
-def expert_kernel(count, place_ref, *refs):
-    kept_ref, given_ref, held = refs[-3:]
+def expert_kernel(count, starts, place_ref, *refs):
+    kept_ref, *given_refs, held = refs[-2 - len(starts) :]
     gate_ref, up_ref, down_ref = refs[count : count + 3]
     rows, model_width = kept_ref.shape
     join(refs[:count], held)
@@ -100,22 +100,27 @@
     hidden = activate(gate_pre, up_pre)
     result = jnp.dot(hidden, down_ref[0], preferred_element_type=jnp.float32) * scale
     kept_ref[...] = result[:rows]
-    given_ref[...] = result[rows:].astype(given_ref.dtype)
-
-
-def expert_rows(place, weights, own, other, *after):
+    for ref, at in zip(given_refs, starts):
+        ref[...] = result[rows + at : rows + at + ref.shape[0]].astype(ref.dtype)
+
+
+def expert_rows(place, weights, own, other, *after, alone=None):
     width = own[0].shape[1]
     _, model_width, hidden_width = weights[0].shape
     count = len(own) + len(other)
     rows = sum(piece.shape[0] for piece in own)
-    return pl.pallas_call(
-        functools.partial(expert_kernel, count),
+    starts, parts = [0], [rows]
+    if alone is not None:
+        starts.append(alone[0])
+        parts.append(alone[1])
+    return pl.pallas_call(
+        functools.partial(expert_kernel, count, starts),
         out_shape=[
             jax.ShapeDtypeStruct((rows, model_width), jnp.float32),
-            jax.ShapeDtypeStruct((rows, model_width), jnp.bfloat16),
+            *[jax.ShapeDtypeStruct((part, model_width), jnp.bfloat16) for part in parts],
         ],
         in_specs=[VMEM] * (count + 4) + [HBM] * len(after),
-        out_specs=[VMEM] * 2,
+        out_specs=[VMEM] * (1 + len(parts)),
         scratch_shapes=[pltpu.VMEM((2 * rows, width), jnp.bfloat16)],
         compiler_params=pltpu.CompilerParams(vmem_limit_bytes=16 << 20),
         cost_estimate=pl.CostEstimate(
@@ -201,8 +206,12 @@
         near_kept, near_back = expert_rows(
             place, weights, near, near_other, far_block
         )
-        far_kept, far_back = expert_rows(place, weights, [far_block], [swap(far_block)], near_kept)
-        far_back, near_back = swap(far_back), swap(near_back)
+        ahead = ((width - 1) * (chips - 1) * tok_rows, tok_rows)
+        far_kept, far_back, far_ahead = expert_rows(
+            place, weights, [far_block], [swap(far_block)], near_kept, alone=ahead
+        )
+        far_ahead = swap(far_ahead)
+        far_back, near_back = swap(pack([far_back], far_ahead)), swap(near_back)
 
         def near_sum(at, *terms):
             begin = at * tok_rows
@@ -210,7 +219,8 @@
 
         def far_sum(at, s):
             begin = (at * (chips - 1) + s - 1) * tok_rows
-            return add_rows(begin, tok_rows, jnp.bfloat16, far_kept, far_back)
+            back = far_ahead if begin == ahead[0] else far_back
+            return add_rows(begin, tok_rows, jnp.bfloat16, far_kept, back)
 
         terms = []
         if first == 0:

time: 37.5 us -> 38.6 us (1.029)
  waiting for transfers between devices: 11.2 us -> 12.1 us
    ppermute x14, waiting for transfers between devices: 10.1 us -> 11.1 us  [step_to(): lax.ppermute(value, ('grp', 'exp'), [(d, o) for o, d in pairs] if back el...]
    ppermute x7 -> x8, starting transfers between devices: 0.86 us -> 1.35 us  [swap(): return lax.ppermute(value, 'exp', [(i, i ^ 1) for i in range(owners)])]
    ppermute x7 -> x8, waiting for transfers between devices: 1.1 us -> 1.02 us  [swap(): return lax.ppermute(value, 'exp', [(i, i ^ 1) for i in range(owners)])]
  transfers between devices with their start and end apart: 21 -> 22, of which waited for: 8 -> 10; matrix products, arithmetic and copies ran while one was open for 0% -> 0% of each run, Pallas kernels for 4% -> 4%
where the time goes in v2:
time: 38.6 us; the launch traced here: 38.5 us
  starting transfers between devices  21.3 us (55%)
  waiting for transfers between devices  12.1 us (31%)
  Pallas kernels  3.38 us (9%)
  local copies, waits for them, and re-layouts  0.85 us (2%)
  other arithmetic  0.7 us (2%)
    ppermute x14, starting transfers between devices, step_to(): lax.ppermute(value, ('grp', 'exp'), [(d, o) for o, d in pairs] if back el...  19.9 us
    ppermute x14, waiting for transfers between devices, step_to(): lax.ppermute(value, ('grp', 'exp'), [(d, o) for o, d in pairs] if back el...  11.1 us
    pallas_call x2, Pallas kernels, expert_rows(): pl.pallas_call(functools.partial(expert_kernel, count, starts), out_shape...  3.01 us
    ppermute x8, starting transfers between devices, swap(): return lax.ppermute(value, 'exp', [(i, i ^ 1) for i in range(owners)])  1.35 us
    ppermute x8, waiting for transfers between devices, swap(): return lax.ppermute(value, 'exp', [(i, i ^ 1) for i in range(owners)])  1.02 us
    unnamed x12, local copies, waits for them, and re-layouts  0.85 us
  transfers between devices with their start and end apart: 22, of which 10 were waited for; matrix products, arithmetic and copies ran while one was open for 0% of the time, Pallas kernels for 4%

profile of v2, /device:TPU:0, one launch (start us, length us, event | category | flops | bytes accessed | tf_op | source)
XLA Modules:
  0.0 38.5 jit_solution(18229371461608438112)
XLA Ops:
  0.0 0.8 %copy-done.3 = bf16[16,2048]{1,0:T(8,128)(2,1)S(1)} copy-done((bf16[16,2048]{1,0:T(8,128)(2,1)S(1)}, bf16[16,2048]{1,0:T(8,128)(2,1)}, u32[]{:S(2)}) %copy-start.3) | copy-done | bytes 65560
  1.0 5.1 %collective-permute-start.2 = (bf16[16,2176]{1,0:T(8,128)(2,1)S(1)}, bf16[16,2176]{1,0:T(8,128)(2,1)S(1)}, u32[]{:S(2)}, u32[]{:S(2)}) collective-permute-start(bf16[16,2176]{1,0:T(8,128)(2,1)S(1)} %shard_map.65.refs_0_), channel_id=1, source_target_pairs={{0,24},{2,26},{4,28},{6,30},{8,16},{10,18},{12,20},{14,22},{16,8},... | collective-permute-start | bytes 208904 | tf_op jit(solution)/shard_map/ppermute | solution.py:188
  6.1 1.5 %collective-permute-start.7 = (bf16[16,2176]{1,0:T(8,128)(2,1)S(1)}, bf16[16,2176]{1,0:T(8,128)(2,1)S(1)}, u32[]{:S(2)}, u32[]{:S(2)}) collective-permute-start(bf16[16,2176]{1,0:T(8,128)(2,1)S(1)} %shard_map.65.refs_0_), channel_id=1, source_target_pairs={{0,4},{2,6},{4,0},{6,2},{8,12},{10,14},{12,8},{14,10},{16,20},{18,... | collective-permute-start | bytes 208904 | tf_op jit(solution)/shard_map/ppermute | solution.py:188
  7.6 0.8 %collective-permute-start = (bf16[16,2176]{1,0:T(8,128)(2,1)S(1)}, bf16[16,2176]{1,0:T(8,128)(2,1)S(1)}, u32[]{:S(2)}, u32[]{:S(2)}) collective-permute-start(bf16[16,2176]{1,0:T(8,128)(2,1)S(1)} %shard_map.65.refs_0_), channel_id=1, source_target_pairs={{0,8},{2,10},{4,12},{6,14},{8,0},{10,2},{12,4},{14,6},{16,24},{18,... | collective-permute-start | bytes 208904 | tf_op jit(solution)/shard_map/ppermute | solution.py:188
  8.6 1.9 %collective-permute-start.10 = (bf16[16,2176]{1,0:T(8,128)(2,1)S(1)}, bf16[16,2176]{1,0:T(8,128)(2,1)S(1)}, u32[]{:S(2)}, u32[]{:S(2)}) collective-permute-start(bf16[16,2176]{1,0:T(8,128)(2,1)S(1)} %collective-permute-done.2.refs_3_), channel_id=1, source_target_pairs={{0,4},{2,6},{4,0},{6,2},{8,12},{10,14},{12,8},{14,10},{16,20},{18,... | collective-permute-start | bytes 208904 | tf_op jit(solution)/shard_map/ppermute | solution.py:188
  10.5 2.4 %collective-permute-done.1.refs_2_ = bf16[16,2176]{1,0:T(8,128)(2,1)S(1)} collective-permute-done((bf16[16,2176]{1,0:T(8,128)(2,1)S(1)}, bf16[16,2176]{1,0:T(8,128)(2,1)S(1)}, u32[]{:S(2)}, u32[]{:S(2)}) %collective-permute-start.1) | collective-permute-done | bytes 69664 | tf_op jit(solution)/shard_map/ppermute | solution.py:188
  12.9 0.7 %collective-permute-start.9 = (bf16[16,2176]{1,0:T(8,128)(2,1)S(1)}, bf16[16,2176]{1,0:T(8,128)(2,1)S(1)}, u32[]{:S(2)}, u32[]{:S(2)}) collective-permute-start(bf16[16,2176]{1,0:T(8,128)(2,1)S(1)} %collective-permute-done.1.refs_2_), channel_id=1, source_target_pairs={{0,4},{2,6},{4,0},{6,2},{8,12},{10,14},{12,8},{14,10},{16,20},{18,... | collective-permute-start | bytes 208904 | tf_op jit(solution)/shard_map/ppermute | solution.py:188
  13.6 1.4 %collective-permute-start.8 = (bf16[16,2176]{1,0:T(8,128)(2,1)S(1)}, bf16[16,2176]{1,0:T(8,128)(2,1)S(1)}, u32[]{:S(2)}, u32[]{:S(2)}) collective-permute-start(bf16[16,2176]{1,0:T(8,128)(2,1)S(1)} %collective-permute-done.refs_1_), channel_id=1, source_target_pairs={{0,4},{2,6},{4,0},{6,2},{8,12},{10,14},{12,8},{14,10},{16,20},{18,... | collective-permute-start | bytes 208904 | tf_op jit(solution)/shard_map/ppermute | solution.py:188
  15.2 2.5 %collective-permute-done.9.refs_2_ = bf16[16,2176]{1,0:T(8,128)(2,1)S(1)} collective-permute-done((bf16[16,2176]{1,0:T(8,128)(2,1)S(1)}, bf16[16,2176]{1,0:T(8,128)(2,1)S(1)}, u32[]{:S(2)}, u32[]{:S(2)}) %collective-permute-start.9) | collective-permute-done | bytes 69664 | tf_op jit(solution)/shard_map/ppermute | solution.py:188
  17.8 1.0 %collective-permute-done.8.refs_1_ = bf16[16,2176]{1,0:T(8,128)(2,1)S(1)} collective-permute-done((bf16[16,2176]{1,0:T(8,128)(2,1)S(1)}, bf16[16,2176]{1,0:T(8,128)(2,1)S(1)}, u32[]{:S(2)}, u32[]{:S(2)}) %collective-permute-start.8) | collective-permute-done | bytes 69664 | tf_op jit(solution)/shard_map/ppermute | solution.py:188
  18.9 1.5 %shard_map.67 = (f32[64,2048]{1,0:T(8,128)S(1)}, bf16[64,2048]{1,0:T(8,128)(2,1)S(1)}) custom-call(s32[8,128]{1,0:T(8,128)S(1)} %shard_map.64.place_ref, bf16[16,2176]{1,0:T(8,128)(2,1)S(1)} %shard_map.65.refs_0_, bf16[16,2176]{1,0:T(8,128)(2,1)S(1)} %collective-permute-done.refs_1_, bf16[16,2176]{1,0:T(8,128)(2,1)S(1)} %collective-permute-done.1.refs_2_, ...), custom_call_target="tpu_custom_call" | custom-call | flops 1207959552 | tf_op jit(solution)/shard_map/pallas_call | solution.py:116
  20.4 1.5 %shard_map.68 = (f32[64,2048]{1,0:T(8,128)S(1)}, bf16[64,2048]{1,0:T(8,128)(2,1)S(1)}, bf16[16,2048]{1,0:T(8,128)(2,1)S(1)}) custom-call(s32[8,128]{1,0:T(8,128)S(1)} %shard_map.64.place_ref, bf16[64,2176]{1,0:T(8,128)(2,1)S(1)} %shard_map.66.refs_11_.refs_0_, bf16[64,2176]{1,0:T(8,128)(2,1)S(1)} %collective-permute-done.12.refs_1_, ...), custom_call_target="tpu_custom_call" | custom-call | flops 1207959552 | tf_op jit(solution)/shard_map/pallas_call | solution.py:116
  21.9 0.5 %collective-permute-start.13 = (bf16[16,2048]{1,0:T(8,128)(2,1)S(1)}, bf16[16,2048]{1,0:T(8,128)(2,1)S(1)}, u32[]{:S(2)}, u32[]{:S(2)}) collective-permute-start(bf16[16,2048]{1,0:T(8,128)(2,1)S(1)} %get-tuple-element.13), channel_id=1, source_target_pairs={{0,2},{2,0},{4,6},{6,4},{1,3},{3,1},{5,7},{7,5},{8,10},{10,8},{12,... | collective-permute-start | bytes 196616 | tf_op jit(solution)/shard_map/ppermute | solution.py:191
  22.5 0.9 %collective-permute-done.13.refs_1_ = bf16[16,2048]{1,0:T(8,128)(2,1)S(1)} collective-permute-done((bf16[16,2048]{1,0:T(8,128)(2,1)S(1)}, bf16[16,2048]{1,0:T(8,128)(2,1)S(1)}, u32[]{:S(2)}, u32[]{:S(2)}) %collective-permute-start.13) | collective-permute-done | bytes 65568 | tf_op jit(solution)/shard_map/ppermute | solution.py:191
  24.0 0.9 %collective-permute-start.14 = (bf16[16,2048]{1,0:T(8,128)(2,1)S(1)}, bf16[16,2048]{1,0:T(8,128)(2,1)S(1)}, u32[]{:S(2)}, u32[]{:S(2)}) collective-permute-start(bf16[16,2048]{1,0:T(8,128)(2,1)S(1)} %shard_map.69), channel_id=1, source_target_pairs={{4,0},{6,2},{0,4},{2,6},{12,8},{14,10},{8,12},{10,14},{20,16},{22,... | collective-permute-start | bytes 196616 | tf_op jit(solution)/shard_map/ppermute | solution.py:188
  25.0 1.2 %collective-permute-start.17 = (bf16[16,2048]{1,0:T(8,128)(2,1)S(1)}, bf16[16,2048]{1,0:T(8,128)(2,1)S(1)}, u32[]{:S(2)}, u32[]{:S(2)}) collective-permute-start(bf16[16,2048]{1,0:T(8,128)(2,1)S(1)} %shard_map.72), channel_id=1, source_target_pairs={{4,0},{6,2},{0,4},{2,6},{12,8},{14,10},{8,12},{10,14},{20,16},{22,... | collective-permute-start | bytes 196616 | tf_op jit(solution)/shard_map/ppermute | solution.py:188
  26.2 1.0 %collective-permute-start.19 = (bf16[16,2048]{1,0:T(8,128)(2,1)S(1)}, bf16[16,2048]{1,0:T(8,128)(2,1)S(1)}, u32[]{:S(2)}, u32[]{:S(2)}) collective-permute-start(bf16[16,2048]{1,0:T(8,128)(2,1)S(1)} %shard_map.74), channel_id=1, source_target_pairs={{4,0},{6,2},{0,4},{2,6},{12,8},{14,10},{8,12},{10,14},{20,16},{22,... | collective-permute-start | bytes 196616 | tf_op jit(solution)/shard_map/ppermute | solution.py:188
  27.2 1.6 %collective-permute-done.14.refs_2_ = bf16[16,2048]{1,0:T(8,128)(2,1)S(1)} collective-permute-done((bf16[16,2048]{1,0:T(8,128)(2,1)S(1)}, bf16[16,2048]{1,0:T(8,128)(2,1)S(1)}, u32[]{:S(2)}, u32[]{:S(2)}) %collective-permute-start.14) | collective-permute-done | bytes 65568 | tf_op jit(solution)/shard_map/ppermute | solution.py:188
  28.8 2.3 %collective-permute-start.15 = (bf16[16,2048]{1,0:T(8,128)(2,1)S(1)}, bf16[16,2048]{1,0:T(8,128)(2,1)S(1)}, u32[]{:S(2)}, u32[]{:S(2)}) collective-permute-start(bf16[16,2048]{1,0:T(8,128)(2,1)S(1)} %shard_map.70), channel_id=1, source_target_pairs={{24,0},{26,2},{28,4},{30,6},{16,8},{18,10},{20,12},{22,14},{8,16},... | collective-permute-start | bytes 196616 | tf_op jit(solution)/shard_map/ppermute | solution.py:188
  31.1 1.2 %collective-permute-start.21 = (bf16[16,2048]{1,0:T(8,128)(2,1)S(1)}, bf16[16,2048]{1,0:T(8,128)(2,1)S(1)}, u32[]{:S(2)}, u32[]{:S(2)}) collective-permute-start(bf16[16,2048]{1,0:T(8,128)(2,1)S(1)} %shard_map.76), channel_id=1, source_target_pairs={{4,0},{6,2},{0,4},{2,6},{12,8},{14,10},{8,12},{10,14},{20,16},{22,... | collective-permute-start | bytes 196616 | tf_op jit(solution)/shard_map/ppermute | solution.py:188
  32.5 1.9 %collective-permute-start.20 = (bf16[16,2048]{1,0:T(8,128)(2,1)S(1)}, bf16[16,2048]{1,0:T(8,128)(2,1)S(1)}, u32[]{:S(2)}, u32[]{:S(2)}) collective-permute-start(bf16[16,2048]{1,0:T(8,128)(2,1)S(1)} %shard_map.75), channel_id=1, source_target_pairs={{8,0},{10,2},{12,4},{14,6},{0,8},{2,10},{4,12},{6,14},{24,16},{26,... | collective-permute-start | bytes 196616 | tf_op jit(solution)/shard_map/ppermute | solution.py:188
  34.4 0.7 %collective-permute-done.15 = bf16[16,2048]{1,0:T(8,128)(2,1)S(1)} collective-permute-done((bf16[16,2048]{1,0:T(8,128)(2,1)S(1)}, bf16[16,2048]{1,0:T(8,128)(2,1)S(1)}, u32[]{:S(2)}, u32[]{:S(2)}) %collective-permute-start.15) | collective-permute-done | bytes 65568 | tf_op jit(solution)/shard_map/ppermute | solution.py:188
  35.4 2.3 %collective-permute-done.18 = bf16[16,2048]{1,0:T(8,128)(2,1)S(1)} collective-permute-done((bf16[16,2048]{1,0:T(8,128)(2,1)S(1)}, bf16[16,2048]{1,0:T(8,128)(2,1)S(1)}, u32[]{:S(2)}, u32[]{:S(2)}) %collective-permute-start.18) | collective-permute-done | bytes 65568 | tf_op jit(solution)/shard_map/ppermute | solution.py:188
  37.8 0.7 %convert_add_fusion = f32[16,2048]{1,0:T(8,128)} fusion(bf16[16,2048]{1,0:T(8,128)(2,1)S(1)} %collective-permute-done.21, bf16[16,2048]{1,0:T(8,128)(2,1)S(1)} %collective-permute-done.20, bf16[16,2048]{1,0:T(8,128)(2,1)S(1)} %collective-permute-done.18, bf16[16,2048]{1,0:T(8,128)(2,1)S(1)} %collective-permute-done.15, ...), kind=kLoop, calls=%fused_computation | loop fusion | flops 327680 | bytes 589824 | tf_op jit(solution)/shard_map/add | solution.py:236
  (46 shorter events, 2.0 us)
Async XLA Ops:
  0.8 18.0 %copy-start.1 = (bf16[1,2048,768]{2,1,0:T(8,128)(2,1)S(1)}, bf16[1,2048,768]{2,1,0:T(8,128)(2,1)}, u32[]{:S(2)}) copy-start(bf16[1,2048,768]{2,1,0:T(8,128)(2,1)} %refs_3_.1) | copy-start | bytes 9437188
  0.9 18.0 %copy-start.2 = (bf16[1,768,2048]{2,1,0:T(8,128)(2,1)S(1)}, bf16[1,768,2048]{2,1,0:T(8,128)(2,1)}, u32[]{:S(2)}) copy-start(bf16[1,768,2048]{2,1,0:T(8,128)(2,1)} %refs_4_.1) | copy-start | bytes 9437188
  1.0 7.5 %collective-permute-start.2 = (bf16[16,2176]{1,0:T(8,128)(2,1)S(1)}, bf16[16,2176]{1,0:T(8,128)(2,1)S(1)}, u32[]{:S(2)}, u32[]{:S(2)}) collective-permute-start(bf16[16,2176]{1,0:T(8,128)(2,1)S(1)} %shard_map.65.refs_0_), channel_id=1, source_target_pairs={{0,24},{2,26},{4,28},{6,30},{8,16},{10,18},{12,20},{14,22},{16,8},... | collective-permute-start | bytes 208904 | tf_op jit(solution)/shard_map/ppermute | solution.py:188
  6.1 4.4 %collective-permute-start.7 = (bf16[16,2176]{1,0:T(8,128)(2,1)S(1)}, bf16[16,2176]{1,0:T(8,128)(2,1)S(1)}, u32[]{:S(2)}, u32[]{:S(2)}) collective-permute-start(bf16[16,2176]{1,0:T(8,128)(2,1)S(1)} %shard_map.65.refs_0_), channel_id=1, source_target_pairs={{0,4},{2,6},{4,0},{6,2},{8,12},{10,14},{12,8},{14,10},{16,20},{18,... | collective-permute-start | bytes 208904 | tf_op jit(solution)/shard_map/ppermute | solution.py:188
  7.6 5.3 %collective-permute-start.1 = (bf16[16,2176]{1,0:T(8,128)(2,1)S(1)}, bf16[16,2176]{1,0:T(8,128)(2,1)S(1)}, u32[]{:S(2)}, u32[]{:S(2)}) collective-permute-start(bf16[16,2176]{1,0:T(8,128)(2,1)S(1)} %shard_map.65.refs_0_), channel_id=1, source_target_pairs={{0,16},{2,18},{4,20},{6,22},{8,24},{10,26},{12,28},{14,30},{16,0},... | collective-permute-start | bytes 208904 | tf_op jit(solution)/shard_map/ppermute | solution.py:188
  7.6 6.0 %collective-permute-start.3 = (bf16[16,2176]{1,0:T(8,128)(2,1)S(1)}, bf16[16,2176]{1,0:T(8,128)(2,1)S(1)}, u32[]{:S(2)}, u32[]{:S(2)}) collective-permute-start(bf16[16,2176]{1,0:T(8,128)(2,1)S(1)} %shard_map.65.refs_0_), channel_id=1, source_target_pairs={{0,2},{2,0},{4,6},{6,4},{1,3},{3,1},{5,7},{7,5},{8,10},{10,8},{12,... | collective-permute-start | bytes 208904 | tf_op jit(solution)/shard_map/ppermute | solution.py:191
  7.6 6.0 %collective-permute-start = (bf16[16,2176]{1,0:T(8,128)(2,1)S(1)}, bf16[16,2176]{1,0:T(8,128)(2,1)S(1)}, u32[]{:S(2)}, u32[]{:S(2)}) collective-permute-start(bf16[16,2176]{1,0:T(8,128)(2,1)S(1)} %shard_map.65.refs_0_), channel_id=1, source_target_pairs={{0,8},{2,10},{4,12},{6,14},{8,0},{10,2},{12,4},{14,6},{16,24},{18,... | collective-permute-start | bytes 208904 | tf_op jit(solution)/shard_map/ppermute | solution.py:188
  8.6 6.5 %collective-permute-start.10 = (bf16[16,2176]{1,0:T(8,128)(2,1)S(1)}, bf16[16,2176]{1,0:T(8,128)(2,1)S(1)}, u32[]{:S(2)}, u32[]{:S(2)}) collective-permute-start(bf16[16,2176]{1,0:T(8,128)(2,1)S(1)} %collective-permute-done.2.refs_3_), channel_id=1, source_target_pairs={{0,4},{2,6},{4,0},{6,2},{8,12},{10,14},{12,8},{14,10},{16,20},{18,... | collective-permute-start | bytes 208904 | tf_op jit(solution)/shard_map/ppermute | solution.py:188
  10.5 4.7 %collective-permute-start.6 = (bf16[16,2176]{1,0:T(8,128)(2,1)S(1)}, bf16[16,2176]{1,0:T(8,128)(2,1)S(1)}, u32[]{:S(2)}, u32[]{:S(2)}) collective-permute-start(bf16[16,2176]{1,0:T(8,128)(2,1)S(1)} %collective-permute-done.2.refs_3_), channel_id=1, source_target_pairs={{0,2},{2,0},{4,6},{6,4},{1,3},{3,1},{5,7},{7,5},{8,10},{10,8},{12,... | collective-permute-start | bytes 208904 | tf_op jit(solution)/shard_map/ppermute | solution.py:191
  12.9 4.8 %collective-permute-start.9 = (bf16[16,2176]{1,0:T(8,128)(2,1)S(1)}, bf16[16,2176]{1,0:T(8,128)(2,1)S(1)}, u32[]{:S(2)}, u32[]{:S(2)}) collective-permute-start(bf16[16,2176]{1,0:T(8,128)(2,1)S(1)} %collective-permute-done.1.refs_2_), channel_id=1, source_target_pairs={{0,4},{2,6},{4,0},{6,2},{8,12},{10,14},{12,8},{14,10},{16,20},{18,... | collective-permute-start | bytes 208904 | tf_op jit(solution)/shard_map/ppermute | solution.py:188
  13.6 4.1 %collective-permute-start.5 = (bf16[16,2176]{1,0:T(8,128)(2,1)S(1)}, bf16[16,2176]{1,0:T(8,128)(2,1)S(1)}, u32[]{:S(2)}, u32[]{:S(2)}) collective-permute-start(bf16[16,2176]{1,0:T(8,128)(2,1)S(1)} %collective-permute-done.1.refs_2_), channel_id=1, source_target_pairs={{0,2},{2,0},{4,6},{6,4},{1,3},{3,1},{5,7},{7,5},{8,10},{10,8},{12,... | collective-permute-start | bytes 208904 | tf_op jit(solution)/shard_map/ppermute | solution.py:191
  13.6 5.1 %collective-permute-start.8 = (bf16[16,2176]{1,0:T(8,128)(2,1)S(1)}, bf16[16,2176]{1,0:T(8,128)(2,1)S(1)}, u32[]{:S(2)}, u32[]{:S(2)}) collective-permute-start(bf16[16,2176]{1,0:T(8,128)(2,1)S(1)} %collective-permute-done.refs_1_), channel_id=1, source_target_pairs={{0,4},{2,6},{4,0},{6,2},{8,12},{10,14},{12,8},{14,10},{16,20},{18,... | collective-permute-start | bytes 208904 | tf_op jit(solution)/shard_map/ppermute | solution.py:188
  15.0 3.7 %collective-permute-start.4 = (bf16[16,2176]{1,0:T(8,128)(2,1)S(1)}, bf16[16,2176]{1,0:T(8,128)(2,1)S(1)}, u32[]{:S(2)}, u32[]{:S(2)}) collective-permute-start(bf16[16,2176]{1,0:T(8,128)(2,1)S(1)} %collective-permute-done.refs_1_), channel_id=1, source_target_pairs={{0,2},{2,0},{4,6},{6,4},{1,3},{3,1},{5,7},{7,5},{8,10},{10,8},{12,... | collective-permute-start | bytes 208904 | tf_op jit(solution)/shard_map/ppermute | solution.py:191
  18.8 1.6 %collective-permute-start.12 = (bf16[64,2176]{1,0:T(8,128)(2,1)S(1)}, bf16[64,2176]{1,0:T(8,128)(2,1)S(1)}, u32[]{:S(2)}, u32[]{:S(2)}) collective-permute-start(bf16[64,2176]{1,0:T(8,128)(2,1)S(1)} %shard_map.66.refs_11_.refs_0_), channel_id=1, source_target_pairs={{0,2},{2,0},{4,6},{6,4},{1,3},{3,1},{5,7},{7,5},{8,10},{10,8},{12,... | collective-permute-start | bytes 835592 | tf_op jit(solution)/shard_map/ppermute | solution.py:191
  21.9 1.4 %collective-permute-start.13 = (bf16[16,2048]{1,0:T(8,128)(2,1)S(1)}, bf16[16,2048]{1,0:T(8,128)(2,1)S(1)}, u32[]{:S(2)}, u32[]{:S(2)}) collective-permute-start(bf16[16,2048]{1,0:T(8,128)(2,1)S(1)} %get-tuple-element.13), channel_id=1, source_target_pairs={{0,2},{2,0},{4,6},{6,4},{1,3},{3,1},{5,7},{7,5},{8,10},{10,8},{12,... | collective-permute-start | bytes 196616 | tf_op jit(solution)/shard_map/ppermute | solution.py:191
  23.4 1.6 %collective-permute-start.16 = (bf16[64,2048]{1,0:T(8,128)(2,1)S(1)}, bf16[64,2048]{1,0:T(8,128)(2,1)S(1)}, u32[]{:S(2)}, u32[]{:S(2)}) collective-permute-start(bf16[64,2048]{1,0:T(8,128)(2,1)S(1)} %shard_map.71), channel_id=1, source_target_pairs={{0,2},{2,0},{4,6},{6,4},{1,3},{3,1},{5,7},{7,5},{8,10},{10,8},{12,... | collective-permute-start | bytes 786440 | tf_op jit(solution)/shard_map/ppermute | solution.py:191
  23.8 3.4 %collective-permute-start.11 = (bf16[64,2048]{1,0:T(8,128)(2,1)S(1)}, bf16[64,2048]{1,0:T(8,128)(2,1)S(1)}, u32[]{:S(2)}, u32[]{:S(2)}) collective-permute-start(bf16[64,2048]{1,0:T(8,128)(2,1)S(1)} %get-tuple-element.11), channel_id=1, source_target_pairs={{0,2},{2,0},{4,6},{6,4},{1,3},{3,1},{5,7},{7,5},{8,10},{10,8},{12,... | collective-permute-start | bytes 786440 | tf_op jit(solution)/shard_map/ppermute | solution.py:191
  24.0 4.8 %collective-permute-start.14 = (bf16[16,2048]{1,0:T(8,128)(2,1)S(1)}, bf16[16,2048]{1,0:T(8,128)(2,1)S(1)}, u32[]{:S(2)}, u32[]{:S(2)}) collective-permute-start(bf16[16,2048]{1,0:T(8,128)(2,1)S(1)} %shard_map.69), channel_id=1, source_target_pairs={{4,0},{6,2},{0,4},{2,6},{12,8},{14,10},{8,12},{10,14},{20,16},{22,... | collective-permute-start | bytes 196616 | tf_op jit(solution)/shard_map/ppermute | solution.py:188
  25.0 7.4 %collective-permute-start.17 = (bf16[16,2048]{1,0:T(8,128)(2,1)S(1)}, bf16[16,2048]{1,0:T(8,128)(2,1)S(1)}, u32[]{:S(2)}, u32[]{:S(2)}) collective-permute-start(bf16[16,2048]{1,0:T(8,128)(2,1)S(1)} %shard_map.72), channel_id=1, source_target_pairs={{4,0},{6,2},{0,4},{2,6},{12,8},{14,10},{8,12},{10,14},{20,16},{22,... | collective-permute-start | bytes 196616 | tf_op jit(solution)/shard_map/ppermute | solution.py:188
  26.2 6.3 %collective-permute-start.19 = (bf16[16,2048]{1,0:T(8,128)(2,1)S(1)}, bf16[16,2048]{1,0:T(8,128)(2,1)S(1)}, u32[]{:S(2)}, u32[]{:S(2)}) collective-permute-start(bf16[16,2048]{1,0:T(8,128)(2,1)S(1)} %shard_map.74), channel_id=1, source_target_pairs={{4,0},{6,2},{0,4},{2,6},{12,8},{14,10},{8,12},{10,14},{20,16},{22,... | collective-permute-start | bytes 196616 | tf_op jit(solution)/shard_map/ppermute | solution.py:188
  28.8 6.3 %collective-permute-start.15 = (bf16[16,2048]{1,0:T(8,128)(2,1)S(1)}, bf16[16,2048]{1,0:T(8,128)(2,1)S(1)}, u32[]{:S(2)}, u32[]{:S(2)}) collective-permute-start(bf16[16,2048]{1,0:T(8,128)(2,1)S(1)} %shard_map.70), channel_id=1, source_target_pairs={{24,0},{26,2},{28,4},{30,6},{16,8},{18,10},{20,12},{22,14},{8,16},... | collective-permute-start | bytes 196616 | tf_op jit(solution)/shard_map/ppermute | solution.py:188
  31.1 4.3 %collective-permute-start.21 = (bf16[16,2048]{1,0:T(8,128)(2,1)S(1)}, bf16[16,2048]{1,0:T(8,128)(2,1)S(1)}, u32[]{:S(2)}, u32[]{:S(2)}) collective-permute-start(bf16[16,2048]{1,0:T(8,128)(2,1)S(1)} %shard_map.76), channel_id=1, source_target_pairs={{4,0},{6,2},{0,4},{2,6},{12,8},{14,10},{8,12},{10,14},{20,16},{22,... | collective-permute-start | bytes 196616 | tf_op jit(solution)/shard_map/ppermute | solution.py:188
  32.4 5.4 %collective-permute-start.18 = (bf16[16,2048]{1,0:T(8,128)(2,1)S(1)}, bf16[16,2048]{1,0:T(8,128)(2,1)S(1)}, u32[]{:S(2)}, u32[]{:S(2)}) collective-permute-start(bf16[16,2048]{1,0:T(8,128)(2,1)S(1)} %shard_map.73), channel_id=1, source_target_pairs={{16,0},{18,2},{20,4},{22,6},{24,8},{26,10},{28,12},{30,14},{0,16},... | collective-permute-start | bytes 196616 | tf_op jit(solution)/shard_map/ppermute | solution.py:188
  32.5 5.3 %collective-permute-start.20 = (bf16[16,2048]{1,0:T(8,128)(2,1)S(1)}, bf16[16,2048]{1,0:T(8,128)(2,1)S(1)}, u32[]{:S(2)}, u32[]{:S(2)}) collective-permute-start(bf16[16,2048]{1,0:T(8,128)(2,1)S(1)} %shard_map.75), channel_id=1, source_target_pairs={{8,0},{10,2},{12,4},{14,6},{0,8},{2,10},{4,12},{6,14},{24,16},{26,... | collective-permute-start | bytes 196616 | tf_op jit(solution)/shard_map/ppermute | solution.py:188
  (4 other events, 20.5 us)

commit v3 on v0

--- a/solution.py
+++ b/solution.py
@@ -189,11 +189,13 @@
     own = prepare(place, tokens, expert_ids, gate_weights)
     weights = (w_gate, w_up, w_down)
     width = groups if experts * tok_rows <= WHOLE_ROWS else 1
+    order = [*range(groups)]
+    order[-2:] = order[:-3:-1]
     total = None
     for first in range(0, groups, width):
         if first:
             own, total = lax.optimization_barrier((own, total))
-        steps = range(first, first + width)
+        steps = order[first : first + width]
         near = [step_to(own, g, 0) if g else own for g in steps]
         far = [step_to(piece, 0, s) for piece in near for s in range(1, chips)]
         near_other = [swap(piece) for piece in near]

time: 37.5 us -> 38.5 us (1.027)
  waiting for transfers between devices: 11.2 us -> 11.8 us
    ppermute x14, waiting for transfers between devices: 10.1 us -> 10.7 us  [step_to(): lax.ppermute(value, ('grp', 'exp'), [(d, o) for o, d in pairs] if back el...]
where the time goes in v3:
time: 38.5 us; the launch traced here: 38.4 us
  starting transfers between devices  21.4 us (56%)
  waiting for transfers between devices  11.8 us (31%)
  Pallas kernels  3.37 us (9%)
  local copies, waits for them, and re-layouts  0.85 us (2%)
  other arithmetic  0.7 us (2%)
    ppermute x14, starting transfers between devices, step_to(): lax.ppermute(value, ('grp', 'exp'), [(d, o) for o, d in pairs] if back el...  20.6 us
    ppermute x14, waiting for transfers between devices, step_to(): lax.ppermute(value, ('grp', 'exp'), [(d, o) for o, d in pairs] if back el...  10.7 us
    pallas_call x2, Pallas kernels, expert_rows(): pl.pallas_call(functools.partial(expert_kernel, count), out_shape=[jax.Sh...  3.02 us
    ppermute x7, waiting for transfers between devices, swap(): return lax.ppermute(value, 'exp', [(i, i ^ 1) for i in range(owners)])  1.1 us
    unnamed x12, local copies, waits for them, and re-layouts  0.85 us
    ppermute x7, starting transfers between devices, swap(): return lax.ppermute(value, 'exp', [(i, i ^ 1) for i in range(owners)])  0.85 us
  transfers between devices with their start and end apart: 21, of which 8 were waited for; matrix products, arithmetic and copies ran while one was open for 0% of the time, Pallas kernels for 4%

profile of v3, /device:TPU:0, one launch (start us, length us, event | category | flops | bytes accessed | tf_op | source)
XLA Modules:
  0.0 38.4 jit_solution(16097925023858145180)
XLA Ops:
  0.0 0.8 %copy-done.3 = bf16[16,2048]{1,0:T(8,128)(2,1)S(1)} copy-done((bf16[16,2048]{1,0:T(8,128)(2,1)S(1)}, bf16[16,2048]{1,0:T(8,128)(2,1)}, u32[]{:S(2)}) %copy-start.3) | copy-done | bytes 65560
  1.0 4.0 %collective-permute-start.2 = (bf16[16,2176]{1,0:T(8,128)(2,1)S(1)}, bf16[16,2176]{1,0:T(8,128)(2,1)S(1)}, u32[]{:S(2)}, u32[]{:S(2)}) collective-permute-start(bf16[16,2176]{1,0:T(8,128)(2,1)S(1)} %shard_map.65.refs_0_), channel_id=1, source_target_pairs={{0,16},{2,18},{4,20},{6,22},{8,24},{10,26},{12,28},{14,30},{16,0},... | collective-permute-start | bytes 208904 | tf_op jit(solution)/shard_map/ppermute | solution.py:183
  5.1 1.5 %collective-permute-start.7 = (bf16[16,2176]{1,0:T(8,128)(2,1)S(1)}, bf16[16,2176]{1,0:T(8,128)(2,1)S(1)}, u32[]{:S(2)}, u32[]{:S(2)}) collective-permute-start(bf16[16,2176]{1,0:T(8,128)(2,1)S(1)} %shard_map.65.refs_0_), channel_id=1, source_target_pairs={{0,4},{2,6},{4,0},{6,2},{8,12},{10,14},{12,8},{14,10},{16,20},{18,... | collective-permute-start | bytes 208904 | tf_op jit(solution)/shard_map/ppermute | solution.py:183
  6.6 1.3 %collective-permute-start.1 = (bf16[16,2176]{1,0:T(8,128)(2,1)S(1)}, bf16[16,2176]{1,0:T(8,128)(2,1)S(1)}, u32[]{:S(2)}, u32[]{:S(2)}) collective-permute-start(bf16[16,2176]{1,0:T(8,128)(2,1)S(1)} %shard_map.65.refs_0_), channel_id=1, source_target_pairs={{0,24},{2,26},{4,28},{6,30},{8,16},{10,18},{12,20},{14,22},{16,8},... | collective-permute-start | bytes 208904 | tf_op jit(solution)/shard_map/ppermute | solution.py:183
  8.2 0.7 %collective-permute-done.2.refs_3_ = bf16[16,2176]{1,0:T(8,128)(2,1)S(1)} collective-permute-done((bf16[16,2176]{1,0:T(8,128)(2,1)S(1)}, bf16[16,2176]{1,0:T(8,128)(2,1)S(1)}, u32[]{:S(2)}, u32[]{:S(2)}) %collective-permute-start.2) | collective-permute-done | bytes 69664 | tf_op jit(solution)/shard_map/ppermute | solution.py:183
  8.9 2.8 %collective-permute-start.10 = (bf16[16,2176]{1,0:T(8,128)(2,1)S(1)}, bf16[16,2176]{1,0:T(8,128)(2,1)S(1)}, u32[]{:S(2)}, u32[]{:S(2)}) collective-permute-start(bf16[16,2176]{1,0:T(8,128)(2,1)S(1)} %collective-permute-done.2.refs_3_), channel_id=1, source_target_pairs={{0,4},{2,6},{4,0},{6,2},{8,12},{10,14},{12,8},{14,10},{16,20},{18,... | collective-permute-start | bytes 208904 | tf_op jit(solution)/shard_map/ppermute | solution.py:183
  11.6 1.6 %collective-permute-done.1.refs_2_ = bf16[16,2176]{1,0:T(8,128)(2,1)S(1)} collective-permute-done((bf16[16,2176]{1,0:T(8,128)(2,1)S(1)}, bf16[16,2176]{1,0:T(8,128)(2,1)S(1)}, u32[]{:S(2)}, u32[]{:S(2)}) %collective-permute-start.1) | collective-permute-done | bytes 69664 | tf_op jit(solution)/shard_map/ppermute | solution.py:183
  13.8 1.6 %collective-permute-start.8 = (bf16[16,2176]{1,0:T(8,128)(2,1)S(1)}, bf16[16,2176]{1,0:T(8,128)(2,1)S(1)}, u32[]{:S(2)}, u32[]{:S(2)}) collective-permute-start(bf16[16,2176]{1,0:T(8,128)(2,1)S(1)} %collective-permute-done.refs_1_), channel_id=1, source_target_pairs={{0,4},{2,6},{4,0},{6,2},{8,12},{10,14},{12,8},{14,10},{16,20},{18,... | collective-permute-start | bytes 208904 | tf_op jit(solution)/shard_map/ppermute | solution.py:183
  15.5 2.7 %collective-permute-done.9.refs_2_ = bf16[16,2176]{1,0:T(8,128)(2,1)S(1)} collective-permute-done((bf16[16,2176]{1,0:T(8,128)(2,1)S(1)}, bf16[16,2176]{1,0:T(8,128)(2,1)S(1)}, u32[]{:S(2)}, u32[]{:S(2)}) %collective-permute-start.9) | collective-permute-done | bytes 69664 | tf_op jit(solution)/shard_map/ppermute | solution.py:183
  18.2 0.8 %collective-permute-done.8.refs_1_ = bf16[16,2176]{1,0:T(8,128)(2,1)S(1)} collective-permute-done((bf16[16,2176]{1,0:T(8,128)(2,1)S(1)}, bf16[16,2176]{1,0:T(8,128)(2,1)S(1)}, u32[]{:S(2)}, u32[]{:S(2)}) %collective-permute-start.8) | collective-permute-done | bytes 69664 | tf_op jit(solution)/shard_map/ppermute | solution.py:183
  19.2 1.5 %shard_map.67 = (f32[64,2048]{1,0:T(8,128)S(1)}, bf16[64,2048]{1,0:T(8,128)(2,1)S(1)}) custom-call(s32[8,128]{1,0:T(8,128)S(1)} %shard_map.64.place_ref, bf16[16,2176]{1,0:T(8,128)(2,1)S(1)} %shard_map.65.refs_0_, bf16[16,2176]{1,0:T(8,128)(2,1)S(1)} %collective-permute-done.refs_1_, bf16[16,2176]{1,0:T(8,128)(2,1)S(1)} %collective-permute-done.1.refs_2_, ...), custom_call_target="tpu_custom_call" | custom-call | flops 1207959552 | tf_op jit(solution)/shard_map/pallas_call | solution.py:111
  20.7 1.5 %shard_map.68 = (f32[64,2048]{1,0:T(8,128)S(1)}, bf16[64,2048]{1,0:T(8,128)(2,1)S(1)}) custom-call(s32[8,128]{1,0:T(8,128)S(1)} %shard_map.64.place_ref, bf16[64,2176]{1,0:T(8,128)(2,1)S(1)} %shard_map.66.refs_11_.refs_0_, bf16[64,2176]{1,0:T(8,128)(2,1)S(1)} %collective-permute-done.12.refs_1_, bf16[1,2048,768]{2,1,0:T(8,128)(2,1)S(1)} %copy-done, ...), custom_call_target="tpu_custom_call" | custom-call | flops 1207959552 | tf_op jit(solution)/shard_map/pallas_call | solution.py:111
  22.2 0.5 %collective-permute-start.13 = (bf16[64,2048]{1,0:T(8,128)(2,1)S(1)}, bf16[64,2048]{1,0:T(8,128)(2,1)S(1)}, u32[]{:S(2)}, u32[]{:S(2)}) collective-permute-start(bf16[64,2048]{1,0:T(8,128)(2,1)S(1)} %get-tuple-element.12), channel_id=1, source_target_pairs={{0,2},{2,0},{4,6},{6,4},{1,3},{3,1},{5,7},{7,5},{8,10},{10,8},{12,... | collective-permute-start | bytes 786440 | tf_op jit(solution)/shard_map/ppermute | solution.py:186
  22.8 1.1 %collective-permute-done.13.refs_1_ = bf16[64,2048]{1,0:T(8,128)(2,1)S(1)} collective-permute-done((bf16[64,2048]{1,0:T(8,128)(2,1)S(1)}, bf16[64,2048]{1,0:T(8,128)(2,1)S(1)}, u32[]{:S(2)}, u32[]{:S(2)}) %collective-permute-start.13) | collective-permute-done | bytes 262176 | tf_op jit(solution)/shard_map/ppermute | solution.py:186
  23.9 0.9 %collective-permute-start.14 = (bf16[16,2048]{1,0:T(8,128)(2,1)S(1)}, bf16[16,2048]{1,0:T(8,128)(2,1)S(1)}, u32[]{:S(2)}, u32[]{:S(2)}) collective-permute-start(bf16[16,2048]{1,0:T(8,128)(2,1)S(1)} %shard_map.69), channel_id=1, source_target_pairs={{4,0},{6,2},{0,4},{2,6},{12,8},{14,10},{8,12},{10,14},{20,16},{22,... | collective-permute-start | bytes 196616 | tf_op jit(solution)/shard_map/ppermute | solution.py:183
  24.9 1.3 %collective-permute-start.16 = (bf16[16,2048]{1,0:T(8,128)(2,1)S(1)}, bf16[16,2048]{1,0:T(8,128)(2,1)S(1)}, u32[]{:S(2)}, u32[]{:S(2)}) collective-permute-start(bf16[16,2048]{1,0:T(8,128)(2,1)S(1)} %shard_map.71), channel_id=1, source_target_pairs={{4,0},{6,2},{0,4},{2,6},{12,8},{14,10},{8,12},{10,14},{20,16},{22,... | collective-permute-start | bytes 196616 | tf_op jit(solution)/shard_map/ppermute | solution.py:183
  26.2 0.9 %collective-permute-start.18 = (bf16[16,2048]{1,0:T(8,128)(2,1)S(1)}, bf16[16,2048]{1,0:T(8,128)(2,1)S(1)}, u32[]{:S(2)}, u32[]{:S(2)}) collective-permute-start(bf16[16,2048]{1,0:T(8,128)(2,1)S(1)} %shard_map.73), channel_id=1, source_target_pairs={{4,0},{6,2},{0,4},{2,6},{12,8},{14,10},{8,12},{10,14},{20,16},{22,... | collective-permute-start | bytes 196616 | tf_op jit(solution)/shard_map/ppermute | solution.py:183
  27.1 1.3 %collective-permute-start.20 = (bf16[16,2048]{1,0:T(8,128)(2,1)S(1)}, bf16[16,2048]{1,0:T(8,128)(2,1)S(1)}, u32[]{:S(2)}, u32[]{:S(2)}) collective-permute-start(bf16[16,2048]{1,0:T(8,128)(2,1)S(1)} %shard_map.75), channel_id=1, source_target_pairs={{4,0},{6,2},{0,4},{2,6},{12,8},{14,10},{8,12},{10,14},{20,16},{22,... | collective-permute-start | bytes 196616 | tf_op jit(solution)/shard_map/ppermute | solution.py:183
  28.3 0.6 %collective-permute-done.14.refs_2_ = bf16[16,2048]{1,0:T(8,128)(2,1)S(1)} collective-permute-done((bf16[16,2048]{1,0:T(8,128)(2,1)S(1)}, bf16[16,2048]{1,0:T(8,128)(2,1)S(1)}, u32[]{:S(2)}, u32[]{:S(2)}) %collective-permute-start.14) | collective-permute-done | bytes 65568 | tf_op jit(solution)/shard_map/ppermute | solution.py:183
  29.0 1.4 %collective-permute-start.15 = (bf16[16,2048]{1,0:T(8,128)(2,1)S(1)}, bf16[16,2048]{1,0:T(8,128)(2,1)S(1)}, u32[]{:S(2)}, u32[]{:S(2)}) collective-permute-start(bf16[16,2048]{1,0:T(8,128)(2,1)S(1)} %shard_map.70), channel_id=1, source_target_pairs={{16,0},{18,2},{20,4},{22,6},{24,8},{26,10},{28,12},{30,14},{0,16},... | collective-permute-start | bytes 196616 | tf_op jit(solution)/shard_map/ppermute | solution.py:183
  30.4 2.8 %collective-permute-start.17 = (bf16[16,2048]{1,0:T(8,128)(2,1)S(1)}, bf16[16,2048]{1,0:T(8,128)(2,1)S(1)}, u32[]{:S(2)}, u32[]{:S(2)}) collective-permute-start(bf16[16,2048]{1,0:T(8,128)(2,1)S(1)} %shard_map.72), channel_id=1, source_target_pairs={{24,0},{26,2},{28,4},{30,6},{16,8},{18,10},{20,12},{22,14},{8,16},... | collective-permute-start | bytes 196616 | tf_op jit(solution)/shard_map/ppermute | solution.py:183
  33.3 3.5 %collective-permute-done.15 = bf16[16,2048]{1,0:T(8,128)(2,1)S(1)} collective-permute-done((bf16[16,2048]{1,0:T(8,128)(2,1)S(1)}, bf16[16,2048]{1,0:T(8,128)(2,1)S(1)}, u32[]{:S(2)}, u32[]{:S(2)}) %collective-permute-start.15) | collective-permute-done | bytes 65568 | tf_op jit(solution)/shard_map/ppermute | solution.py:183
  36.8 0.9 %collective-permute-done.19 = bf16[16,2048]{1,0:T(8,128)(2,1)S(1)} collective-permute-done((bf16[16,2048]{1,0:T(8,128)(2,1)S(1)}, bf16[16,2048]{1,0:T(8,128)(2,1)S(1)}, u32[]{:S(2)}, u32[]{:S(2)}) %collective-permute-start.19) | collective-permute-done | bytes 65568 | tf_op jit(solution)/shard_map/ppermute | solution.py:183
  37.6 0.7 %convert_add_fusion = f32[16,2048]{1,0:T(8,128)} fusion(bf16[16,2048]{1,0:T(8,128)(2,1)S(1)} %collective-permute-done.20, bf16[16,2048]{1,0:T(8,128)(2,1)S(1)} %collective-permute-done.19, bf16[16,2048]{1,0:T(8,128)(2,1)S(1)} %collective-permute-done.17, bf16[16,2048]{1,0:T(8,128)(2,1)S(1)} %collective-permute-done.15, ...), kind=kLoop, calls=%fused_computation | loop fusion | flops 327680 | bytes 589824 | tf_op jit(solution)/shard_map/add | solution.py:228
  (43 shorter events, 1.5 us)
Async XLA Ops:
  0.8 18.3 %copy-start = (bf16[1,2048,768]{2,1,0:T(8,128)(2,1)S(1)}, bf16[1,2048,768]{2,1,0:T(8,128)(2,1)}, u32[]{:S(2)}) copy-start(bf16[1,2048,768]{2,1,0:T(8,128)(2,1)} %refs_2_.1) | copy-start | bytes 9437188
  0.8 18.3 %copy-start.1 = (bf16[1,2048,768]{2,1,0:T(8,128)(2,1)S(1)}, bf16[1,2048,768]{2,1,0:T(8,128)(2,1)}, u32[]{:S(2)}) copy-start(bf16[1,2048,768]{2,1,0:T(8,128)(2,1)} %refs_3_.1) | copy-start | bytes 9437188
  0.9 18.3 %copy-start.2 = (bf16[1,768,2048]{2,1,0:T(8,128)(2,1)S(1)}, bf16[1,768,2048]{2,1,0:T(8,128)(2,1)}, u32[]{:S(2)}) copy-start(bf16[1,768,2048]{2,1,0:T(8,128)(2,1)} %refs_4_.1) | copy-start | bytes 9437188
  1.0 7.8 %collective-permute-start.2 = (bf16[16,2176]{1,0:T(8,128)(2,1)S(1)}, bf16[16,2176]{1,0:T(8,128)(2,1)S(1)}, u32[]{:S(2)}, u32[]{:S(2)}) collective-permute-start(bf16[16,2176]{1,0:T(8,128)(2,1)S(1)} %shard_map.65.refs_0_), channel_id=1, source_target_pairs={{0,16},{2,18},{4,20},{6,22},{8,24},{10,26},{12,28},{14,30},{16,0},... | collective-permute-start | bytes 208904 | tf_op jit(solution)/shard_map/ppermute | solution.py:183
  5.1 6.6 %collective-permute-start.7 = (bf16[16,2176]{1,0:T(8,128)(2,1)S(1)}, bf16[16,2176]{1,0:T(8,128)(2,1)S(1)}, u32[]{:S(2)}, u32[]{:S(2)}) collective-permute-start(bf16[16,2176]{1,0:T(8,128)(2,1)S(1)} %shard_map.65.refs_0_), channel_id=1, source_target_pairs={{0,4},{2,6},{4,0},{6,2},{8,12},{10,14},{12,8},{14,10},{16,20},{18,... | collective-permute-start | bytes 208904 | tf_op jit(solution)/shard_map/ppermute | solution.py:183
  6.6 6.6 %collective-permute-start.1 = (bf16[16,2176]{1,0:T(8,128)(2,1)S(1)}, bf16[16,2176]{1,0:T(8,128)(2,1)S(1)}, u32[]{:S(2)}, u32[]{:S(2)}) collective-permute-start(bf16[16,2176]{1,0:T(8,128)(2,1)S(1)} %shard_map.65.refs_0_), channel_id=1, source_target_pairs={{0,24},{2,26},{4,28},{6,30},{8,16},{10,18},{12,20},{14,22},{16,8},... | collective-permute-start | bytes 208904 | tf_op jit(solution)/shard_map/ppermute | solution.py:183
  8.0 5.8 %collective-permute-start.3 = (bf16[16,2176]{1,0:T(8,128)(2,1)S(1)}, bf16[16,2176]{1,0:T(8,128)(2,1)S(1)}, u32[]{:S(2)}, u32[]{:S(2)}) collective-permute-start(bf16[16,2176]{1,0:T(8,128)(2,1)S(1)} %shard_map.65.refs_0_), channel_id=1, source_target_pairs={{0,2},{2,0},{4,6},{6,4},{1,3},{3,1},{5,7},{7,5},{8,10},{10,8},{12,... | collective-permute-start | bytes 208904 | tf_op jit(solution)/shard_map/ppermute | solution.py:186
  8.0 5.8 %collective-permute-start = (bf16[16,2176]{1,0:T(8,128)(2,1)S(1)}, bf16[16,2176]{1,0:T(8,128)(2,1)S(1)}, u32[]{:S(2)}, u32[]{:S(2)}) collective-permute-start(bf16[16,2176]{1,0:T(8,128)(2,1)S(1)} %shard_map.65.refs_0_), channel_id=1, source_target_pairs={{0,8},{2,10},{4,12},{6,14},{8,0},{10,2},{12,4},{14,6},{16,24},{18,... | collective-permute-start | bytes 208904 | tf_op jit(solution)/shard_map/ppermute | solution.py:183
  8.9 6.5 %collective-permute-start.10 = (bf16[16,2176]{1,0:T(8,128)(2,1)S(1)}, bf16[16,2176]{1,0:T(8,128)(2,1)S(1)}, u32[]{:S(2)}, u32[]{:S(2)}) collective-permute-start(bf16[16,2176]{1,0:T(8,128)(2,1)S(1)} %collective-permute-done.2.refs_3_), channel_id=1, source_target_pairs={{0,4},{2,6},{4,0},{6,2},{8,12},{10,14},{12,8},{14,10},{16,20},{18,... | collective-permute-start | bytes 208904 | tf_op jit(solution)/shard_map/ppermute | solution.py:183
  11.6 3.9 %collective-permute-start.6 = (bf16[16,2176]{1,0:T(8,128)(2,1)S(1)}, bf16[16,2176]{1,0:T(8,128)(2,1)S(1)}, u32[]{:S(2)}, u32[]{:S(2)}) collective-permute-start(bf16[16,2176]{1,0:T(8,128)(2,1)S(1)} %collective-permute-done.2.refs_3_), channel_id=1, source_target_pairs={{0,2},{2,0},{4,6},{6,4},{1,3},{3,1},{5,7},{7,5},{8,10},{10,8},{12,... | collective-permute-start | bytes 208904 | tf_op jit(solution)/shard_map/ppermute | solution.py:186
  13.2 5.0 %collective-permute-start.9 = (bf16[16,2176]{1,0:T(8,128)(2,1)S(1)}, bf16[16,2176]{1,0:T(8,128)(2,1)S(1)}, u32[]{:S(2)}, u32[]{:S(2)}) collective-permute-start(bf16[16,2176]{1,0:T(8,128)(2,1)S(1)} %collective-permute-done.1.refs_2_), channel_id=1, source_target_pairs={{0,4},{2,6},{4,0},{6,2},{8,12},{10,14},{12,8},{14,10},{16,20},{18,... | collective-permute-start | bytes 208904 | tf_op jit(solution)/shard_map/ppermute | solution.py:183
  13.8 4.5 %collective-permute-start.5 = (bf16[16,2176]{1,0:T(8,128)(2,1)S(1)}, bf16[16,2176]{1,0:T(8,128)(2,1)S(1)}, u32[]{:S(2)}, u32[]{:S(2)}) collective-permute-start(bf16[16,2176]{1,0:T(8,128)(2,1)S(1)} %collective-permute-done.1.refs_2_), channel_id=1, source_target_pairs={{0,2},{2,0},{4,6},{6,4},{1,3},{3,1},{5,7},{7,5},{8,10},{10,8},{12,... | collective-permute-start | bytes 208904 | tf_op jit(solution)/shard_map/ppermute | solution.py:186
  13.8 5.3 %collective-permute-start.8 = (bf16[16,2176]{1,0:T(8,128)(2,1)S(1)}, bf16[16,2176]{1,0:T(8,128)(2,1)S(1)}, u32[]{:S(2)}, u32[]{:S(2)}) collective-permute-start(bf16[16,2176]{1,0:T(8,128)(2,1)S(1)} %collective-permute-done.refs_1_), channel_id=1, source_target_pairs={{0,4},{2,6},{4,0},{6,2},{8,12},{10,14},{12,8},{14,10},{16,20},{18,... | collective-permute-start | bytes 208904 | tf_op jit(solution)/shard_map/ppermute | solution.py:183
  15.4 3.7 %collective-permute-start.4 = (bf16[16,2176]{1,0:T(8,128)(2,1)S(1)}, bf16[16,2176]{1,0:T(8,128)(2,1)S(1)}, u32[]{:S(2)}, u32[]{:S(2)}) collective-permute-start(bf16[16,2176]{1,0:T(8,128)(2,1)S(1)} %collective-permute-done.refs_1_), channel_id=1, source_target_pairs={{0,2},{2,0},{4,6},{6,4},{1,3},{3,1},{5,7},{7,5},{8,10},{10,8},{12,... | collective-permute-start | bytes 208904 | tf_op jit(solution)/shard_map/ppermute | solution.py:186
  19.1 1.6 %collective-permute-start.12 = (bf16[64,2176]{1,0:T(8,128)(2,1)S(1)}, bf16[64,2176]{1,0:T(8,128)(2,1)S(1)}, u32[]{:S(2)}, u32[]{:S(2)}) collective-permute-start(bf16[64,2176]{1,0:T(8,128)(2,1)S(1)} %shard_map.66.refs_11_.refs_0_), channel_id=1, source_target_pairs={{0,2},{2,0},{4,6},{6,4},{1,3},{3,1},{5,7},{7,5},{8,10},{10,8},{12,... | collective-permute-start | bytes 835592 | tf_op jit(solution)/shard_map/ppermute | solution.py:186
  22.2 1.7 %collective-permute-start.13 = (bf16[64,2048]{1,0:T(8,128)(2,1)S(1)}, bf16[64,2048]{1,0:T(8,128)(2,1)S(1)}, u32[]{:S(2)}, u32[]{:S(2)}) collective-permute-start(bf16[64,2048]{1,0:T(8,128)(2,1)S(1)} %get-tuple-element.12), channel_id=1, source_target_pairs={{0,2},{2,0},{4,6},{6,4},{1,3},{3,1},{5,7},{7,5},{8,10},{10,8},{12,... | collective-permute-start | bytes 786440 | tf_op jit(solution)/shard_map/ppermute | solution.py:186
  22.8 5.6 %collective-permute-start.11 = (bf16[64,2048]{1,0:T(8,128)(2,1)S(1)}, bf16[64,2048]{1,0:T(8,128)(2,1)S(1)}, u32[]{:S(2)}, u32[]{:S(2)}) collective-permute-start(bf16[64,2048]{1,0:T(8,128)(2,1)S(1)} %get-tuple-element.10), channel_id=1, source_target_pairs={{0,2},{2,0},{4,6},{6,4},{1,3},{3,1},{5,7},{7,5},{8,10},{10,8},{12,... | collective-permute-start | bytes 786440 | tf_op jit(solution)/shard_map/ppermute | solution.py:186
  23.9 5.0 %collective-permute-start.14 = (bf16[16,2048]{1,0:T(8,128)(2,1)S(1)}, bf16[16,2048]{1,0:T(8,128)(2,1)S(1)}, u32[]{:S(2)}, u32[]{:S(2)}) collective-permute-start(bf16[16,2048]{1,0:T(8,128)(2,1)S(1)} %shard_map.69), channel_id=1, source_target_pairs={{4,0},{6,2},{0,4},{2,6},{12,8},{14,10},{8,12},{10,14},{20,16},{22,... | collective-permute-start | bytes 196616 | tf_op jit(solution)/shard_map/ppermute | solution.py:183
  24.9 5.5 %collective-permute-start.16 = (bf16[16,2048]{1,0:T(8,128)(2,1)S(1)}, bf16[16,2048]{1,0:T(8,128)(2,1)S(1)}, u32[]{:S(2)}, u32[]{:S(2)}) collective-permute-start(bf16[16,2048]{1,0:T(8,128)(2,1)S(1)} %shard_map.71), channel_id=1, source_target_pairs={{4,0},{6,2},{0,4},{2,6},{12,8},{14,10},{8,12},{10,14},{20,16},{22,... | collective-permute-start | bytes 196616 | tf_op jit(solution)/shard_map/ppermute | solution.py:183
  26.2 7.0 %collective-permute-start.18 = (bf16[16,2048]{1,0:T(8,128)(2,1)S(1)}, bf16[16,2048]{1,0:T(8,128)(2,1)S(1)}, u32[]{:S(2)}, u32[]{:S(2)}) collective-permute-start(bf16[16,2048]{1,0:T(8,128)(2,1)S(1)} %shard_map.73), channel_id=1, source_target_pairs={{4,0},{6,2},{0,4},{2,6},{12,8},{14,10},{8,12},{10,14},{20,16},{22,... | collective-permute-start | bytes 196616 | tf_op jit(solution)/shard_map/ppermute | solution.py:183
  27.1 6.2 %collective-permute-start.20 = (bf16[16,2048]{1,0:T(8,128)(2,1)S(1)}, bf16[16,2048]{1,0:T(8,128)(2,1)S(1)}, u32[]{:S(2)}, u32[]{:S(2)}) collective-permute-start(bf16[16,2048]{1,0:T(8,128)(2,1)S(1)} %shard_map.75), channel_id=1, source_target_pairs={{4,0},{6,2},{0,4},{2,6},{12,8},{14,10},{8,12},{10,14},{20,16},{22,... | collective-permute-start | bytes 196616 | tf_op jit(solution)/shard_map/ppermute | solution.py:183
  29.0 7.8 %collective-permute-start.15 = (bf16[16,2048]{1,0:T(8,128)(2,1)S(1)}, bf16[16,2048]{1,0:T(8,128)(2,1)S(1)}, u32[]{:S(2)}, u32[]{:S(2)}) collective-permute-start(bf16[16,2048]{1,0:T(8,128)(2,1)S(1)} %shard_map.70), channel_id=1, source_target_pairs={{16,0},{18,2},{20,4},{22,6},{24,8},{26,10},{28,12},{30,14},{0,16},... | collective-permute-start | bytes 196616 | tf_op jit(solution)/shard_map/ppermute | solution.py:183
  30.4 6.4 %collective-permute-start.17 = (bf16[16,2048]{1,0:T(8,128)(2,1)S(1)}, bf16[16,2048]{1,0:T(8,128)(2,1)S(1)}, u32[]{:S(2)}, u32[]{:S(2)}) collective-permute-start(bf16[16,2048]{1,0:T(8,128)(2,1)S(1)} %shard_map.72), channel_id=1, source_target_pairs={{24,0},{26,2},{28,4},{30,6},{16,8},{18,10},{20,12},{22,14},{8,16},... | collective-permute-start | bytes 196616 | tf_op jit(solution)/shard_map/ppermute | solution.py:183
  33.2 4.4 %collective-permute-start.19 = (bf16[16,2048]{1,0:T(8,128)(2,1)S(1)}, bf16[16,2048]{1,0:T(8,128)(2,1)S(1)}, u32[]{:S(2)}, u32[]{:S(2)}) collective-permute-start(bf16[16,2048]{1,0:T(8,128)(2,1)S(1)} %shard_map.74), channel_id=1, source_target_pairs={{8,0},{10,2},{12,4},{14,6},{0,8},{2,10},{4,12},{6,14},{24,16},{26,... | collective-permute-start | bytes 196616 | tf_op jit(solution)/shard_map/ppermute | solution.py:183
  (3 other events, 2.5 us)

commit v4 on v3

--- a/solution.py
+++ b/solution.py
@@ -189,8 +189,7 @@
     own = prepare(place, tokens, expert_ids, gate_weights)
     weights = (w_gate, w_up, w_down)
     width = groups if experts * tok_rows <= WHOLE_ROWS else 1
-    order = [*range(groups)]
-    order[-2:] = order[:-3:-1]
+    order = [0, *range(groups - 1, 0, -1)]
     total = None
     for first in range(0, groups, width):
         if first:
@@ -217,12 +216,17 @@
         terms = []
         if first == 0:
             terms += [part[:tok_rows] for part in (near_kept, near_back)]
-        by_chip = {
-            at: [step_to(far_sum(at, s), 0, s, True) for s in range(1, chips)]
-            for at in reversed(range(width))
-        }
+        by_chip, direct = {}, []
         for at, g in reversed(list(enumerate(steps))):
-            terms += [step_to(near_sum(at, *by_chip[at]), g, 0, True)] if g else by_chip[at]
+            if g == 1:
+                direct.append(step_to(near_sum(at), g, 0, True))
+                direct += [step_to(far_sum(at, s), g, s, True) for s in range(1, chips)]
+            else:
+                by_chip[at] = [step_to(far_sum(at, s), 0, s, True) for s in range(1, chips)]
+        terms += direct
+        for at, g in reversed(list(enumerate(steps))):
+            if at in by_chip:
+                terms += [step_to(near_sum(at, *by_chip[at]), g, 0, True)] if g else by_chip[at]
         for term in terms:
             term = term.astype(jnp.float32)
             total = term if total is None else total + term

time: 38.5 us -> 38 us (0.987)
    ppermute x14, starting transfers between devices: 20.6 us -> 20 us  [step_to(): lax.ppermute(value, ('grp', 'exp'), [(d, o) for o, d in pairs] if back el...]
where the time goes in v4:
time: 38 us; the launch traced here: 37.9 us
  starting transfers between devices  21.2 us (56%)
  waiting for transfers between devices  11.6 us (31%)
  Pallas kernels  3.38 us (9%)
  local copies, waits for them, and re-layouts  0.85 us (2%)
  other arithmetic  0.71 us (2%)
    ppermute x14, starting transfers between devices, step_to(): lax.ppermute(value, ('grp', 'exp'), [(d, o) for o, d in pairs] if back el...  20 us
    ppermute x14, waiting for transfers between devices, step_to(): lax.ppermute(value, ('grp', 'exp'), [(d, o) for o, d in pairs] if back el...  10.5 us
    pallas_call x2, Pallas kernels, expert_rows(): pl.pallas_call(functools.partial(expert_kernel, count), out_shape=[jax.Sh...  3.03 us
    ppermute x7, starting transfers between devices, swap(): return lax.ppermute(value, 'exp', [(i, i ^ 1) for i in range(owners)])  1.2 us
    ppermute x7, waiting for transfers between devices, swap(): return lax.ppermute(value, 'exp', [(i, i ^ 1) for i in range(owners)])  1.1 us
    unnamed x12, local copies, waits for them, and re-layouts  0.85 us
  transfers between devices with their start and end apart: 21, of which 8 were waited for; matrix products, arithmetic and copies ran while one was open for 0% of the time, Pallas kernels for 4%

profile of v4, /device:TPU:0, one launch (start us, length us, event | category | flops | bytes accessed | tf_op | source)
XLA Modules:
  0.0 37.9 jit_solution(12926098054550988550)
XLA Ops:
  0.0 0.8 %copy-done.3 = bf16[16,2048]{1,0:T(8,128)(2,1)S(1)} copy-done((bf16[16,2048]{1,0:T(8,128)(2,1)S(1)}, bf16[16,2048]{1,0:T(8,128)(2,1)}, u32[]{:S(2)}) %copy-start.3) | copy-done | bytes 65560
  1.0 5.1 %collective-permute-start = (bf16[16,2176]{1,0:T(8,128)(2,1)S(1)}, bf16[16,2176]{1,0:T(8,128)(2,1)S(1)}, u32[]{:S(2)}, u32[]{:S(2)}) collective-permute-start(bf16[16,2176]{1,0:T(8,128)(2,1)S(1)} %shard_map.65.refs_0_), channel_id=1, source_target_pairs={{0,24},{2,26},{4,28},{6,30},{8,16},{10,18},{12,20},{14,22},{16,8},... | collective-permute-start | bytes 208904 | tf_op jit(solution)/shard_map/ppermute | solution.py:183
  6.1 1.5 %collective-permute-start.7 = (bf16[16,2176]{1,0:T(8,128)(2,1)S(1)}, bf16[16,2176]{1,0:T(8,128)(2,1)S(1)}, u32[]{:S(2)}, u32[]{:S(2)}) collective-permute-start(bf16[16,2176]{1,0:T(8,128)(2,1)S(1)} %shard_map.65.refs_0_), channel_id=1, source_target_pairs={{0,4},{2,6},{4,0},{6,2},{8,12},{10,14},{12,8},{14,10},{16,20},{18,... | collective-permute-start | bytes 208904 | tf_op jit(solution)/shard_map/ppermute | solution.py:183
  7.6 0.8 %collective-permute-start.2 = (bf16[16,2176]{1,0:T(8,128)(2,1)S(1)}, bf16[16,2176]{1,0:T(8,128)(2,1)S(1)}, u32[]{:S(2)}, u32[]{:S(2)}) collective-permute-start(bf16[16,2176]{1,0:T(8,128)(2,1)S(1)} %shard_map.65.refs_0_), channel_id=1, source_target_pairs={{0,8},{2,10},{4,12},{6,14},{8,0},{10,2},{12,4},{14,6},{16,24},{18,... | collective-permute-start | bytes 208904 | tf_op jit(solution)/shard_map/ppermute | solution.py:183
  8.6 1.9 %collective-permute-start.8 = (bf16[16,2176]{1,0:T(8,128)(2,1)S(1)}, bf16[16,2176]{1,0:T(8,128)(2,1)S(1)}, u32[]{:S(2)}, u32[]{:S(2)}) collective-permute-start(bf16[16,2176]{1,0:T(8,128)(2,1)S(1)} %collective-permute-done.refs_1_), channel_id=1, source_target_pairs={{0,4},{2,6},{4,0},{6,2},{8,12},{10,14},{12,8},{14,10},{16,20},{18,... | collective-permute-start | bytes 208904 | tf_op jit(solution)/shard_map/ppermute | solution.py:183
  10.5 2.4 %collective-permute-done.1.refs_2_ = bf16[16,2176]{1,0:T(8,128)(2,1)S(1)} collective-permute-done((bf16[16,2176]{1,0:T(8,128)(2,1)S(1)}, bf16[16,2176]{1,0:T(8,128)(2,1)S(1)}, u32[]{:S(2)}, u32[]{:S(2)}) %collective-permute-start.1) | collective-permute-done | bytes 69664 | tf_op jit(solution)/shard_map/ppermute | solution.py:183
  12.9 0.7 %collective-permute-start.9 = (bf16[16,2176]{1,0:T(8,128)(2,1)S(1)}, bf16[16,2176]{1,0:T(8,128)(2,1)S(1)}, u32[]{:S(2)}, u32[]{:S(2)}) collective-permute-start(bf16[16,2176]{1,0:T(8,128)(2,1)S(1)} %collective-permute-done.1.refs_2_), channel_id=1, source_target_pairs={{0,4},{2,6},{4,0},{6,2},{8,12},{10,14},{12,8},{14,10},{16,20},{18,... | collective-permute-start | bytes 208904 | tf_op jit(solution)/shard_map/ppermute | solution.py:183
  13.5 1.3 %collective-permute-start.10 = (bf16[16,2176]{1,0:T(8,128)(2,1)S(1)}, bf16[16,2176]{1,0:T(8,128)(2,1)S(1)}, u32[]{:S(2)}, u32[]{:S(2)}) collective-permute-start(bf16[16,2176]{1,0:T(8,128)(2,1)S(1)} %collective-permute-done.2.refs_3_), channel_id=1, source_target_pairs={{0,4},{2,6},{4,0},{6,2},{8,12},{10,14},{12,8},{14,10},{16,20},{18,... | collective-permute-start | bytes 208904 | tf_op jit(solution)/shard_map/ppermute | solution.py:183
  14.9 0.5 %collective-permute-start.6 = (bf16[16,2176]{1,0:T(8,128)(2,1)S(1)}, bf16[16,2176]{1,0:T(8,128)(2,1)S(1)}, u32[]{:S(2)}, u32[]{:S(2)}) collective-permute-start(bf16[16,2176]{1,0:T(8,128)(2,1)S(1)} %collective-permute-done.2.refs_3_), channel_id=1, source_target_pairs={{0,2},{2,0},{4,6},{6,4},{1,3},{3,1},{5,7},{7,5},{8,10},{10,8},{12,... | collective-permute-start | bytes 208904 | tf_op jit(solution)/shard_map/ppermute | solution.py:186
  15.4 1.8 %collective-permute-done.9.refs_2_ = bf16[16,2176]{1,0:T(8,128)(2,1)S(1)} collective-permute-done((bf16[16,2176]{1,0:T(8,128)(2,1)S(1)}, bf16[16,2176]{1,0:T(8,128)(2,1)S(1)}, u32[]{:S(2)}, u32[]{:S(2)}) %collective-permute-start.9) | collective-permute-done | bytes 69664 | tf_op jit(solution)/shard_map/ppermute | solution.py:183
  17.2 0.7 %collective-permute-done.10.refs_3_ = bf16[16,2176]{1,0:T(8,128)(2,1)S(1)} collective-permute-done((bf16[16,2176]{1,0:T(8,128)(2,1)S(1)}, bf16[16,2176]{1,0:T(8,128)(2,1)S(1)}, u32[]{:S(2)}, u32[]{:S(2)}) %collective-permute-start.10) | collective-permute-done | bytes 69664 | tf_op jit(solution)/shard_map/ppermute | solution.py:183
  18.1 1.5 %shard_map.67 = (f32[64,2048]{1,0:T(8,128)S(1)}, bf16[64,2048]{1,0:T(8,128)(2,1)S(1)}) custom-call(s32[8,128]{1,0:T(8,128)S(1)} %shard_map.64.place_ref, bf16[16,2176]{1,0:T(8,128)(2,1)S(1)} %shard_map.65.refs_0_, bf16[16,2176]{1,0:T(8,128)(2,1)S(1)} %collective-permute-done.refs_1_, bf16[16,2176]{1,0:T(8,128)(2,1)S(1)} %collective-permute-done.1.refs_2_, ...), custom_call_target="tpu_custom_call" | custom-call | flops 1207959552 | tf_op jit(solution)/shard_map/pallas_call | solution.py:111
  19.6 1.5 %shard_map.69 = (f32[64,2048]{1,0:T(8,128)S(1)}, bf16[64,2048]{1,0:T(8,128)(2,1)S(1)}) custom-call(s32[8,128]{1,0:T(8,128)S(1)} %shard_map.64.place_ref, bf16[64,2176]{1,0:T(8,128)(2,1)S(1)} %shard_map.66.refs_11_.refs_0_, bf16[64,2176]{1,0:T(8,128)(2,1)S(1)} %collective-permute-done.13.refs_1_, bf16[1,2048,768]{2,1,0:T(8,128)(2,1)S(1)} %copy-done, ...), custom_call_target="tpu_custom_call" | custom-call | flops 1207959552 | tf_op jit(solution)/shard_map/pallas_call | solution.py:111
  21.1 0.5 %collective-permute-start.14 = (bf16[64,2048]{1,0:T(8,128)(2,1)S(1)}, bf16[64,2048]{1,0:T(8,128)(2,1)S(1)}, u32[]{:S(2)}, u32[]{:S(2)}) collective-permute-start(bf16[64,2048]{1,0:T(8,128)(2,1)S(1)} %get-tuple-element.12), channel_id=1, source_target_pairs={{0,2},{2,0},{4,6},{6,4},{1,3},{3,1},{5,7},{7,5},{8,10},{10,8},{12,... | collective-permute-start | bytes 786440 | tf_op jit(solution)/shard_map/ppermute | solution.py:186
  21.7 1.1 %collective-permute-done.14.refs_1_ = bf16[64,2048]{1,0:T(8,128)(2,1)S(1)} collective-permute-done((bf16[64,2048]{1,0:T(8,128)(2,1)S(1)}, bf16[64,2048]{1,0:T(8,128)(2,1)S(1)}, u32[]{:S(2)}, u32[]{:S(2)}) %collective-permute-start.14) | collective-permute-done | bytes 262176 | tf_op jit(solution)/shard_map/ppermute | solution.py:186
  22.8 1.4 %collective-permute-start.18 = (bf16[16,2048]{1,0:T(8,128)(2,1)S(1)}, bf16[16,2048]{1,0:T(8,128)(2,1)S(1)}, u32[]{:S(2)}, u32[]{:S(2)}) collective-permute-start(bf16[16,2048]{1,0:T(8,128)(2,1)S(1)} %shard_map.73), channel_id=1, source_target_pairs={{4,0},{6,2},{0,4},{2,6},{12,8},{14,10},{8,12},{10,14},{20,16},{22,... | collective-permute-start | bytes 196616 | tf_op jit(solution)/shard_map/ppermute | solution.py:183
  24.2 0.8 %collective-permute-start.16 = (bf16[16,2048]{1,0:T(8,128)(2,1)S(1)}, bf16[16,2048]{1,0:T(8,128)(2,1)S(1)}, u32[]{:S(2)}, u32[]{:S(2)}) collective-permute-start(bf16[16,2048]{1,0:T(8,128)(2,1)S(1)} %shard_map.71), channel_id=1, source_target_pairs={{4,0},{6,2},{0,4},{2,6},{12,8},{14,10},{8,12},{10,14},{20,16},{22,... | collective-permute-start | bytes 196616 | tf_op jit(solution)/shard_map/ppermute | solution.py:183
  25.1 0.4 %collective-permute-start.12 = (bf16[16,2048]{1,0:T(8,128)(2,1)S(1)}, bf16[16,2048]{1,0:T(8,128)(2,1)S(1)}, u32[]{:S(2)}, u32[]{:S(2)}) collective-permute-start(bf16[16,2048]{1,0:T(8,128)(2,1)S(1)} %shard_map.68), channel_id=1, source_target_pairs={{8,0},{10,2},{12,4},{14,6},{0,8},{2,10},{4,12},{6,14},{24,16},{26,... | collective-permute-start | bytes 196616 | tf_op jit(solution)/shard_map/ppermute | solution.py:183
  25.5 1.1 %collective-permute-start.20 = (bf16[16,2048]{1,0:T(8,128)(2,1)S(1)}, bf16[16,2048]{1,0:T(8,128)(2,1)S(1)}, u32[]{:S(2)}, u32[]{:S(2)}) collective-permute-start(bf16[16,2048]{1,0:T(8,128)(2,1)S(1)} %shard_map.75), channel_id=1, source_target_pairs={{4,0},{6,2},{0,4},{2,6},{12,8},{14,10},{8,12},{10,14},{20,16},{22,... | collective-permute-start | bytes 196616 | tf_op jit(solution)/shard_map/ppermute | solution.py:183
  26.6 2.2 %collective-permute-start.15 = (bf16[16,2048]{1,0:T(8,128)(2,1)S(1)}, bf16[16,2048]{1,0:T(8,128)(2,1)S(1)}, u32[]{:S(2)}, u32[]{:S(2)}) collective-permute-start(bf16[16,2048]{1,0:T(8,128)(2,1)S(1)} %shard_map.70), channel_id=1, source_target_pairs={{12,0},{14,2},{8,4},{10,6},{4,8},{6,10},{0,12},{2,14},{28,16},{30,... | collective-permute-start | bytes 196616 | tf_op jit(solution)/shard_map/ppermute | solution.py:183
  28.8 2.8 %collective-permute-start.19 = (bf16[16,2048]{1,0:T(8,128)(2,1)S(1)}, bf16[16,2048]{1,0:T(8,128)(2,1)S(1)}, u32[]{:S(2)}, u32[]{:S(2)}) collective-permute-start(bf16[16,2048]{1,0:T(8,128)(2,1)S(1)} %shard_map.74), channel_id=1, source_target_pairs={{24,0},{26,2},{28,4},{30,6},{16,8},{18,10},{20,12},{22,14},{8,16},... | collective-permute-start | bytes 196616 | tf_op jit(solution)/shard_map/ppermute | solution.py:183
  31.8 3.3 %collective-permute-done.19 = bf16[16,2048]{1,0:T(8,128)(2,1)S(1)} collective-permute-done((bf16[16,2048]{1,0:T(8,128)(2,1)S(1)}, bf16[16,2048]{1,0:T(8,128)(2,1)S(1)}, u32[]{:S(2)}, u32[]{:S(2)}) %collective-permute-start.19) | collective-permute-done | bytes 65568 | tf_op jit(solution)/shard_map/ppermute | solution.py:183
  35.1 2.0 %collective-permute-done.17 = bf16[16,2048]{1,0:T(8,128)(2,1)S(1)} collective-permute-done((bf16[16,2048]{1,0:T(8,128)(2,1)S(1)}, bf16[16,2048]{1,0:T(8,128)(2,1)S(1)}, u32[]{:S(2)}, u32[]{:S(2)}) %collective-permute-start.17) | collective-permute-done | bytes 65568 | tf_op jit(solution)/shard_map/ppermute | solution.py:183
  37.1 0.7 %convert_add_fusion = f32[16,2048]{1,0:T(8,128)} fusion(bf16[16,2048]{1,0:T(8,128)(2,1)S(1)} %collective-permute-done.20, bf16[16,2048]{1,0:T(8,128)(2,1)S(1)} %collective-permute-done.19, bf16[16,2048]{1,0:T(8,128)(2,1)S(1)} %collective-permute-done.17, bf16[16,2048]{1,0:T(8,128)(2,1)S(1)} %collective-permute-done.15, ...), kind=kLoop, calls=%fused_computation | loop fusion | flops 393216 | bytes 655360 | tf_op jit(solution)/shard_map/add | solution.py:232
  (43 shorter events, 0.9 us)
Async XLA Ops:
  0.8 17.2 %copy-start = (bf16[1,2048,768]{2,1,0:T(8,128)(2,1)S(1)}, bf16[1,2048,768]{2,1,0:T(8,128)(2,1)}, u32[]{:S(2)}) copy-start(bf16[1,2048,768]{2,1,0:T(8,128)(2,1)} %refs_2_.1) | copy-start | bytes 9437188
  0.8 17.2 %copy-start.1 = (bf16[1,2048,768]{2,1,0:T(8,128)(2,1)S(1)}, bf16[1,2048,768]{2,1,0:T(8,128)(2,1)}, u32[]{:S(2)}) copy-start(bf16[1,2048,768]{2,1,0:T(8,128)(2,1)} %refs_3_.1) | copy-start | bytes 9437188
  0.9 17.2 %copy-start.2 = (bf16[1,768,2048]{2,1,0:T(8,128)(2,1)S(1)}, bf16[1,768,2048]{2,1,0:T(8,128)(2,1)}, u32[]{:S(2)}) copy-start(bf16[1,768,2048]{2,1,0:T(8,128)(2,1)} %refs_4_.1) | copy-start | bytes 9437188
  1.0 7.5 %collective-permute-start = (bf16[16,2176]{1,0:T(8,128)(2,1)S(1)}, bf16[16,2176]{1,0:T(8,128)(2,1)S(1)}, u32[]{:S(2)}, u32[]{:S(2)}) collective-permute-start(bf16[16,2176]{1,0:T(8,128)(2,1)S(1)} %shard_map.65.refs_0_), channel_id=1, source_target_pairs={{0,24},{2,26},{4,28},{6,30},{8,16},{10,18},{12,20},{14,22},{16,8},... | collective-permute-start | bytes 208904 | tf_op jit(solution)/shard_map/ppermute | solution.py:183
  6.1 4.4 %collective-permute-start.7 = (bf16[16,2176]{1,0:T(8,128)(2,1)S(1)}, bf16[16,2176]{1,0:T(8,128)(2,1)S(1)}, u32[]{:S(2)}, u32[]{:S(2)}) collective-permute-start(bf16[16,2176]{1,0:T(8,128)(2,1)S(1)} %shard_map.65.refs_0_), channel_id=1, source_target_pairs={{0,4},{2,6},{4,0},{6,2},{8,12},{10,14},{12,8},{14,10},{16,20},{18,... | collective-permute-start | bytes 208904 | tf_op jit(solution)/shard_map/ppermute | solution.py:183
  7.6 5.2 %collective-permute-start.1 = (bf16[16,2176]{1,0:T(8,128)(2,1)S(1)}, bf16[16,2176]{1,0:T(8,128)(2,1)S(1)}, u32[]{:S(2)}, u32[]{:S(2)}) collective-permute-start(bf16[16,2176]{1,0:T(8,128)(2,1)S(1)} %shard_map.65.refs_0_), channel_id=1, source_target_pairs={{0,16},{2,18},{4,20},{6,22},{8,24},{10,26},{12,28},{14,30},{16,0},... | collective-permute-start | bytes 208904 | tf_op jit(solution)/shard_map/ppermute | solution.py:183
  7.6 5.9 %collective-permute-start.2 = (bf16[16,2176]{1,0:T(8,128)(2,1)S(1)}, bf16[16,2176]{1,0:T(8,128)(2,1)S(1)}, u32[]{:S(2)}, u32[]{:S(2)}) collective-permute-start(bf16[16,2176]{1,0:T(8,128)(2,1)S(1)} %shard_map.65.refs_0_), channel_id=1, source_target_pairs={{0,8},{2,10},{4,12},{6,14},{8,0},{10,2},{12,4},{14,6},{16,24},{18,... | collective-permute-start | bytes 208904 | tf_op jit(solution)/shard_map/ppermute | solution.py:183
  8.4 6.5 %collective-permute-start.3 = (bf16[16,2176]{1,0:T(8,128)(2,1)S(1)}, bf16[16,2176]{1,0:T(8,128)(2,1)S(1)}, u32[]{:S(2)}, u32[]{:S(2)}) collective-permute-start(bf16[16,2176]{1,0:T(8,128)(2,1)S(1)} %shard_map.65.refs_0_), channel_id=1, source_target_pairs={{0,2},{2,0},{4,6},{6,4},{1,3},{3,1},{5,7},{7,5},{8,10},{10,8},{12,... | collective-permute-start | bytes 208904 | tf_op jit(solution)/shard_map/ppermute | solution.py:186
  8.6 6.3 %collective-permute-start.8 = (bf16[16,2176]{1,0:T(8,128)(2,1)S(1)}, bf16[16,2176]{1,0:T(8,128)(2,1)S(1)}, u32[]{:S(2)}, u32[]{:S(2)}) collective-permute-start(bf16[16,2176]{1,0:T(8,128)(2,1)S(1)} %collective-permute-done.refs_1_), channel_id=1, source_target_pairs={{0,4},{2,6},{4,0},{6,2},{8,12},{10,14},{12,8},{14,10},{16,20},{18,... | collective-permute-start | bytes 208904 | tf_op jit(solution)/shard_map/ppermute | solution.py:183
  10.5 7.4 %collective-permute-start.4 = (bf16[16,2176]{1,0:T(8,128)(2,1)S(1)}, bf16[16,2176]{1,0:T(8,128)(2,1)S(1)}, u32[]{:S(2)}, u32[]{:S(2)}) collective-permute-start(bf16[16,2176]{1,0:T(8,128)(2,1)S(1)} %collective-permute-done.refs_1_), channel_id=1, source_target_pairs={{0,2},{2,0},{4,6},{6,4},{1,3},{3,1},{5,7},{7,5},{8,10},{10,8},{12,... | collective-permute-start | bytes 208904 | tf_op jit(solution)/shard_map/ppermute | solution.py:186
  12.9 4.3 %collective-permute-start.9 = (bf16[16,2176]{1,0:T(8,128)(2,1)S(1)}, bf16[16,2176]{1,0:T(8,128)(2,1)S(1)}, u32[]{:S(2)}, u32[]{:S(2)}) collective-permute-start(bf16[16,2176]{1,0:T(8,128)(2,1)S(1)} %collective-permute-done.1.refs_2_), channel_id=1, source_target_pairs={{0,4},{2,6},{4,0},{6,2},{8,12},{10,14},{12,8},{14,10},{16,20},{18,... | collective-permute-start | bytes 208904 | tf_op jit(solution)/shard_map/ppermute | solution.py:183
  13.5 4.4 %collective-permute-start.10 = (bf16[16,2176]{1,0:T(8,128)(2,1)S(1)}, bf16[16,2176]{1,0:T(8,128)(2,1)S(1)}, u32[]{:S(2)}, u32[]{:S(2)}) collective-permute-start(bf16[16,2176]{1,0:T(8,128)(2,1)S(1)} %collective-permute-done.2.refs_3_), channel_id=1, source_target_pairs={{0,4},{2,6},{4,0},{6,2},{8,12},{10,14},{12,8},{14,10},{16,20},{18,... | collective-permute-start | bytes 208904 | tf_op jit(solution)/shard_map/ppermute | solution.py:183
  14.9 3.0 %collective-permute-start.5 = (bf16[16,2176]{1,0:T(8,128)(2,1)S(1)}, bf16[16,2176]{1,0:T(8,128)(2,1)S(1)}, u32[]{:S(2)}, u32[]{:S(2)}) collective-permute-start(bf16[16,2176]{1,0:T(8,128)(2,1)S(1)} %collective-permute-done.1.refs_2_), channel_id=1, source_target_pairs={{0,2},{2,0},{4,6},{6,4},{1,3},{3,1},{5,7},{7,5},{8,10},{10,8},{12,... | collective-permute-start | bytes 208904 | tf_op jit(solution)/shard_map/ppermute | solution.py:186
  14.9 3.0 %collective-permute-start.6 = (bf16[16,2176]{1,0:T(8,128)(2,1)S(1)}, bf16[16,2176]{1,0:T(8,128)(2,1)S(1)}, u32[]{:S(2)}, u32[]{:S(2)}) collective-permute-start(bf16[16,2176]{1,0:T(8,128)(2,1)S(1)} %collective-permute-done.2.refs_3_), channel_id=1, source_target_pairs={{0,2},{2,0},{4,6},{6,4},{1,3},{3,1},{5,7},{7,5},{8,10},{10,8},{12,... | collective-permute-start | bytes 208904 | tf_op jit(solution)/shard_map/ppermute | solution.py:186
  18.0 1.6 %collective-permute-start.13 = (bf16[64,2176]{1,0:T(8,128)(2,1)S(1)}, bf16[64,2176]{1,0:T(8,128)(2,1)S(1)}, u32[]{:S(2)}, u32[]{:S(2)}) collective-permute-start(bf16[64,2176]{1,0:T(8,128)(2,1)S(1)} %shard_map.66.refs_11_.refs_0_), channel_id=1, source_target_pairs={{0,2},{2,0},{4,6},{6,4},{1,3},{3,1},{5,7},{7,5},{8,10},{10,8},{12,... | collective-permute-start | bytes 835592 | tf_op jit(solution)/shard_map/ppermute | solution.py:186
  21.1 1.7 %collective-permute-start.14 = (bf16[64,2048]{1,0:T(8,128)(2,1)S(1)}, bf16[64,2048]{1,0:T(8,128)(2,1)S(1)}, u32[]{:S(2)}, u32[]{:S(2)}) collective-permute-start(bf16[64,2048]{1,0:T(8,128)(2,1)S(1)} %get-tuple-element.12), channel_id=1, source_target_pairs={{0,2},{2,0},{4,6},{6,4},{1,3},{3,1},{5,7},{7,5},{8,10},{10,8},{12,... | collective-permute-start | bytes 786440 | tf_op jit(solution)/shard_map/ppermute | solution.py:186
  21.7 3.4 %collective-permute-start.11 = (bf16[64,2048]{1,0:T(8,128)(2,1)S(1)}, bf16[64,2048]{1,0:T(8,128)(2,1)S(1)}, u32[]{:S(2)}, u32[]{:S(2)}) collective-permute-start(bf16[64,2048]{1,0:T(8,128)(2,1)S(1)} %get-tuple-element.10), channel_id=1, source_target_pairs={{0,2},{2,0},{4,6},{6,4},{1,3},{3,1},{5,7},{7,5},{8,10},{10,8},{12,... | collective-permute-start | bytes 786440 | tf_op jit(solution)/shard_map/ppermute | solution.py:186
  22.8 5.9 %collective-permute-start.18 = (bf16[16,2048]{1,0:T(8,128)(2,1)S(1)}, bf16[16,2048]{1,0:T(8,128)(2,1)S(1)}, u32[]{:S(2)}, u32[]{:S(2)}) collective-permute-start(bf16[16,2048]{1,0:T(8,128)(2,1)S(1)} %shard_map.73), channel_id=1, source_target_pairs={{4,0},{6,2},{0,4},{2,6},{12,8},{14,10},{8,12},{10,14},{20,16},{22,... | collective-permute-start | bytes 196616 | tf_op jit(solution)/shard_map/ppermute | solution.py:183
  24.2 7.4 %collective-permute-start.16 = (bf16[16,2048]{1,0:T(8,128)(2,1)S(1)}, bf16[16,2048]{1,0:T(8,128)(2,1)S(1)}, u32[]{:S(2)}, u32[]{:S(2)}) collective-permute-start(bf16[16,2048]{1,0:T(8,128)(2,1)S(1)} %shard_map.71), channel_id=1, source_target_pairs={{4,0},{6,2},{0,4},{2,6},{12,8},{14,10},{8,12},{10,14},{20,16},{22,... | collective-permute-start | bytes 196616 | tf_op jit(solution)/shard_map/ppermute | solution.py:183
  25.1 6.6 %collective-permute-start.12 = (bf16[16,2048]{1,0:T(8,128)(2,1)S(1)}, bf16[16,2048]{1,0:T(8,128)(2,1)S(1)}, u32[]{:S(2)}, u32[]{:S(2)}) collective-permute-start(bf16[16,2048]{1,0:T(8,128)(2,1)S(1)} %shard_map.68), channel_id=1, source_target_pairs={{8,0},{10,2},{12,4},{14,6},{0,8},{2,10},{4,12},{6,14},{24,16},{26,... | collective-permute-start | bytes 196616 | tf_op jit(solution)/shard_map/ppermute | solution.py:183
  25.5 6.2 %collective-permute-start.20 = (bf16[16,2048]{1,0:T(8,128)(2,1)S(1)}, bf16[16,2048]{1,0:T(8,128)(2,1)S(1)}, u32[]{:S(2)}, u32[]{:S(2)}) collective-permute-start(bf16[16,2048]{1,0:T(8,128)(2,1)S(1)} %shard_map.75), channel_id=1, source_target_pairs={{4,0},{6,2},{0,4},{2,6},{12,8},{14,10},{8,12},{10,14},{20,16},{22,... | collective-permute-start | bytes 196616 | tf_op jit(solution)/shard_map/ppermute | solution.py:183
  26.6 5.2 %collective-permute-start.15 = (bf16[16,2048]{1,0:T(8,128)(2,1)S(1)}, bf16[16,2048]{1,0:T(8,128)(2,1)S(1)}, u32[]{:S(2)}, u32[]{:S(2)}) collective-permute-start(bf16[16,2048]{1,0:T(8,128)(2,1)S(1)} %shard_map.70), channel_id=1, source_target_pairs={{12,0},{14,2},{8,4},{10,6},{4,8},{6,10},{0,12},{2,14},{28,16},{30,... | collective-permute-start | bytes 196616 | tf_op jit(solution)/shard_map/ppermute | solution.py:183
  28.8 6.3 %collective-permute-start.19 = (bf16[16,2048]{1,0:T(8,128)(2,1)S(1)}, bf16[16,2048]{1,0:T(8,128)(2,1)S(1)}, u32[]{:S(2)}, u32[]{:S(2)}) collective-permute-start(bf16[16,2048]{1,0:T(8,128)(2,1)S(1)} %shard_map.74), channel_id=1, source_target_pairs={{24,0},{26,2},{28,4},{30,6},{16,8},{18,10},{20,12},{22,14},{8,16},... | collective-permute-start | bytes 196616 | tf_op jit(solution)/shard_map/ppermute | solution.py:183
  31.6 5.5 %collective-permute-start.17 = (bf16[16,2048]{1,0:T(8,128)(2,1)S(1)}, bf16[16,2048]{1,0:T(8,128)(2,1)S(1)}, u32[]{:S(2)}, u32[]{:S(2)}) collective-permute-start(bf16[16,2048]{1,0:T(8,128)(2,1)S(1)} %shard_map.72), channel_id=1, source_target_pairs={{16,0},{18,2},{20,4},{22,6},{24,8},{26,10},{28,12},{30,14},{0,16},... | collective-permute-start | bytes 196616 | tf_op jit(solution)/shard_map/ppermute | solution.py:183
  (3 other events, 2.5 us)

commit v5 on v4

--- a/solution.py
+++ b/solution.py
@@ -141,25 +141,25 @@
     )(*pieces, *after)
 
 
-def add_kernel(first, *refs):
+def add_kernel(first, count, *refs):
     out_ref = refs[-1]
     rows = out_ref.shape[0]
     total = None
-    for ref in refs[:-1]:
+    for ref in refs[:count]:
         part = ref[...] if ref.shape[0] == rows else ref[first : first + rows, :]
         part = part.astype(jnp.float32)
         total = part if total is None else total + part
     out_ref[...] = total.astype(out_ref.dtype)
 
 
-def add_rows(first, rows, out_type, *terms):
-    return pl.pallas_call(
-        functools.partial(add_kernel, first),
+def add_rows(first, rows, out_type, *terms, after=()):
+    return pl.pallas_call(
+        functools.partial(add_kernel, first, len(terms)),
         out_shape=jax.ShapeDtypeStruct((rows, terms[0].shape[1]), out_type),
-        in_specs=[VMEM] * len(terms),
-        out_specs=VMEM,
-        compiler_params=pltpu.CompilerParams(vmem_limit_bytes=8 << 20),
-    )(*terms)
+        in_specs=[VMEM] * len(terms) + [HBM] * len(after),
+        out_specs=VMEM,
+        compiler_params=pltpu.CompilerParams(vmem_limit_bytes=8 << 20),
+    )(*terms, *after)
 
 
 def shards(tokens, expert_ids, gate_weights, w_gate, w_up, w_down):
@@ -209,20 +209,22 @@
             begin = at * tok_rows
             return add_rows(begin, tok_rows, jnp.bfloat16, near_kept, near_back, *terms)
 
-        def far_sum(at, s):
+        def far_sum(at, s, after=()):
             begin = (at * (chips - 1) + s - 1) * tok_rows
-            return add_rows(begin, tok_rows, jnp.bfloat16, far_kept, far_back)
+            return add_rows(begin, tok_rows, jnp.bfloat16, far_kept, far_back, after=after)
 
         terms = []
         if first == 0:
             terms += [part[:tok_rows] for part in (near_kept, near_back)]
         by_chip, direct = {}, []
         for at, g in reversed(list(enumerate(steps))):
+            if g != 1:
+                by_chip[at] = [step_to(far_sum(at, s), 0, s, True) for s in range(1, chips)]
+        for at, g in reversed(list(enumerate(steps))):
             if g == 1:
                 direct.append(step_to(near_sum(at), g, 0, True))
-                direct += [step_to(far_sum(at, s), g, s, True) for s in range(1, chips)]
-            else:
-                by_chip[at] = [step_to(far_sum(at, s), 0, s, True) for s in range(1, chips)]
+                after = by_chip[1] if 1 in by_chip else ()
+                direct += [step_to(far_sum(at, s, after), g, s, True) for s in range(1, chips)]
         terms += direct
         for at, g in reversed(list(enumerate(steps))):
             if at in by_chip:

time: 38 us -> 38 us (level)
  starting transfers between devices: 21.2 us -> 21.7 us
  waiting for transfers between devices: 11.6 us -> 11.1 us
    ppermute x14, starting transfers between devices: 20 us -> 20.5 us  [step_to(): lax.ppermute(value, ('grp', 'exp'), [(d, o) for o, d in pairs] if back el...]
    ppermute x14, waiting for transfers between devices: 10.5 us -> 9.96 us  [step_to(): lax.ppermute(value, ('grp', 'exp'), [(d, o) for o, d in pairs] if back el...]
  transfers between devices with their start and end apart: 21 -> 21, of which waited for: 8 -> 9; matrix products, arithmetic and copies ran while one was open for 0% -> 0% of each run, Pallas kernels for 4% -> 4%
where the time goes in v5:
time: 38 us; the launch traced here: 37.9 us
  starting transfers between devices  21.7 us (57%)
  waiting for transfers between devices  11.1 us (29%)
  Pallas kernels  3.38 us (9%)
  local copies, waits for them, and re-layouts  0.85 us (2%)
  other arithmetic  0.71 us (2%)
    ppermute x14, starting transfers between devices, step_to(): lax.ppermute(value, ('grp', 'exp'), [(d, o) for o, d in pairs] if back el...  20.5 us
    ppermute x14, waiting for transfers between devices, step_to(): lax.ppermute(value, ('grp', 'exp'), [(d, o) for o, d in pairs] if back el...  9.96 us
    pallas_call x2, Pallas kernels, expert_rows(): pl.pallas_call(functools.partial(expert_kernel, count), out_shape=[jax.Sh...  3.03 us
    ppermute x7, starting transfers between devices, swap(): return lax.ppermute(value, 'exp', [(i, i ^ 1) for i in range(owners)])  1.2 us
    ppermute x7, waiting for transfers between devices, swap(): return lax.ppermute(value, 'exp', [(i, i ^ 1) for i in range(owners)])  1.1 us
    unnamed x12, local copies, waits for them, and re-layouts  0.85 us
  transfers between devices with their start and end apart: 21, of which 9 were waited for; matrix products, arithmetic and copies ran while one was open for 0% of the time, Pallas kernels for 4%

profile of v5, /device:TPU:0, one launch (start us, length us, event | category | flops | bytes accessed | tf_op | source)
XLA Modules:
  0.0 37.9 jit_solution(13487993243573177123)
XLA Ops:
  0.0 0.8 %copy-done.3 = bf16[16,2048]{1,0:T(8,128)(2,1)S(1)} copy-done((bf16[16,2048]{1,0:T(8,128)(2,1)S(1)}, bf16[16,2048]{1,0:T(8,128)(2,1)}, u32[]{:S(2)}) %copy-start.3) | copy-done | bytes 65560
  1.0 5.1 %collective-permute-start = (bf16[16,2176]{1,0:T(8,128)(2,1)S(1)}, bf16[16,2176]{1,0:T(8,128)(2,1)S(1)}, u32[]{:S(2)}, u32[]{:S(2)}) collective-permute-start(bf16[16,2176]{1,0:T(8,128)(2,1)S(1)} %shard_map.65.refs_0_), channel_id=1, source_target_pairs={{0,24},{2,26},{4,28},{6,30},{8,16},{10,18},{12,20},{14,22},{16,8},... | collective-permute-start | bytes 208904 | tf_op jit(solution)/shard_map/ppermute | solution.py:183
  6.1 1.5 %collective-permute-start.7 = (bf16[16,2176]{1,0:T(8,128)(2,1)S(1)}, bf16[16,2176]{1,0:T(8,128)(2,1)S(1)}, u32[]{:S(2)}, u32[]{:S(2)}) collective-permute-start(bf16[16,2176]{1,0:T(8,128)(2,1)S(1)} %shard_map.65.refs_0_), channel_id=1, source_target_pairs={{0,4},{2,6},{4,0},{6,2},{8,12},{10,14},{12,8},{14,10},{16,20},{18,... | collective-permute-start | bytes 208904 | tf_op jit(solution)/shard_map/ppermute | solution.py:183
  7.6 0.8 %collective-permute-start.2 = (bf16[16,2176]{1,0:T(8,128)(2,1)S(1)}, bf16[16,2176]{1,0:T(8,128)(2,1)S(1)}, u32[]{:S(2)}, u32[]{:S(2)}) collective-permute-start(bf16[16,2176]{1,0:T(8,128)(2,1)S(1)} %shard_map.65.refs_0_), channel_id=1, source_target_pairs={{0,8},{2,10},{4,12},{6,14},{8,0},{10,2},{12,4},{14,6},{16,24},{18,... | collective-permute-start | bytes 208904 | tf_op jit(solution)/shard_map/ppermute | solution.py:183
  8.6 1.9 %collective-permute-start.8 = (bf16[16,2176]{1,0:T(8,128)(2,1)S(1)}, bf16[16,2176]{1,0:T(8,128)(2,1)S(1)}, u32[]{:S(2)}, u32[]{:S(2)}) collective-permute-start(bf16[16,2176]{1,0:T(8,128)(2,1)S(1)} %collective-permute-done.refs_1_), channel_id=1, source_target_pairs={{0,4},{2,6},{4,0},{6,2},{8,12},{10,14},{12,8},{14,10},{16,20},{18,... | collective-permute-start | bytes 208904 | tf_op jit(solution)/shard_map/ppermute | solution.py:183
  10.5 2.4 %collective-permute-done.1.refs_2_ = bf16[16,2176]{1,0:T(8,128)(2,1)S(1)} collective-permute-done((bf16[16,2176]{1,0:T(8,128)(2,1)S(1)}, bf16[16,2176]{1,0:T(8,128)(2,1)S(1)}, u32[]{:S(2)}, u32[]{:S(2)}) %collective-permute-start.1) | collective-permute-done | bytes 69664 | tf_op jit(solution)/shard_map/ppermute | solution.py:183
  12.9 0.7 %collective-permute-start.9 = (bf16[16,2176]{1,0:T(8,128)(2,1)S(1)}, bf16[16,2176]{1,0:T(8,128)(2,1)S(1)}, u32[]{:S(2)}, u32[]{:S(2)}) collective-permute-start(bf16[16,2176]{1,0:T(8,128)(2,1)S(1)} %collective-permute-done.1.refs_2_), channel_id=1, source_target_pairs={{0,4},{2,6},{4,0},{6,2},{8,12},{10,14},{12,8},{14,10},{16,20},{18,... | collective-permute-start | bytes 208904 | tf_op jit(solution)/shard_map/ppermute | solution.py:183
  13.5 1.3 %collective-permute-start.10 = (bf16[16,2176]{1,0:T(8,128)(2,1)S(1)}, bf16[16,2176]{1,0:T(8,128)(2,1)S(1)}, u32[]{:S(2)}, u32[]{:S(2)}) collective-permute-start(bf16[16,2176]{1,0:T(8,128)(2,1)S(1)} %collective-permute-done.2.refs_3_), channel_id=1, source_target_pairs={{0,4},{2,6},{4,0},{6,2},{8,12},{10,14},{12,8},{14,10},{16,20},{18,... | collective-permute-start | bytes 208904 | tf_op jit(solution)/shard_map/ppermute | solution.py:183
  15.4 1.8 %collective-permute-done.9.refs_2_ = bf16[16,2176]{1,0:T(8,128)(2,1)S(1)} collective-permute-done((bf16[16,2176]{1,0:T(8,128)(2,1)S(1)}, bf16[16,2176]{1,0:T(8,128)(2,1)S(1)}, u32[]{:S(2)}, u32[]{:S(2)}) %collective-permute-start.9) | collective-permute-done | bytes 69664 | tf_op jit(solution)/shard_map/ppermute | solution.py:183
  17.2 0.7 %collective-permute-done.10.refs_3_ = bf16[16,2176]{1,0:T(8,128)(2,1)S(1)} collective-permute-done((bf16[16,2176]{1,0:T(8,128)(2,1)S(1)}, bf16[16,2176]{1,0:T(8,128)(2,1)S(1)}, u32[]{:S(2)}, u32[]{:S(2)}) %collective-permute-start.10) | collective-permute-done | bytes 69664 | tf_op jit(solution)/shard_map/ppermute | solution.py:183
  18.1 1.5 %shard_map.67 = (f32[64,2048]{1,0:T(8,128)S(1)}, bf16[64,2048]{1,0:T(8,128)(2,1)S(1)}) custom-call(s32[8,128]{1,0:T(8,128)S(1)} %shard_map.64.place_ref, bf16[16,2176]{1,0:T(8,128)(2,1)S(1)} %shard_map.65.refs_0_, bf16[16,2176]{1,0:T(8,128)(2,1)S(1)} %collective-permute-done.refs_1_, bf16[16,2176]{1,0:T(8,128)(2,1)S(1)} %collective-permute-done.1.refs_2_, ...), custom_call_target="tpu_custom_call" | custom-call | flops 1207959552 | tf_op jit(solution)/shard_map/pallas_call | solution.py:111
  19.6 1.5 %shard_map.69 = (f32[64,2048]{1,0:T(8,128)S(1)}, bf16[64,2048]{1,0:T(8,128)(2,1)S(1)}) custom-call(s32[8,128]{1,0:T(8,128)S(1)} %shard_map.64.place_ref, bf16[64,2176]{1,0:T(8,128)(2,1)S(1)} %shard_map.66.refs_11_.refs_0_, bf16[64,2176]{1,0:T(8,128)(2,1)S(1)} %collective-permute-done.13.refs_1_, bf16[1,2048,768]{2,1,0:T(8,128)(2,1)S(1)} %copy-done, ...), custom_call_target="tpu_custom_call" | custom-call | flops 1207959552 | tf_op jit(solution)/shard_map/pallas_call | solution.py:111
  21.1 0.5 %collective-permute-start.14 = (bf16[64,2048]{1,0:T(8,128)(2,1)S(1)}, bf16[64,2048]{1,0:T(8,128)(2,1)S(1)}, u32[]{:S(2)}, u32[]{:S(2)}) collective-permute-start(bf16[64,2048]{1,0:T(8,128)(2,1)S(1)} %get-tuple-element.12), channel_id=1, source_target_pairs={{0,2},{2,0},{4,6},{6,4},{1,3},{3,1},{5,7},{7,5},{8,10},{10,8},{12,... | collective-permute-start | bytes 786440 | tf_op jit(solution)/shard_map/ppermute | solution.py:186
  21.7 1.1 %collective-permute-done.14.refs_1_ = bf16[64,2048]{1,0:T(8,128)(2,1)S(1)} collective-permute-done((bf16[64,2048]{1,0:T(8,128)(2,1)S(1)}, bf16[64,2048]{1,0:T(8,128)(2,1)S(1)}, u32[]{:S(2)}, u32[]{:S(2)}) %collective-permute-start.14) | collective-permute-done | bytes 262176 | tf_op jit(solution)/shard_map/ppermute | solution.py:186
  22.8 1.4 %collective-permute-start.15 = (bf16[16,2048]{1,0:T(8,128)(2,1)S(1)}, bf16[16,2048]{1,0:T(8,128)(2,1)S(1)}, u32[]{:S(2)}, u32[]{:S(2)}) collective-permute-start(bf16[16,2048]{1,0:T(8,128)(2,1)S(1)} %shard_map.70), channel_id=1, source_target_pairs={{4,0},{6,2},{0,4},{2,6},{12,8},{14,10},{8,12},{10,14},{20,16},{22,... | collective-permute-start | bytes 196616 | tf_op jit(solution)/shard_map/ppermute | solution.py:183
  24.2 0.8 %collective-permute-start.17 = (bf16[16,2048]{1,0:T(8,128)(2,1)S(1)}, bf16[16,2048]{1,0:T(8,128)(2,1)S(1)}, u32[]{:S(2)}, u32[]{:S(2)}) collective-permute-start(bf16[16,2048]{1,0:T(8,128)(2,1)S(1)} %shard_map.72), channel_id=1, source_target_pairs={{4,0},{6,2},{0,4},{2,6},{12,8},{14,10},{8,12},{10,14},{20,16},{22,... | collective-permute-start | bytes 196616 | tf_op jit(solution)/shard_map/ppermute | solution.py:183
  25.5 1.1 %collective-permute-start.20 = (bf16[16,2048]{1,0:T(8,128)(2,1)S(1)}, bf16[16,2048]{1,0:T(8,128)(2,1)S(1)}, u32[]{:S(2)}, u32[]{:S(2)}) collective-permute-start(bf16[16,2048]{1,0:T(8,128)(2,1)S(1)} %shard_map.75), channel_id=1, source_target_pairs={{4,0},{6,2},{0,4},{2,6},{12,8},{14,10},{8,12},{10,14},{20,16},{22,... | collective-permute-start | bytes 196616 | tf_op jit(solution)/shard_map/ppermute | solution.py:183
  26.6 1.1 %collective-permute-done.15.refs_2_ = bf16[16,2048]{1,0:T(8,128)(2,1)S(1)} collective-permute-done((bf16[16,2048]{1,0:T(8,128)(2,1)S(1)}, bf16[16,2048]{1,0:T(8,128)(2,1)S(1)}, u32[]{:S(2)}, u32[]{:S(2)}) %collective-permute-start.15) | collective-permute-done | bytes 65568 | tf_op jit(solution)/shard_map/ppermute | solution.py:183
  27.7 2.8 %collective-permute-start.19 = (bf16[16,2048]{1,0:T(8,128)(2,1)S(1)}, bf16[16,2048]{1,0:T(8,128)(2,1)S(1)}, u32[]{:S(2)}, u32[]{:S(2)}) collective-permute-start(bf16[16,2048]{1,0:T(8,128)(2,1)S(1)} %shard_map.74), channel_id=1, source_target_pairs={{24,0},{26,2},{28,4},{30,6},{16,8},{18,10},{20,12},{22,14},{8,16},... | collective-permute-start | bytes 196616 | tf_op jit(solution)/shard_map/ppermute | solution.py:183
  31.0 2.3 %collective-permute-start.16 = (bf16[16,2048]{1,0:T(8,128)(2,1)S(1)}, bf16[16,2048]{1,0:T(8,128)(2,1)S(1)}, u32[]{:S(2)}, u32[]{:S(2)}) collective-permute-start(bf16[16,2048]{1,0:T(8,128)(2,1)S(1)} %shard_map.71), channel_id=1, source_target_pairs={{12,0},{14,2},{8,4},{10,6},{4,8},{6,10},{0,12},{2,14},{28,16},{30,... | collective-permute-start | bytes 196616 | tf_op jit(solution)/shard_map/ppermute | solution.py:183
  33.3 0.6 %collective-permute-done.19 = bf16[16,2048]{1,0:T(8,128)(2,1)S(1)} collective-permute-done((bf16[16,2048]{1,0:T(8,128)(2,1)S(1)}, bf16[16,2048]{1,0:T(8,128)(2,1)S(1)}, u32[]{:S(2)}, u32[]{:S(2)}) %collective-permute-start.19) | collective-permute-done | bytes 65568 | tf_op jit(solution)/shard_map/ppermute | solution.py:183
  33.9 2.4 %collective-permute-done.18 = bf16[16,2048]{1,0:T(8,128)(2,1)S(1)} collective-permute-done((bf16[16,2048]{1,0:T(8,128)(2,1)S(1)}, bf16[16,2048]{1,0:T(8,128)(2,1)S(1)}, u32[]{:S(2)}, u32[]{:S(2)}) %collective-permute-start.18) | collective-permute-done | bytes 65568 | tf_op jit(solution)/shard_map/ppermute | solution.py:183
  36.2 0.9 %collective-permute-done.16 = bf16[16,2048]{1,0:T(8,128)(2,1)S(1)} collective-permute-done((bf16[16,2048]{1,0:T(8,128)(2,1)S(1)}, bf16[16,2048]{1,0:T(8,128)(2,1)S(1)}, u32[]{:S(2)}, u32[]{:S(2)}) %collective-permute-start.16) | collective-permute-done | bytes 65568 | tf_op jit(solution)/shard_map/ppermute | solution.py:183
  37.1 0.7 %convert_add_fusion = f32[16,2048]{1,0:T(8,128)} fusion(bf16[16,2048]{1,0:T(8,128)(2,1)S(1)} %collective-permute-done.20, bf16[16,2048]{1,0:T(8,128)(2,1)S(1)} %collective-permute-done.19, bf16[16,2048]{1,0:T(8,128)(2,1)S(1)} %collective-permute-done.18, bf16[16,2048]{1,0:T(8,128)(2,1)S(1)} %collective-permute-done.16, ...), kind=kLoop, calls=%fused_computation | loop fusion | flops 393216 | bytes 655360 | tf_op jit(solution)/shard_map/add | solution.py:234
  (43 shorter events, 2.1 us)
Async XLA Ops:
  0.8 17.2 %copy-start = (bf16[1,2048,768]{2,1,0:T(8,128)(2,1)S(1)}, bf16[1,2048,768]{2,1,0:T(8,128)(2,1)}, u32[]{:S(2)}) copy-start(bf16[1,2048,768]{2,1,0:T(8,128)(2,1)} %refs_2_.1) | copy-start | bytes 9437188
  0.8 17.2 %copy-start.1 = (bf16[1,2048,768]{2,1,0:T(8,128)(2,1)S(1)}, bf16[1,2048,768]{2,1,0:T(8,128)(2,1)}, u32[]{:S(2)}) copy-start(bf16[1,2048,768]{2,1,0:T(8,128)(2,1)} %refs_3_.1) | copy-start | bytes 9437188
  0.9 17.2 %copy-start.2 = (bf16[1,768,2048]{2,1,0:T(8,128)(2,1)S(1)}, bf16[1,768,2048]{2,1,0:T(8,128)(2,1)}, u32[]{:S(2)}) copy-start(bf16[1,768,2048]{2,1,0:T(8,128)(2,1)} %refs_4_.1) | copy-start | bytes 9437188
  1.0 7.5 %collective-permute-start = (bf16[16,2176]{1,0:T(8,128)(2,1)S(1)}, bf16[16,2176]{1,0:T(8,128)(2,1)S(1)}, u32[]{:S(2)}, u32[]{:S(2)}) collective-permute-start(bf16[16,2176]{1,0:T(8,128)(2,1)S(1)} %shard_map.65.refs_0_), channel_id=1, source_target_pairs={{0,24},{2,26},{4,28},{6,30},{8,16},{10,18},{12,20},{14,22},{16,8},... | collective-permute-start | bytes 208904 | tf_op jit(solution)/shard_map/ppermute | solution.py:183
  6.1 4.4 %collective-permute-start.7 = (bf16[16,2176]{1,0:T(8,128)(2,1)S(1)}, bf16[16,2176]{1,0:T(8,128)(2,1)S(1)}, u32[]{:S(2)}, u32[]{:S(2)}) collective-permute-start(bf16[16,2176]{1,0:T(8,128)(2,1)S(1)} %shard_map.65.refs_0_), channel_id=1, source_target_pairs={{0,4},{2,6},{4,0},{6,2},{8,12},{10,14},{12,8},{14,10},{16,20},{18,... | collective-permute-start | bytes 208904 | tf_op jit(solution)/shard_map/ppermute | solution.py:183
  7.6 5.2 %collective-permute-start.1 = (bf16[16,2176]{1,0:T(8,128)(2,1)S(1)}, bf16[16,2176]{1,0:T(8,128)(2,1)S(1)}, u32[]{:S(2)}, u32[]{:S(2)}) collective-permute-start(bf16[16,2176]{1,0:T(8,128)(2,1)S(1)} %shard_map.65.refs_0_), channel_id=1, source_target_pairs={{0,16},{2,18},{4,20},{6,22},{8,24},{10,26},{12,28},{14,30},{16,0},... | collective-permute-start | bytes 208904 | tf_op jit(solution)/shard_map/ppermute | solution.py:183
  7.6 5.9 %collective-permute-start.2 = (bf16[16,2176]{1,0:T(8,128)(2,1)S(1)}, bf16[16,2176]{1,0:T(8,128)(2,1)S(1)}, u32[]{:S(2)}, u32[]{:S(2)}) collective-permute-start(bf16[16,2176]{1,0:T(8,128)(2,1)S(1)} %shard_map.65.refs_0_), channel_id=1, source_target_pairs={{0,8},{2,10},{4,12},{6,14},{8,0},{10,2},{12,4},{14,6},{16,24},{18,... | collective-permute-start | bytes 208904 | tf_op jit(solution)/shard_map/ppermute | solution.py:183
  8.4 6.5 %collective-permute-start.3 = (bf16[16,2176]{1,0:T(8,128)(2,1)S(1)}, bf16[16,2176]{1,0:T(8,128)(2,1)S(1)}, u32[]{:S(2)}, u32[]{:S(2)}) collective-permute-start(bf16[16,2176]{1,0:T(8,128)(2,1)S(1)} %shard_map.65.refs_0_), channel_id=1, source_target_pairs={{0,2},{2,0},{4,6},{6,4},{1,3},{3,1},{5,7},{7,5},{8,10},{10,8},{12,... | collective-permute-start | bytes 208904 | tf_op jit(solution)/shard_map/ppermute | solution.py:186
  8.6 6.3 %collective-permute-start.8 = (bf16[16,2176]{1,0:T(8,128)(2,1)S(1)}, bf16[16,2176]{1,0:T(8,128)(2,1)S(1)}, u32[]{:S(2)}, u32[]{:S(2)}) collective-permute-start(bf16[16,2176]{1,0:T(8,128)(2,1)S(1)} %collective-permute-done.refs_1_), channel_id=1, source_target_pairs={{0,4},{2,6},{4,0},{6,2},{8,12},{10,14},{12,8},{14,10},{16,20},{18,... | collective-permute-start | bytes 208904 | tf_op jit(solution)/shard_map/ppermute | solution.py:183
  10.5 7.4 %collective-permute-start.4 = (bf16[16,2176]{1,0:T(8,128)(2,1)S(1)}, bf16[16,2176]{1,0:T(8,128)(2,1)S(1)}, u32[]{:S(2)}, u32[]{:S(2)}) collective-permute-start(bf16[16,2176]{1,0:T(8,128)(2,1)S(1)} %collective-permute-done.refs_1_), channel_id=1, source_target_pairs={{0,2},{2,0},{4,6},{6,4},{1,3},{3,1},{5,7},{7,5},{8,10},{10,8},{12,... | collective-permute-start | bytes 208904 | tf_op jit(solution)/shard_map/ppermute | solution.py:186
  12.9 4.3 %collective-permute-start.9 = (bf16[16,2176]{1,0:T(8,128)(2,1)S(1)}, bf16[16,2176]{1,0:T(8,128)(2,1)S(1)}, u32[]{:S(2)}, u32[]{:S(2)}) collective-permute-start(bf16[16,2176]{1,0:T(8,128)(2,1)S(1)} %collective-permute-done.1.refs_2_), channel_id=1, source_target_pairs={{0,4},{2,6},{4,0},{6,2},{8,12},{10,14},{12,8},{14,10},{16,20},{18,... | collective-permute-start | bytes 208904 | tf_op jit(solution)/shard_map/ppermute | solution.py:183
  13.5 4.4 %collective-permute-start.10 = (bf16[16,2176]{1,0:T(8,128)(2,1)S(1)}, bf16[16,2176]{1,0:T(8,128)(2,1)S(1)}, u32[]{:S(2)}, u32[]{:S(2)}) collective-permute-start(bf16[16,2176]{1,0:T(8,128)(2,1)S(1)} %collective-permute-done.2.refs_3_), channel_id=1, source_target_pairs={{0,4},{2,6},{4,0},{6,2},{8,12},{10,14},{12,8},{14,10},{16,20},{18,... | collective-permute-start | bytes 208904 | tf_op jit(solution)/shard_map/ppermute | solution.py:183
  14.9 3.0 %collective-permute-start.5 = (bf16[16,2176]{1,0:T(8,128)(2,1)S(1)}, bf16[16,2176]{1,0:T(8,128)(2,1)S(1)}, u32[]{:S(2)}, u32[]{:S(2)}) collective-permute-start(bf16[16,2176]{1,0:T(8,128)(2,1)S(1)} %collective-permute-done.1.refs_2_), channel_id=1, source_target_pairs={{0,2},{2,0},{4,6},{6,4},{1,3},{3,1},{5,7},{7,5},{8,10},{10,8},{12,... | collective-permute-start | bytes 208904 | tf_op jit(solution)/shard_map/ppermute | solution.py:186
  14.9 3.0 %collective-permute-start.6 = (bf16[16,2176]{1,0:T(8,128)(2,1)S(1)}, bf16[16,2176]{1,0:T(8,128)(2,1)S(1)}, u32[]{:S(2)}, u32[]{:S(2)}) collective-permute-start(bf16[16,2176]{1,0:T(8,128)(2,1)S(1)} %collective-permute-done.2.refs_3_), channel_id=1, source_target_pairs={{0,2},{2,0},{4,6},{6,4},{1,3},{3,1},{5,7},{7,5},{8,10},{10,8},{12,... | collective-permute-start | bytes 208904 | tf_op jit(solution)/shard_map/ppermute | solution.py:186
  18.0 1.6 %collective-permute-start.13 = (bf16[64,2176]{1,0:T(8,128)(2,1)S(1)}, bf16[64,2176]{1,0:T(8,128)(2,1)S(1)}, u32[]{:S(2)}, u32[]{:S(2)}) collective-permute-start(bf16[64,2176]{1,0:T(8,128)(2,1)S(1)} %shard_map.66.refs_11_.refs_0_), channel_id=1, source_target_pairs={{0,2},{2,0},{4,6},{6,4},{1,3},{3,1},{5,7},{7,5},{8,10},{10,8},{12,... | collective-permute-start | bytes 835592 | tf_op jit(solution)/shard_map/ppermute | solution.py:186
  21.1 1.7 %collective-permute-start.14 = (bf16[64,2048]{1,0:T(8,128)(2,1)S(1)}, bf16[64,2048]{1,0:T(8,128)(2,1)S(1)}, u32[]{:S(2)}, u32[]{:S(2)}) collective-permute-start(bf16[64,2048]{1,0:T(8,128)(2,1)S(1)} %get-tuple-element.12), channel_id=1, source_target_pairs={{0,2},{2,0},{4,6},{6,4},{1,3},{3,1},{5,7},{7,5},{8,10},{10,8},{12,... | collective-permute-start | bytes 786440 | tf_op jit(solution)/shard_map/ppermute | solution.py:186
  21.7 3.4 %collective-permute-start.11 = (bf16[64,2048]{1,0:T(8,128)(2,1)S(1)}, bf16[64,2048]{1,0:T(8,128)(2,1)S(1)}, u32[]{:S(2)}, u32[]{:S(2)}) collective-permute-start(bf16[64,2048]{1,0:T(8,128)(2,1)S(1)} %get-tuple-element.10), channel_id=1, source_target_pairs={{0,2},{2,0},{4,6},{6,4},{1,3},{3,1},{5,7},{7,5},{8,10},{10,8},{12,... | collective-permute-start | bytes 786440 | tf_op jit(solution)/shard_map/ppermute | solution.py:186
  22.8 4.8 %collective-permute-start.15 = (bf16[16,2048]{1,0:T(8,128)(2,1)S(1)}, bf16[16,2048]{1,0:T(8,128)(2,1)S(1)}, u32[]{:S(2)}, u32[]{:S(2)}) collective-permute-start(bf16[16,2048]{1,0:T(8,128)(2,1)S(1)} %shard_map.70), channel_id=1, source_target_pairs={{4,0},{6,2},{0,4},{2,6},{12,8},{14,10},{8,12},{10,14},{20,16},{22,... | collective-permute-start | bytes 196616 | tf_op jit(solution)/shard_map/ppermute | solution.py:183
  24.2 6.3 %collective-permute-start.17 = (bf16[16,2048]{1,0:T(8,128)(2,1)S(1)}, bf16[16,2048]{1,0:T(8,128)(2,1)S(1)}, u32[]{:S(2)}, u32[]{:S(2)}) collective-permute-start(bf16[16,2048]{1,0:T(8,128)(2,1)S(1)} %shard_map.72), channel_id=1, source_target_pairs={{4,0},{6,2},{0,4},{2,6},{12,8},{14,10},{8,12},{10,14},{20,16},{22,... | collective-permute-start | bytes 196616 | tf_op jit(solution)/shard_map/ppermute | solution.py:183
  25.1 8.2 %collective-permute-start.12 = (bf16[16,2048]{1,0:T(8,128)(2,1)S(1)}, bf16[16,2048]{1,0:T(8,128)(2,1)S(1)}, u32[]{:S(2)}, u32[]{:S(2)}) collective-permute-start(bf16[16,2048]{1,0:T(8,128)(2,1)S(1)} %shard_map.68), channel_id=1, source_target_pairs={{8,0},{10,2},{12,4},{14,6},{0,8},{2,10},{4,12},{6,14},{24,16},{26,... | collective-permute-start | bytes 196616 | tf_op jit(solution)/shard_map/ppermute | solution.py:183
  25.5 7.8 %collective-permute-start.20 = (bf16[16,2048]{1,0:T(8,128)(2,1)S(1)}, bf16[16,2048]{1,0:T(8,128)(2,1)S(1)}, u32[]{:S(2)}, u32[]{:S(2)}) collective-permute-start(bf16[16,2048]{1,0:T(8,128)(2,1)S(1)} %shard_map.75), channel_id=1, source_target_pairs={{4,0},{6,2},{0,4},{2,6},{12,8},{14,10},{8,12},{10,14},{20,16},{22,... | collective-permute-start | bytes 196616 | tf_op jit(solution)/shard_map/ppermute | solution.py:183
  27.7 6.2 %collective-permute-start.19 = (bf16[16,2048]{1,0:T(8,128)(2,1)S(1)}, bf16[16,2048]{1,0:T(8,128)(2,1)S(1)}, u32[]{:S(2)}, u32[]{:S(2)}) collective-permute-start(bf16[16,2048]{1,0:T(8,128)(2,1)S(1)} %shard_map.74), channel_id=1, source_target_pairs={{24,0},{26,2},{28,4},{30,6},{16,8},{18,10},{20,12},{22,14},{8,16},... | collective-permute-start | bytes 196616 | tf_op jit(solution)/shard_map/ppermute | solution.py:183
  30.5 5.7 %collective-permute-start.18 = (bf16[16,2048]{1,0:T(8,128)(2,1)S(1)}, bf16[16,2048]{1,0:T(8,128)(2,1)S(1)}, u32[]{:S(2)}, u32[]{:S(2)}) collective-permute-start(bf16[16,2048]{1,0:T(8,128)(2,1)S(1)} %shard_map.73), channel_id=1, source_target_pairs={{16,0},{18,2},{20,4},{22,6},{24,8},{26,10},{28,12},{30,14},{0,16},... | collective-permute-start | bytes 196616 | tf_op jit(solution)/shard_map/ppermute | solution.py:183
  31.0 6.1 %collective-permute-start.16 = (bf16[16,2048]{1,0:T(8,128)(2,1)S(1)}, bf16[16,2048]{1,0:T(8,128)(2,1)S(1)}, u32[]{:S(2)}, u32[]{:S(2)}) collective-permute-start(bf16[16,2048]{1,0:T(8,128)(2,1)S(1)} %shard_map.71), channel_id=1, source_target_pairs={{12,0},{14,2},{8,4},{10,6},{4,8},{6,10},{0,12},{2,14},{28,16},{30,... | collective-permute-start | bytes 196616 | tf_op jit(solution)/shard_map/ppermute | solution.py:183
  (3 other events, 2.5 us)

commit v6 on v0

--- a/solution.py
+++ b/solution.py
@@ -88,7 +88,8 @@
         at += ref.shape[0]
 
 
-def expert_kernel(count, place_ref, *refs):
+def expert_kernel(skip, count, *refs):
+    place_ref, *refs = refs[skip:]
     kept_ref, given_ref, held = refs[-3:]
     gate_ref, up_ref, down_ref = refs[count : count + 3]
     rows, model_width = kept_ref.shape
@@ -109,12 +110,12 @@
     count = len(own) + len(other)
     rows = sum(piece.shape[0] for piece in own)
     return pl.pallas_call(
-        functools.partial(expert_kernel, count),
+        functools.partial(expert_kernel, len(after), count),
         out_shape=[
             jax.ShapeDtypeStruct((rows, model_width), jnp.float32),
             jax.ShapeDtypeStruct((rows, model_width), jnp.bfloat16),
         ],
-        in_specs=[VMEM] * (count + 4) + [HBM] * len(after),
+        in_specs=[HBM] * len(after) + [VMEM] * (count + 4),
         out_specs=[VMEM] * 2,
         scratch_shapes=[pltpu.VMEM((2 * rows, width), jnp.bfloat16)],
         compiler_params=pltpu.CompilerParams(vmem_limit_bytes=16 << 20),
@@ -123,7 +124,7 @@
             bytes_accessed=0,
             transcendentals=2 * rows * hidden_width,
         ),
-    )(place, *own, *other, *weights, *after)
+    )(*after, place, *own, *other, *weights)
 
 
 def pack_kernel(count, *refs):

time: 37.5 us -> 37.6 us (level)
  transfers between devices with their start and end apart: 21 -> 21, of which waited for: 8 -> 10; matrix products, arithmetic and copies ran while one was open for 0% -> 0% of each run, Pallas kernels for 4% -> 4%
where the time goes in v6:
time: 37.6 us; the launch traced here: 37.5 us
  starting transfers between devices  21.3 us (57%)
  waiting for transfers between devices  11.2 us (30%)
  Pallas kernels  3.36 us (9%)
  local copies, waits for them, and re-layouts  0.85 us (2%)
  other arithmetic  0.7 us (2%)
    ppermute x14, starting transfers between devices, step_to(): lax.ppermute(value, ('grp', 'exp'), [(d, o) for o, d in pairs] if back el...  20.4 us
    ppermute x14, waiting for transfers between devices, step_to(): lax.ppermute(value, ('grp', 'exp'), [(d, o) for o, d in pairs] if back el...  10.1 us
    pallas_call x2, Pallas kernels, expert_rows(): pl.pallas_call(functools.partial(expert_kernel, len(after), count), out_s...  3.01 us
    ppermute x7, waiting for transfers between devices, swap(): return lax.ppermute(value, 'exp', [(i, i ^ 1) for i in range(owners)])  1.1 us
    ppermute x7, starting transfers between devices, swap(): return lax.ppermute(value, 'exp', [(i, i ^ 1) for i in range(owners)])  0.88 us
    unnamed x12, local copies, waits for them, and re-layouts  0.85 us
  transfers between devices with their start and end apart: 21, of which 10 were waited for; matrix products, arithmetic and copies ran while one was open for 0% of the time, Pallas kernels for 4%

profile of v6, /device:TPU:0, one launch (start us, length us, event | category | flops | bytes accessed | tf_op | source)
XLA Modules:
  0.0 37.5 jit_solution(14471760525162593054)
XLA Ops:
  0.0 0.8 %copy-done.3 = bf16[16,2048]{1,0:T(8,128)(2,1)S(1)} copy-done((bf16[16,2048]{1,0:T(8,128)(2,1)S(1)}, bf16[16,2048]{1,0:T(8,128)(2,1)}, u32[]{:S(2)}) %copy-start.3) | copy-done | bytes 65560
  1.0 5.1 %collective-permute-start.5 = (bf16[16,2176]{1,0:T(8,128)(2,1)S(1)}, bf16[16,2176]{1,0:T(8,128)(2,1)S(1)}, u32[]{:S(2)}, u32[]{:S(2)}) collective-permute-start(bf16[16,2176]{1,0:T(8,128)(2,1)S(1)} %shard_map.65.refs_2_), channel_id=1, source_target_pairs={{0,24},{2,26},{4,28},{6,30},{8,16},{10,18},{12,20},{14,22},{16,8},... | collective-permute-start | bytes 208904 | tf_op jit(solution)/shard_map/ppermute | solution.py:184
  6.1 0.7 %collective-permute-start.1 = (bf16[16,2176]{1,0:T(8,128)(2,1)S(1)}, bf16[16,2176]{1,0:T(8,128)(2,1)S(1)}, u32[]{:S(2)}, u32[]{:S(2)}) collective-permute-start(bf16[16,2176]{1,0:T(8,128)(2,1)S(1)} %shard_map.65.refs_2_), channel_id=1, source_target_pairs={{0,8},{2,10},{4,12},{6,14},{8,0},{10,2},{12,4},{14,6},{16,24},{18,... | collective-permute-start | bytes 208904 | tf_op jit(solution)/shard_map/ppermute | solution.py:184
  6.8 1.6 %collective-permute-start = (bf16[16,2176]{1,0:T(8,128)(2,1)S(1)}, bf16[16,2176]{1,0:T(8,128)(2,1)S(1)}, u32[]{:S(2)}, u32[]{:S(2)}) collective-permute-start(bf16[16,2176]{1,0:T(8,128)(2,1)S(1)} %shard_map.65.refs_2_), channel_id=1, source_target_pairs={{0,4},{2,6},{4,0},{6,2},{8,12},{10,14},{12,8},{14,10},{16,20},{18,... | collective-permute-start | bytes 208904 | tf_op jit(solution)/shard_map/ppermute | solution.py:184
  8.7 1.5 %collective-permute-start.6 = (bf16[16,2176]{1,0:T(8,128)(2,1)S(1)}, bf16[16,2176]{1,0:T(8,128)(2,1)S(1)}, u32[]{:S(2)}, u32[]{:S(2)}) collective-permute-start(bf16[16,2176]{1,0:T(8,128)(2,1)S(1)} %collective-permute-done.5.refs_5_), channel_id=1, source_target_pairs={{0,4},{2,6},{4,0},{6,2},{8,12},{10,14},{12,8},{14,10},{16,20},{18,... | collective-permute-start | bytes 208904 | tf_op jit(solution)/shard_map/ppermute | solution.py:184
  10.2 2.0 %collective-permute-done.3.refs_4_ = bf16[16,2176]{1,0:T(8,128)(2,1)S(1)} collective-permute-done((bf16[16,2176]{1,0:T(8,128)(2,1)S(1)}, bf16[16,2176]{1,0:T(8,128)(2,1)S(1)}, u32[]{:S(2)}, u32[]{:S(2)}) %collective-permute-start.3) | collective-permute-done | bytes 69664 | tf_op jit(solution)/shard_map/ppermute | solution.py:184
  12.2 1.6 %collective-permute-start.4 = (bf16[16,2176]{1,0:T(8,128)(2,1)S(1)}, bf16[16,2176]{1,0:T(8,128)(2,1)S(1)}, u32[]{:S(2)}, u32[]{:S(2)}) collective-permute-start(bf16[16,2176]{1,0:T(8,128)(2,1)S(1)} %collective-permute-done.3.refs_4_), channel_id=1, source_target_pairs={{0,4},{2,6},{4,0},{6,2},{8,12},{10,14},{12,8},{14,10},{16,20},{18,... | collective-permute-start | bytes 208904 | tf_op jit(solution)/shard_map/ppermute | solution.py:184
  13.9 0.5 %collective-permute-start.2 = (bf16[16,2176]{1,0:T(8,128)(2,1)S(1)}, bf16[16,2176]{1,0:T(8,128)(2,1)S(1)}, u32[]{:S(2)}, u32[]{:S(2)}) collective-permute-start(bf16[16,2176]{1,0:T(8,128)(2,1)S(1)} %collective-permute-done.1.refs_3_), channel_id=1, source_target_pairs={{0,4},{2,6},{4,0},{6,2},{8,12},{10,14},{12,8},{14,10},{16,20},{18,... | collective-permute-start | bytes 208904 | tf_op jit(solution)/shard_map/ppermute | solution.py:184
  14.5 2.3 %collective-permute-done.4.refs_2_ = bf16[16,2176]{1,0:T(8,128)(2,1)S(1)} collective-permute-done((bf16[16,2176]{1,0:T(8,128)(2,1)S(1)}, bf16[16,2176]{1,0:T(8,128)(2,1)S(1)}, u32[]{:S(2)}, u32[]{:S(2)}) %collective-permute-start.4) | collective-permute-done | bytes 69664 | tf_op jit(solution)/shard_map/ppermute | solution.py:184
  16.8 1.6 %collective-permute-done.2.refs_1_ = bf16[16,2176]{1,0:T(8,128)(2,1)S(1)} collective-permute-done((bf16[16,2176]{1,0:T(8,128)(2,1)S(1)}, bf16[16,2176]{1,0:T(8,128)(2,1)S(1)}, u32[]{:S(2)}, u32[]{:S(2)}) %collective-permute-start.2) | collective-permute-done | bytes 69664 | tf_op jit(solution)/shard_map/ppermute | solution.py:184
  18.5 1.5 %shard_map.67 = (f32[64,2048]{1,0:T(8,128)S(1)}, bf16[64,2048]{1,0:T(8,128)(2,1)S(1)}) custom-call(bf16[64,2176]{1,0:T(8,128)(2,1)S(1)} %shard_map.66.refs_0_.refs_2_, s32[8,128]{1,0:T(8,128)S(1)} %shard_map.64.place_ref.refs_1_, bf16[16,2176]{1,0:T(8,128)(2,1)S(1)} %shard_map.65.refs_2_, bf16[16,2176]{1,0:T(8,128)(2,1)S(1)} %collective-permute-done.1.refs_3_, ...), custom_call_target="tpu_custom_call" | custom-call | flops 1207959552 | tf_op jit(solution)/shard_map/pallas_call | solution.py:112
  20.0 1.5 %shard_map.68 = (f32[64,2048]{1,0:T(8,128)S(1)}, bf16[64,2048]{1,0:T(8,128)(2,1)S(1)}) custom-call(f32[64,2048]{1,0:T(8,128)S(1)} %get-tuple-element.9.refs_0_, s32[8,128]{1,0:T(8,128)S(1)} %shard_map.64.place_ref.refs_1_, bf16[64,2176]{1,0:T(8,128)(2,1)S(1)} %shard_map.66.refs_0_.refs_2_, bf16[64,2176]{1,0:T(8,128)(2,1)S(1)} %collective-permute-done.12.refs_3_, ...), custom_call_target="tpu_custom_call" | custom-call | flops 1207959552 | tf_op jit(solution)/shard_map/pallas_call | solution.py:112
  21.5 0.5 %collective-permute-start.13 = (bf16[64,2048]{1,0:T(8,128)(2,1)S(1)}, bf16[64,2048]{1,0:T(8,128)(2,1)S(1)}, u32[]{:S(2)}, u32[]{:S(2)}) collective-permute-start(bf16[64,2048]{1,0:T(8,128)(2,1)S(1)} %get-tuple-element.12), channel_id=1, source_target_pairs={{0,2},{2,0},{4,6},{6,4},{1,3},{3,1},{5,7},{7,5},{8,10},{10,8},{12,... | collective-permute-start | bytes 786440 | tf_op jit(solution)/shard_map/ppermute | solution.py:187
  22.1 1.1 %collective-permute-done.13.refs_1_ = bf16[64,2048]{1,0:T(8,128)(2,1)S(1)} collective-permute-done((bf16[64,2048]{1,0:T(8,128)(2,1)S(1)}, bf16[64,2048]{1,0:T(8,128)(2,1)S(1)}, u32[]{:S(2)}, u32[]{:S(2)}) %collective-permute-start.13) | collective-permute-done | bytes 262176 | tf_op jit(solution)/shard_map/ppermute | solution.py:187
  23.3 1.5 %collective-permute-start.14 = (bf16[16,2048]{1,0:T(8,128)(2,1)S(1)}, bf16[16,2048]{1,0:T(8,128)(2,1)S(1)}, u32[]{:S(2)}, u32[]{:S(2)}) collective-permute-start(bf16[16,2048]{1,0:T(8,128)(2,1)S(1)} %shard_map.69), channel_id=1, source_target_pairs={{4,0},{6,2},{0,4},{2,6},{12,8},{14,10},{8,12},{10,14},{20,16},{22,... | collective-permute-start | bytes 196616 | tf_op jit(solution)/shard_map/ppermute | solution.py:184
  24.8 0.7 %collective-permute-start.16 = (bf16[16,2048]{1,0:T(8,128)(2,1)S(1)}, bf16[16,2048]{1,0:T(8,128)(2,1)S(1)}, u32[]{:S(2)}, u32[]{:S(2)}) collective-permute-start(bf16[16,2048]{1,0:T(8,128)(2,1)S(1)} %shard_map.71), channel_id=1, source_target_pairs={{4,0},{6,2},{0,4},{2,6},{12,8},{14,10},{8,12},{10,14},{20,16},{22,... | collective-permute-start | bytes 196616 | tf_op jit(solution)/shard_map/ppermute | solution.py:184
  25.5 1.5 %collective-permute-start.18 = (bf16[16,2048]{1,0:T(8,128)(2,1)S(1)}, bf16[16,2048]{1,0:T(8,128)(2,1)S(1)}, u32[]{:S(2)}, u32[]{:S(2)}) collective-permute-start(bf16[16,2048]{1,0:T(8,128)(2,1)S(1)} %shard_map.73), channel_id=1, source_target_pairs={{4,0},{6,2},{0,4},{2,6},{12,8},{14,10},{8,12},{10,14},{20,16},{22,... | collective-permute-start | bytes 196616 | tf_op jit(solution)/shard_map/ppermute | solution.py:184
  27.0 0.7 %collective-permute-start.20 = (bf16[16,2048]{1,0:T(8,128)(2,1)S(1)}, bf16[16,2048]{1,0:T(8,128)(2,1)S(1)}, u32[]{:S(2)}, u32[]{:S(2)}) collective-permute-start(bf16[16,2048]{1,0:T(8,128)(2,1)S(1)} %shard_map.75), channel_id=1, source_target_pairs={{4,0},{6,2},{0,4},{2,6},{12,8},{14,10},{8,12},{10,14},{20,16},{22,... | collective-permute-start | bytes 196616 | tf_op jit(solution)/shard_map/ppermute | solution.py:184
  27.6 0.3 collective-permute-done.14.refs_2_
  28.0 3.0 %collective-permute-start.15 = (bf16[16,2048]{1,0:T(8,128)(2,1)S(1)}, bf16[16,2048]{1,0:T(8,128)(2,1)S(1)}, u32[]{:S(2)}, u32[]{:S(2)}) collective-permute-start(bf16[16,2048]{1,0:T(8,128)(2,1)S(1)} %shard_map.70), channel_id=1, source_target_pairs={{24,0},{26,2},{28,4},{30,6},{16,8},{18,10},{20,12},{22,14},{8,16},... | collective-permute-start | bytes 196616 | tf_op jit(solution)/shard_map/ppermute | solution.py:184
  31.2 2.0 %collective-permute-start.19 = (bf16[16,2048]{1,0:T(8,128)(2,1)S(1)}, bf16[16,2048]{1,0:T(8,128)(2,1)S(1)}, u32[]{:S(2)}, u32[]{:S(2)}) collective-permute-start(bf16[16,2048]{1,0:T(8,128)(2,1)S(1)} %shard_map.74), channel_id=1, source_target_pairs={{8,0},{10,2},{12,4},{14,6},{0,8},{2,10},{4,12},{6,14},{24,16},{26,... | collective-permute-start | bytes 196616 | tf_op jit(solution)/shard_map/ppermute | solution.py:184
  33.2 1.0 %collective-permute-done.15 = bf16[16,2048]{1,0:T(8,128)(2,1)S(1)} collective-permute-done((bf16[16,2048]{1,0:T(8,128)(2,1)S(1)}, bf16[16,2048]{1,0:T(8,128)(2,1)S(1)}, u32[]{:S(2)}, u32[]{:S(2)}) %collective-permute-start.15) | collective-permute-done | bytes 65568 | tf_op jit(solution)/shard_map/ppermute | solution.py:184
  34.2 2.5 %collective-permute-done.17 = bf16[16,2048]{1,0:T(8,128)(2,1)S(1)} collective-permute-done((bf16[16,2048]{1,0:T(8,128)(2,1)S(1)}, bf16[16,2048]{1,0:T(8,128)(2,1)S(1)}, u32[]{:S(2)}, u32[]{:S(2)}) %collective-permute-start.17) | collective-permute-done | bytes 65568 | tf_op jit(solution)/shard_map/ppermute | solution.py:184
  36.8 0.7 %convert_add_fusion = f32[16,2048]{1,0:T(8,128)} fusion(bf16[16,2048]{1,0:T(8,128)(2,1)S(1)} %collective-permute-done.20, bf16[16,2048]{1,0:T(8,128)(2,1)S(1)} %collective-permute-done.19, bf16[16,2048]{1,0:T(8,128)(2,1)S(1)} %collective-permute-done.17, bf16[16,2048]{1,0:T(8,128)(2,1)S(1)} %collective-permute-done.15, ...), kind=kLoop, calls=%fused_computation | loop fusion | flops 327680 | bytes 589824 | tf_op jit(solution)/shard_map/add | solution.py:227
  (43 shorter events, 1.3 us)
Async XLA Ops:
  0.8 17.6 %copy-start = (bf16[1,2048,768]{2,1,0:T(8,128)(2,1)S(1)}, bf16[1,2048,768]{2,1,0:T(8,128)(2,1)}, u32[]{:S(2)}) copy-start(bf16[1,2048,768]{2,1,0:T(8,128)(2,1)} %refs_4_.1) | copy-start | bytes 9437188
  0.8 17.6 %copy-start.1 = (bf16[1,2048,768]{2,1,0:T(8,128)(2,1)S(1)}, bf16[1,2048,768]{2,1,0:T(8,128)(2,1)}, u32[]{:S(2)}) copy-start(bf16[1,2048,768]{2,1,0:T(8,128)(2,1)} %refs_5_.1) | copy-start | bytes 9437188
  0.9 17.6 %copy-start.2 = (bf16[1,768,2048]{2,1,0:T(8,128)(2,1)S(1)}, bf16[1,768,2048]{2,1,0:T(8,128)(2,1)}, u32[]{:S(2)}) copy-start(bf16[1,768,2048]{2,1,0:T(8,128)(2,1)} %refs_6_.1) | copy-start | bytes 9437188
  1.0 7.6 %collective-permute-start.5 = (bf16[16,2176]{1,0:T(8,128)(2,1)S(1)}, bf16[16,2176]{1,0:T(8,128)(2,1)S(1)}, u32[]{:S(2)}, u32[]{:S(2)}) collective-permute-start(bf16[16,2176]{1,0:T(8,128)(2,1)S(1)} %shard_map.65.refs_2_), channel_id=1, source_target_pairs={{0,24},{2,26},{4,28},{6,30},{8,16},{10,18},{12,20},{14,22},{16,8},... | collective-permute-start | bytes 208904 | tf_op jit(solution)/shard_map/ppermute | solution.py:184
  6.1 2.6 %collective-permute-start.7 = (bf16[16,2176]{1,0:T(8,128)(2,1)S(1)}, bf16[16,2176]{1,0:T(8,128)(2,1)S(1)}, u32[]{:S(2)}, u32[]{:S(2)}) collective-permute-start(bf16[16,2176]{1,0:T(8,128)(2,1)S(1)} %shard_map.65.refs_2_), channel_id=1, source_target_pairs={{0,2},{2,0},{4,6},{6,4},{1,3},{3,1},{5,7},{7,5},{8,10},{10,8},{12,... | collective-permute-start | bytes 208904 | tf_op jit(solution)/shard_map/ppermute | solution.py:187
  6.1 6.1 %collective-permute-start.3 = (bf16[16,2176]{1,0:T(8,128)(2,1)S(1)}, bf16[16,2176]{1,0:T(8,128)(2,1)S(1)}, u32[]{:S(2)}, u32[]{:S(2)}) collective-permute-start(bf16[16,2176]{1,0:T(8,128)(2,1)S(1)} %shard_map.65.refs_2_), channel_id=1, source_target_pairs={{0,16},{2,18},{4,20},{6,22},{8,24},{10,26},{12,28},{14,30},{16,0},... | collective-permute-start | bytes 208904 | tf_op jit(solution)/shard_map/ppermute | solution.py:184
  6.1 6.1 %collective-permute-start.1 = (bf16[16,2176]{1,0:T(8,128)(2,1)S(1)}, bf16[16,2176]{1,0:T(8,128)(2,1)S(1)}, u32[]{:S(2)}, u32[]{:S(2)}) collective-permute-start(bf16[16,2176]{1,0:T(8,128)(2,1)S(1)} %shard_map.65.refs_2_), channel_id=1, source_target_pairs={{0,8},{2,10},{4,12},{6,14},{8,0},{10,2},{12,4},{14,6},{16,24},{18,... | collective-permute-start | bytes 208904 | tf_op jit(solution)/shard_map/ppermute | solution.py:184
  6.8 7.0 %collective-permute-start = (bf16[16,2176]{1,0:T(8,128)(2,1)S(1)}, bf16[16,2176]{1,0:T(8,128)(2,1)S(1)}, u32[]{:S(2)}, u32[]{:S(2)}) collective-permute-start(bf16[16,2176]{1,0:T(8,128)(2,1)S(1)} %shard_map.65.refs_2_), channel_id=1, source_target_pairs={{0,4},{2,6},{4,0},{6,2},{8,12},{10,14},{12,8},{14,10},{16,20},{18,... | collective-permute-start | bytes 208904 | tf_op jit(solution)/shard_map/ppermute | solution.py:184
  8.7 5.3 %collective-permute-start.10 = (bf16[16,2176]{1,0:T(8,128)(2,1)S(1)}, bf16[16,2176]{1,0:T(8,128)(2,1)S(1)}, u32[]{:S(2)}, u32[]{:S(2)}) collective-permute-start(bf16[16,2176]{1,0:T(8,128)(2,1)S(1)} %collective-permute-done.5.refs_5_), channel_id=1, source_target_pairs={{0,2},{2,0},{4,6},{6,4},{1,3},{3,1},{5,7},{7,5},{8,10},{10,8},{12,... | collective-permute-start | bytes 208904 | tf_op jit(solution)/shard_map/ppermute | solution.py:187
  8.7 5.8 %collective-permute-start.6 = (bf16[16,2176]{1,0:T(8,128)(2,1)S(1)}, bf16[16,2176]{1,0:T(8,128)(2,1)S(1)}, u32[]{:S(2)}, u32[]{:S(2)}) collective-permute-start(bf16[16,2176]{1,0:T(8,128)(2,1)S(1)} %collective-permute-done.5.refs_5_), channel_id=1, source_target_pairs={{0,4},{2,6},{4,0},{6,2},{8,12},{10,14},{12,8},{14,10},{16,20},{18,... | collective-permute-start | bytes 208904 | tf_op jit(solution)/shard_map/ppermute | solution.py:184
  12.2 2.3 %collective-permute-start.9 = (bf16[16,2176]{1,0:T(8,128)(2,1)S(1)}, bf16[16,2176]{1,0:T(8,128)(2,1)S(1)}, u32[]{:S(2)}, u32[]{:S(2)}) collective-permute-start(bf16[16,2176]{1,0:T(8,128)(2,1)S(1)} %collective-permute-done.3.refs_4_), channel_id=1, source_target_pairs={{0,2},{2,0},{4,6},{6,4},{1,3},{3,1},{5,7},{7,5},{8,10},{10,8},{12,... | collective-permute-start | bytes 208904 | tf_op jit(solution)/shard_map/ppermute | solution.py:187
  12.2 4.6 %collective-permute-start.4 = (bf16[16,2176]{1,0:T(8,128)(2,1)S(1)}, bf16[16,2176]{1,0:T(8,128)(2,1)S(1)}, u32[]{:S(2)}, u32[]{:S(2)}) collective-permute-start(bf16[16,2176]{1,0:T(8,128)(2,1)S(1)} %collective-permute-done.3.refs_4_), channel_id=1, source_target_pairs={{0,4},{2,6},{4,0},{6,2},{8,12},{10,14},{12,8},{14,10},{16,20},{18,... | collective-permute-start | bytes 208904 | tf_op jit(solution)/shard_map/ppermute | solution.py:184
  13.8 3.0 %collective-permute-start.8 = (bf16[16,2176]{1,0:T(8,128)(2,1)S(1)}, bf16[16,2176]{1,0:T(8,128)(2,1)S(1)}, u32[]{:S(2)}, u32[]{:S(2)}) collective-permute-start(bf16[16,2176]{1,0:T(8,128)(2,1)S(1)} %collective-permute-done.1.refs_3_), channel_id=1, source_target_pairs={{0,2},{2,0},{4,6},{6,4},{1,3},{3,1},{5,7},{7,5},{8,10},{10,8},{12,... | collective-permute-start | bytes 208904 | tf_op jit(solution)/shard_map/ppermute | solution.py:187
  13.9 4.4 %collective-permute-start.2 = (bf16[16,2176]{1,0:T(8,128)(2,1)S(1)}, bf16[16,2176]{1,0:T(8,128)(2,1)S(1)}, u32[]{:S(2)}, u32[]{:S(2)}) collective-permute-start(bf16[16,2176]{1,0:T(8,128)(2,1)S(1)} %collective-permute-done.1.refs_3_), channel_id=1, source_target_pairs={{0,4},{2,6},{4,0},{6,2},{8,12},{10,14},{12,8},{14,10},{16,20},{18,... | collective-permute-start | bytes 208904 | tf_op jit(solution)/shard_map/ppermute | solution.py:184
  18.4 1.6 %collective-permute-start.12 = (bf16[64,2176]{1,0:T(8,128)(2,1)S(1)}, bf16[64,2176]{1,0:T(8,128)(2,1)S(1)}, u32[]{:S(2)}, u32[]{:S(2)}) collective-permute-start(bf16[64,2176]{1,0:T(8,128)(2,1)S(1)} %shard_map.66.refs_0_.refs_2_), channel_id=1, source_target_pairs={{0,2},{2,0},{4,6},{6,4},{1,3},{3,1},{5,7},{7,5},{8,10},{10,8},{12,... | collective-permute-start | bytes 835592 | tf_op jit(solution)/shard_map/ppermute | solution.py:187
  21.5 1.7 %collective-permute-start.13 = (bf16[64,2048]{1,0:T(8,128)(2,1)S(1)}, bf16[64,2048]{1,0:T(8,128)(2,1)S(1)}, u32[]{:S(2)}, u32[]{:S(2)}) collective-permute-start(bf16[64,2048]{1,0:T(8,128)(2,1)S(1)} %get-tuple-element.12), channel_id=1, source_target_pairs={{0,2},{2,0},{4,6},{6,4},{1,3},{3,1},{5,7},{7,5},{8,10},{10,8},{12,... | collective-permute-start | bytes 786440 | tf_op jit(solution)/shard_map/ppermute | solution.py:187
  22.1 5.6 %collective-permute-start.11 = (bf16[64,2048]{1,0:T(8,128)(2,1)S(1)}, bf16[64,2048]{1,0:T(8,128)(2,1)S(1)}, u32[]{:S(2)}, u32[]{:S(2)}) collective-permute-start(bf16[64,2048]{1,0:T(8,128)(2,1)S(1)} %get-tuple-element.10), channel_id=1, source_target_pairs={{0,2},{2,0},{4,6},{6,4},{1,3},{3,1},{5,7},{7,5},{8,10},{10,8},{12,... | collective-permute-start | bytes 786440 | tf_op jit(solution)/shard_map/ppermute | solution.py:187
  23.3 4.7 %collective-permute-start.14 = (bf16[16,2048]{1,0:T(8,128)(2,1)S(1)}, bf16[16,2048]{1,0:T(8,128)(2,1)S(1)}, u32[]{:S(2)}, u32[]{:S(2)}) collective-permute-start(bf16[16,2048]{1,0:T(8,128)(2,1)S(1)} %shard_map.69), channel_id=1, source_target_pairs={{4,0},{6,2},{0,4},{2,6},{12,8},{14,10},{8,12},{10,14},{20,16},{22,... | collective-permute-start | bytes 196616 | tf_op jit(solution)/shard_map/ppermute | solution.py:184
  24.8 6.2 %collective-permute-start.16 = (bf16[16,2048]{1,0:T(8,128)(2,1)S(1)}, bf16[16,2048]{1,0:T(8,128)(2,1)S(1)}, u32[]{:S(2)}, u32[]{:S(2)}) collective-permute-start(bf16[16,2048]{1,0:T(8,128)(2,1)S(1)} %shard_map.71), channel_id=1, source_target_pairs={{4,0},{6,2},{0,4},{2,6},{12,8},{14,10},{8,12},{10,14},{20,16},{22,... | collective-permute-start | bytes 196616 | tf_op jit(solution)/shard_map/ppermute | solution.py:184
  25.5 5.7 %collective-permute-start.18 = (bf16[16,2048]{1,0:T(8,128)(2,1)S(1)}, bf16[16,2048]{1,0:T(8,128)(2,1)S(1)}, u32[]{:S(2)}, u32[]{:S(2)}) collective-permute-start(bf16[16,2048]{1,0:T(8,128)(2,1)S(1)} %shard_map.73), channel_id=1, source_target_pairs={{4,0},{6,2},{0,4},{2,6},{12,8},{14,10},{8,12},{10,14},{20,16},{22,... | collective-permute-start | bytes 196616 | tf_op jit(solution)/shard_map/ppermute | solution.py:184
  27.0 6.3 %collective-permute-start.20 = (bf16[16,2048]{1,0:T(8,128)(2,1)S(1)}, bf16[16,2048]{1,0:T(8,128)(2,1)S(1)}, u32[]{:S(2)}, u32[]{:S(2)}) collective-permute-start(bf16[16,2048]{1,0:T(8,128)(2,1)S(1)} %shard_map.75), channel_id=1, source_target_pairs={{4,0},{6,2},{0,4},{2,6},{12,8},{14,10},{8,12},{10,14},{20,16},{22,... | collective-permute-start | bytes 196616 | tf_op jit(solution)/shard_map/ppermute | solution.py:184
  28.0 6.2 %collective-permute-start.15 = (bf16[16,2048]{1,0:T(8,128)(2,1)S(1)}, bf16[16,2048]{1,0:T(8,128)(2,1)S(1)}, u32[]{:S(2)}, u32[]{:S(2)}) collective-permute-start(bf16[16,2048]{1,0:T(8,128)(2,1)S(1)} %shard_map.70), channel_id=1, source_target_pairs={{24,0},{26,2},{28,4},{30,6},{16,8},{18,10},{20,12},{22,14},{8,16},... | collective-permute-start | bytes 196616 | tf_op jit(solution)/shard_map/ppermute | solution.py:184
  31.0 5.7 %collective-permute-start.17 = (bf16[16,2048]{1,0:T(8,128)(2,1)S(1)}, bf16[16,2048]{1,0:T(8,128)(2,1)S(1)}, u32[]{:S(2)}, u32[]{:S(2)}) collective-permute-start(bf16[16,2048]{1,0:T(8,128)(2,1)S(1)} %shard_map.72), channel_id=1, source_target_pairs={{16,0},{18,2},{20,4},{22,6},{24,8},{26,10},{28,12},{30,14},{0,16},... | collective-permute-start | bytes 196616 | tf_op jit(solution)/shard_map/ppermute | solution.py:184
  31.2 5.5 %collective-permute-start.19 = (bf16[16,2048]{1,0:T(8,128)(2,1)S(1)}, bf16[16,2048]{1,0:T(8,128)(2,1)S(1)}, u32[]{:S(2)}, u32[]{:S(2)}) collective-permute-start(bf16[16,2048]{1,0:T(8,128)(2,1)S(1)} %shard_map.74), channel_id=1, source_target_pairs={{8,0},{10,2},{12,4},{14,6},{0,8},{2,10},{4,12},{6,14},{24,16},{26,... | collective-permute-start | bytes 196616 | tf_op jit(solution)/shard_map/ppermute | solution.py:184
  (3 other events, 2.5 us)
